TPU v7x, 32 devices: a whole 2x2x4 slice. The times are simulated.
32 devices in a mesh: section: 8 (over z, core), mp: 4 (over y, x).
Axes of the slice: x: 2, y: 2, z: 4, core: 2. Of those that a mesh axis runs over, the one named last changes fastest.
Arguments:
- matches: int32 [1024, 2], P('section'), may hold values from 0 to 7, all different within a row; in each aligned block of 128 rows (0 to 127, 128 to 255, ...) at most 64 rows name the same one
- actions: int32 [2, 1024, 2], P(None, 'section'), may hold values from 0 to 1023
- state: float32 [1024, 2, 2048], P('section', None, 'mp'), may hold values from -6 to 6
- embed: bfloat16 [1024, 2048], P(None, 'mp'), may hold values from -3 to 3
- w_in: bfloat16 [8, 1, 2048, 8192], P('section', None, None, 'mp'), may hold values from -0.125 to 0.125
- w_out: bfloat16 [8, 1, 8192, 2048], P('section', None, 'mp'), may hold values from -0.0625 to 0.0625
- head: bfloat16 [8, 2048, 1024], P('section', None, 'mp'), may hold values from -16 to 16
Outputs:
- logp: float32 [2, 1024, 2], P(None, 'section')
Inputs may be any that keep to these rules, and one draw needn't show every extreme that they name: `matches`: each game names two different agents; among the 128 games of one index of section no agent is named more than 64 times, a bound that some block reaches in some of these groups.
All inputs are finite; a program needn't handle non-finite values.
Results may differ from a plain program's by a relative error of at most 0.0095.
Values may be sent and summed in bfloat16 or wider, within the bound.
No kernel may reach another device: no remote copies, remote signals or barrier semaphores. Data moves between devices by JAX's collectives and lax.ppermute only.
A program may use at most 64 MiB of HBM per device.

v0:
```python
import functools

import jax
import jax.numpy as jnp
from jax import lax
from jax.experimental import pallas as pl
from jax.experimental.pallas import tpu as pltpu
from jax.sharding import PartitionSpec as P

STEPS = 2
META = 8
DIGIT = 32
SHARES = ((1, 1), (3, 4), (1, 2))
TILE = 512
VMEM = 20 * 1024 * 1024

norm_eps = 1e-06
f32 = jnp.float32
bf16 = jnp.bfloat16


def rms_round(source):
    widened = source.astype(f32)
    scale = lax.rsqrt(jnp.mean(widened * widened, axis=-1, keepdims=True) + norm_eps)
    return (widened * scale).astype(bf16)


def iota(shape, dim):
    return lax.broadcasted_iota(jnp.int32, shape, dim)


def nt_dot(left, right):
    return lax.dot_general(left, right, (((1,), (1,)), ((), ())), preferred_element_type=f32)


def slots_row(own_row, own_col):
    rows = own_row.shape[1]
    earlier = (own_col == own_row) & (iota((rows, rows), 0) < iota((rows, rows), 1))
    return jnp.sum(earlier.astype(jnp.int32), axis=0, keepdims=True)


def pack_kernel(sections, cap, own_row, own_col, meta, state, out):
    games, _, feat = state.shape
    rows = 2 * games
    dest = own_row[...] * cap + slots_row(own_row[...], own_col[...])
    select = (iota((sections * cap, rows), 0) == dest).astype(bf16)
    first = jnp.dot(select[:, :games], state[:, 0, :].astype(bf16), preferred_element_type=f32)
    second = jnp.dot(select[:, games:], state[:, 1, :].astype(bf16), preferred_element_type=f32)
    packed = (first + second).astype(bf16)
    notes = nt_dot(meta[...], select).astype(bf16)
    for s in range(sections):
        out[s, :cap, :] = packed[s * cap : (s + 1) * cap]
        out[s, cap:, :] = jnp.zeros((META, feat), bf16)
        out[s, cap:, :cap] = notes[:, s * cap : (s + 1) * cap]


def unpack_kernel(sections, cap, mp_ref, arrived, embed, x0_out, x1_out, notes_out, place_out, count_out):
    slots = sections * cap
    m = mp_ref[0]
    rows = jnp.concatenate([arrived[s, :cap, :] for s in range(sections)], axis=0)
    notes = jnp.concatenate([arrived[s, cap:, :cap] for s in range(sections)], axis=1)
    live = notes[META - 1 : META, :].astype(f32)
    before = (iota((slots, slots), 0) < iota((slots, slots), 1)).astype(bf16)
    rank = jnp.dot(jnp.broadcast_to(live, (8, slots)).astype(bf16), before, preferred_element_type=f32)
    rank = rank[:1].astype(jnp.int32)
    served = jnp.sum(live).astype(jnp.int32)
    fits = [(served * den <= slots * num).astype(jnp.int32) for num, den in SHARES]
    count_out[0] = sum(fits[1:], 0)
    group = slots // 4
    for (num, den), fit in zip(SHARES[1:], fits[1:]):
        group = group + fit * (slots * num // den // 4 - group)
    block = sum((rank >= j * group).astype(jnp.int32) for j in range(1, 4))
    place = jnp.where(live > 0, (block ^ m) * group + (rank - block * group), -1)
    size = slots
    select = (iota((size, slots), 0) == place).astype(bf16)
    x0 = jnp.dot(select, rows, preferred_element_type=f32)
    mine = nt_dot(select, notes)
    own = (mine[:, 0:1] * DIGIT + mine[:, 1:2]).astype(jnp.int32)
    other = (mine[:, 2:3] * DIGIT + mine[:, 3:4]).astype(jnp.int32)
    columns = iota((size, embed.shape[0]), 1)
    effect = jnp.where(columns == own, 1.0, 0.0) + jnp.where(columns == other, 0.5, 0.0)
    moved = jnp.dot(effect.astype(bf16), embed[...], preferred_element_type=f32)
    x0_out[...] = x0.astype(bf16)
    x1_out[...] = (0.8 * x0 + moved).astype(bf16)
    notes_out[...] = mine[: size // 4]
    place_out[...] = place


def hidden_kernel(size, tile, mp_ref, own, px, py, da, db, w_in, hidden, mine, x_full, scale):
    feat = own.shape[1]
    group = size // 4
    width, inner = w_in.shape
    m = mp_ref[0]
    total = jnp.zeros((size, 1), f32)
    for k in range(4):
        parts = []
        for j in range(4):
            b = j ^ k
            if k == 3:
                src = da if b < 2 else db
                parts.append(src[(b % 2) * group : (b % 2 + 1) * group, :])
            else:
                src = (own, px, py)[k]
                parts.append(src[b * group : (b + 1) * group, :])
        chunk = jnp.concatenate(parts, axis=0)
        x_full[:, pl.ds(pl.multiple_of((m ^ k) * feat, feat), feat)] = chunk
        wide = chunk.astype(f32)
        total = total + jnp.sum(wide * wide, axis=1, keepdims=True)
    scale[...] = lax.rsqrt(total / width + norm_eps)
    mine[...] = x_full[:group, :]

    @pl.loop(0, inner // tile)
    def _(t):
        cols = pl.ds(pl.multiple_of(t * tile, tile), tile)
        z = jnp.dot(x_full[...], w_in[:, cols], preferred_element_type=f32)
        hidden[:, cols] = jax.nn.gelu(z * scale[...]).astype(bf16)


def near_kernel(size, tile, mp_ref, own, px, py, w_in, z, square, chunks, w_here, arrived):
    feat = own.shape[1]
    group = size // 4
    m = mp_ref[0]

    def fetch(k, t):
        rows = pl.ds(pl.multiple_of((m ^ k) * feat, feat), feat)
        cols = pl.ds(pl.multiple_of(t * tile, tile), tile)
        return pltpu.make_async_copy(w_in.at[rows, cols], w_here.at[k, :, cols], arrived.at[k, t])

    tiles = w_in.shape[1] // tile
    for t in range(tiles):
        for k in range(3):
            fetch(k, t).start()
    total = jnp.zeros((size, 1), f32)
    for k, src in enumerate((own, px, py)):
        for j in range(4):
            chunks[k, j * group : (j + 1) * group, :] = src[(j ^ k) * group : ((j ^ k) + 1) * group, :]
        wide = chunks[k].astype(f32)
        total = total + jnp.sum(wide * wide, axis=1, keepdims=True)
    square[...] = total

    @pl.loop(0, tiles)
    def _(t):
        cols = pl.ds(pl.multiple_of(t * tile, tile), tile)
        for k in range(3):
            fetch(k, t).wait()
        z[:, cols] = sum(jnp.dot(chunks[k], w_here[k, :, cols], preferred_element_type=f32) for k in range(3))


def far_kernel(size, tile, mp_ref, z, square, own, px, py, da, db, w_in, hidden, mine, chunk, scale):
    feat = own.shape[1]
    group = size // 4
    width = 4 * feat
    m = mp_ref[0]
    for j in range(4):
        src = db if j < 2 else da
        chunk[j * group : (j + 1) * group, :] = src[((j ^ 3) % 2) * group : ((j ^ 3) % 2 + 1) * group, :]
    wide = chunk[...].astype(f32)
    total = square[...] + jnp.sum(wide * wide, axis=1, keepdims=True)
    scale[...] = lax.rsqrt(total / width + norm_eps)
    rows = [pl.ds(pl.multiple_of((m ^ k) * feat, feat), feat) for k in range(4)]
    mine[:, rows[0]] = own[:group, :]
    mine[:, rows[1]] = px[group : 2 * group, :]
    mine[:, rows[2]] = py[2 * group : 3 * group, :]
    mine[:, rows[3]] = chunk[:group, :]

    @pl.loop(0, w_in.shape[1] // tile)
    def _(t):
        cols = pl.ds(pl.multiple_of(t * tile, tile), tile)
        total = z[:, cols] + jnp.dot(chunk[...], w_in[rows[3], cols], preferred_element_type=f32)
        hidden[:, cols] = jax.nn.gelu(total * scale[...]).astype(bf16)


def part_kernel(size, tile, hidden, w_out, send_a, send_b, keep_a, keep_b):
    group = size // 4
    half = w_out.shape[1] // 2
    for side in range(2):
        keep, send, order = ((keep_a, send_a, (0, 2, 1, 3)), (keep_b, send_b, (0, 1, 2, 3)))[side]

        @pl.loop(0, half // tile)
        def _(t):
            cols = pl.ds(pl.multiple_of(t * tile, tile), tile)
            from_cols = pl.ds(pl.multiple_of(t * tile + side * half, tile), tile)
            part = jnp.dot(hidden[...], w_out[:, from_cols], preferred_element_type=f32).astype(bf16)
            for i, j in enumerate(order):
                ref = keep if i < 2 else send
                ref[(i % 2) * group : (i % 2 + 1) * group, cols] = part[j * group : (j + 1) * group]


def fold_kernel(keep_a, got_a, keep_b, got_b, out_a, out_b):
    out_a[...] = (keep_a[...].astype(f32) + got_a[...].astype(f32)).astype(bf16)
    out_b[...] = (keep_b[...].astype(f32) + got_b[...].astype(f32)).astype(bf16)


def score_kernel(sections, cap, step_idx, mp_ref, mine, keep_a, got_a, last_a, keep_b, got_b, last_b, h0, h1_top, h1_bottom, h2_top, h2_bottom, h3_top, h3_bottom, notes, place, *rest):
    earlier, out = rest[:-1], rest[-1]
    group, width = mine.shape
    half = width // 2
    m = mp_ref[0]
    wide = lambda ref: ref[...].astype(f32)
    sum_a = keep_a[:group].astype(f32) + got_a[:group].astype(f32) + wide(last_a)
    sum_b = keep_b[:group].astype(f32) + got_b[:group].astype(f32) + wide(last_b)
    x = wide(mine)
    ha = x[:, :half] + sum_a
    hb = x[:, half:] + sum_b
    square = jnp.sum(ha * ha, axis=1, keepdims=True) + jnp.sum(hb * hb, axis=1, keepdims=True)
    scale = lax.rsqrt(square / width + norm_eps)
    na = (ha * scale).astype(bf16)
    nb = (hb * scale).astype(bf16)
    c = 4 * step_idx
    chosen = (notes[:, c : c + 1] * DIGIT + notes[:, c + 1 : c + 2]).astype(jnp.int32)
    logits = []
    heads = ((h0[:half], h0[half:]), (h1_top[...], h1_bottom[...]), (h2_top[...], h2_bottom[...]), (h3_top[...], h3_bottom[...]))
    for top, bottom in heads:
        logits.append(
            jnp.dot(na, top, preferred_element_type=f32) + jnp.dot(nb, bottom, preferred_element_type=f32)
        )
    peak = functools.reduce(jnp.maximum, [jnp.max(v, axis=1, keepdims=True) for v in logits])
    total = jnp.zeros((group, 1), f32)
    picked = jnp.zeros((group, 1), f32)
    for k, v in enumerate(logits):
        columns = iota(v.shape, 1) + (m ^ k) * v.shape[1]
        total = total + jnp.sum(jnp.exp(v - peak), axis=1, keepdims=True)
        picked = picked + jnp.sum(jnp.where(columns == chosen, v, 0.0), axis=1, keepdims=True)
    logp = picked - peak - jnp.log(total)
    slots = sections * cap
    spread = jnp.where(iota((group, slots), 0) == place[...], logp, 0.0)
    spread = jnp.sum(spread, axis=0, keepdims=True)
    if not earlier:
        for s in range(sections):
            out[s : s + 1, :] = spread[:, s * cap : (s + 1) * cap]
        return
    for s in range(sections):
        row = jnp.concatenate([earlier[0][s : s + 1, :], spread[:, s * cap : (s + 1) * cap]], axis=1)
        out[4 * s : 4 * s + 4, :] = jnp.broadcast_to(row, (4, 2 * cap))


def return_kernel(sections, cap, own_row, own_col, got, out):
    rows = own_row.shape[1]
    dest = own_row[...] * cap + slots_row(own_row[...], own_col[...])
    pick = (iota((sections * cap, rows), 0) == dest).astype(f32)
    agents = [jnp.sum(got[4 * a : 4 * a + 4, :], axis=0, keepdims=True) for a in range(sections)]
    steps = [jnp.concatenate([v[:, t * cap : (t + 1) * cap] for v in agents], axis=1) for t in range(STEPS)]
    steps = jnp.concatenate(steps + [jnp.zeros((8 - STEPS, sections * cap), f32)], axis=0)
    found = jnp.dot(steps, pick, precision=lax.Precision.HIGHEST, preferred_element_type=f32)
    out[...] = found[:STEPS]


def halves_kernel(source, top, bottom, done):
    h = top.shape[0]
    copies = [
        pltpu.make_async_copy(source.at[pl.ds(i * h, h)], half, done.at[i]) for i, half in enumerate((top, bottom))
    ]
    for copy in copies:
        copy.start()
    for copy in copies:
        copy.wait()


def call(kernel, outs, cost=None, **kw):
    return pl.pallas_call(
        kernel,
        out_shape=outs,
        compiler_params=pltpu.CompilerParams(vmem_limit_bytes=VMEM),
        cost_estimate=cost,
        **kw,
    )


def shape(*dims, dtype=bf16):
    return jax.ShapeDtypeStruct(dims, dtype)


SMEM_SPEC = pl.BlockSpec(memory_space=pltpu.SMEM)
VMEM_SPEC = pl.BlockSpec(memory_space=pltpu.VMEM)


def serve_rows(sections, cap, size, over_x, over_y, m, x0, x1, notes, place, w_in, w_out, *heads):
    feat = x0.shape[1]
    width = w_in.shape[0]
    inner = w_in.shape[1]
    group = size // 4

    h = size // 2
    flops = 2 * size * width * inner

    def near(v):
        return over_x(v), over_y(v)

    def far(from_x, from_y):
        return over_y(from_x[:h]), over_x(from_y[h:])

    def to_hidden(x, near_x, far_x):
        return call(
            functools.partial(hidden_kernel, size, TILE),
            (shape(size, inner), shape(group, width)),
            cost=pl.CostEstimate(flops=flops, bytes_accessed=2 * width * inner, transcendentals=size * inner),
            in_specs=[SMEM_SPEC] + [VMEM_SPEC] * 6,
            scratch_shapes=[pltpu.VMEM((size, width), bf16), pltpu.VMEM((size, 1), f32)],
        )(m, x, *near_x, *far_x, w_in)

    def to_near(x, near_x):
        return call(
            functools.partial(near_kernel, size, TILE),
            (shape(size, inner, dtype=f32), shape(size, 1, dtype=f32)),
            cost=pl.CostEstimate(flops=3 * flops // 4, bytes_accessed=2 * width * inner, transcendentals=0),
            in_specs=[SMEM_SPEC] + [VMEM_SPEC] * 3 + [pl.BlockSpec(memory_space=pl.ANY)],
            scratch_shapes=[
                pltpu.VMEM((3, size, feat), bf16),
                pltpu.VMEM((3, feat, inner), bf16),
                pltpu.SemaphoreType.DMA((3, inner // TILE)),
            ],
        )(m, x, *near_x, w_in)

    def finish_hidden(z, square, x, near_x, far_x):
        return call(
            functools.partial(far_kernel, size, TILE),
            (shape(size, inner), shape(group, width)),
            cost=pl.CostEstimate(flops=flops // 4, bytes_accessed=width * inner // 2, transcendentals=size * inner),
            in_specs=[SMEM_SPEC] + [VMEM_SPEC] * 8,
            scratch_shapes=[pltpu.VMEM((size, feat), bf16), pltpu.VMEM((size, 1), f32)],
        )(m, z, square, x, *near_x, *far_x, w_in)

    def to_parts(hidden):
        return call(
            functools.partial(part_kernel, size, TILE),
            (shape(h, width // 2),) * 4,
            cost=pl.CostEstimate(flops=flops, bytes_accessed=2 * width * inner, transcendentals=0),
        )(hidden, w_out)

    def fold(keep_a, got_a, keep_b, got_b):
        second = pl.BlockSpec((group, width // 2), lambda i: (1, 0))
        whole = pl.BlockSpec((group, width // 2), lambda i: (0, 0))
        return call(
            fold_kernel,
            (shape(group, width // 2),) * 2,
            grid=(1,),
            in_specs=[second] * 4,
            out_specs=(whole,) * 2,
        )(keep_a, got_a, keep_b, got_b)

    def score(step_idx, pieces, *earlier):
        return call(
            functools.partial(score_kernel, sections, cap, step_idx),
            shape(4 * sections, 2 * cap, dtype=f32) if earlier else shape(sections, cap, dtype=f32),
            in_specs=[SMEM_SPEC] + [VMEM_SPEC] * (9 + len(heads) + len(earlier)),
        )(m, *pieces, *heads, notes, place, *earlier)

    x0, x1, notes = x0[:size], x1[:size], notes[:group]
    near0 = near(x0)
    far0 = far(*near0)
    z0, square0 = to_near(x0, near0)
    x1, *near0 = lax.optimization_barrier((x1, *near0))
    near1 = near(x1)
    z0, *near1 = lax.optimization_barrier((z0, *near1))
    hidden0, mine0 = finish_hidden(z0, square0, x0, near0, far0)
    far1 = far(*near1)
    send_a0, send_b0, keep_a0, keep_b0 = to_parts(hidden0)
    got_a0, got_b0 = over_x(send_a0), over_y(send_b0)
    hidden1, mine1 = to_hidden(x1, near1, far1)
    hidden1, got_a0, got_b0 = lax.optimization_barrier((hidden1, got_a0, got_b0))
    fold_a0, fold_b0 = fold(keep_a0, got_a0, keep_b0, got_b0)
    last_a0, last_b0 = over_y(fold_a0), over_x(fold_b0)
    hidden1, fold_a0 = lax.optimization_barrier((hidden1, fold_a0))
    send_a1, send_b1, keep_a1, keep_b1 = to_parts(hidden1)
    got_a1, got_b1 = over_x(send_a1), over_y(send_b1)
    fold_a1, fold_b1 = fold(keep_a1, got_a1, keep_b1, got_b1)
    last_a1, last_b1 = over_y(fold_a1), over_x(fold_b1)
    first = score(0, (mine0, keep_a0, got_a0, last_a0, keep_b0, got_b0, last_b0))
    return score(1, (mine1, keep_a1, got_a1, last_a1, keep_b1, got_b1, last_b1), first)


def plane_plan(matches, actions, state, embed, w_in, w_out, head):
    sections = lax.axis_size("section")
    games, _, feat = state.shape
    cap = 4 * games // sections
    rows = 2 * games
    slots = sections * cap
    width = 4 * feat
    m = lax.axis_index("mp").astype(jnp.int32).reshape(1)
    over_x = lambda v: lax.ppermute(v, "mp", [(i, i ^ 1) for i in range(4)])
    over_y = lambda v: lax.ppermute(v, "mp", [(i, i ^ 2) for i in range(4)])

    own_row = matches.T.reshape(1, rows)
    own_col = own_row.reshape(rows, 1)
    acts = actions.transpose(0, 2, 1)
    mine0, other0, mine1 = acts[0].reshape(rows), acts[0, ::-1].reshape(rows), acts[1].reshape(rows)
    notes = jnp.stack(
        [
            mine0 // DIGIT, mine0 % DIGIT, other0 // DIGIT, other0 % DIGIT,
            mine1 // DIGIT, mine1 % DIGIT, jnp.zeros_like(mine0), jnp.ones_like(mine0),
        ]
    ).astype(bf16)

    head_own = head[0]
    rows_half = head_own.shape[0] // 2
    top, bottom = call(
        halves_kernel,
        (shape(rows_half, head_own.shape[1]),) * 2,
        in_specs=[pl.BlockSpec(memory_space=pl.ANY)],
        scratch_shapes=[pltpu.SemaphoreType.DMA((2,))],
    )(head_own)
    x_top, y_bottom = over_x(top), over_y(bottom)
    others = (x_top, over_x(bottom), over_y(top), y_bottom, over_y(x_top), over_x(y_bottom))

    packed = call(functools.partial(pack_kernel, sections, cap), shape(sections, cap + META, feat))(
        own_row, own_col, notes, state
    )
    arrived = lax.all_to_all(packed, "section", split_axis=0, concat_axis=0, tiled=True)
    x0, x1, notes_c, place, count = call(
        functools.partial(unpack_kernel, sections, cap),
        (
            shape(slots, feat), shape(slots, feat), shape(slots // 4, META, dtype=f32),
            shape(1, slots, dtype=jnp.int32), shape(1, dtype=jnp.int32),
        ),
        in_specs=[SMEM_SPEC, VMEM_SPEC, VMEM_SPEC],
        out_specs=(VMEM_SPEC,) * 4 + (SMEM_SPEC,),
    )(m, arrived, embed)

    x0, *others = lax.optimization_barrier((x0,) + others)
    heads = (head_own, *others)

    branches = [
        functools.partial(serve_rows, sections, cap, slots * num // den, over_x, over_y) for num, den in SHARES
    ]
    sent = lax.switch(count[0], branches, m, x0, x1, notes_c, place, w_in[0, 0], w_out[0, 0], *heads)
    back = lax.all_to_all(sent, ("section", "mp"), split_axis=0, concat_axis=0, tiled=True)
    logp = call(functools.partial(return_kernel, sections, cap), shape(STEPS, rows, dtype=f32))(own_row, own_col, back)
    return logp.reshape(STEPS, 2, games).transpose(0, 2, 1)


def general_plan(matches, actions, state, embed, w_in, w_out, head):
    sections = lax.axis_size("section")
    game_count = matches.shape[0]
    feat_width = state.shape[2]
    slot_cap = 4 * game_count // sections
    served = sections * slot_cap
    owners = matches.reshape(-1)
    onehot = (owners[:, None] == jnp.arange(sections, dtype=jnp.int32)[None, :]).astype(jnp.int32)
    slot_of = jnp.sum((jnp.cumsum(onehot, axis=0) - onehot) * onehot, axis=1)
    action_width = head.shape[2]
    columns = lax.axis_index("mp") * action_width + jnp.arange(action_width, dtype=jnp.int32)
    current = state
    results = []
    for step_idx in range(STEPS):
        observed = current.astype(bf16).reshape(2 * game_count, feat_width)
        outgoing = jnp.zeros((sections, slot_cap, feat_width), bf16).at[owners, slot_of].set(observed)
        arrived = lax.all_to_all(outgoing, "section", split_axis=0, concat_axis=0, tiled=True)
        inputs = lax.all_gather(arrived.reshape(served, feat_width), "mp", axis=1, tiled=True)
        normed = rms_round(inputs)
        hidden = jax.nn.gelu(jnp.dot(normed, w_in[0, 0], preferred_element_type=f32)).astype(bf16)
        partial_value = jnp.dot(hidden, w_out[0, 0], preferred_element_type=f32)
        summed = inputs.astype(f32) + lax.psum(partial_value.astype(bf16), "mp").astype(f32)
        logits = jnp.dot(rms_round(summed), head[0], preferred_element_type=f32)
        returned = lax.all_to_all(
            logits.reshape(sections, slot_cap, action_width).astype(bf16),
            "section",
            split_axis=0,
            concat_axis=0,
            tiled=True,
        ).astype(f32)
        row_logits = returned[owners, slot_of]
        row_peak = lax.pmax(jnp.max(row_logits, axis=1), "mp")
        chosen = actions[step_idx].reshape(-1)
        local_total = jnp.sum(jnp.exp(row_logits - row_peak[:, None]), axis=1)
        local_pick = jnp.sum(jnp.where(columns[None, :] == chosen[:, None], row_logits, 0.0), axis=1)
        row_total, picked = lax.psum((local_total, local_pick), "mp")
        results.append((picked - row_peak - jnp.log(row_total)).reshape(game_count, 2))
        picked_rows = jnp.take(embed, actions[step_idx], axis=0).astype(f32)
        current = 0.8 * current + picked_rows + 0.5 * picked_rows[:, ::-1, :]
    return jnp.stack(results)


def solution(mesh):
    return jax.shard_map(
        plane_plan if mesh.shape["mp"] == 4 else general_plan,
        mesh=mesh,
        in_specs=(
            P("section", None),
            P(None, "section", None),
            P("section", None, "mp"),
            P(None, "mp"),
            P("section", None, None, "mp"),
            P("section", None, "mp", None),
            P("section", None, "mp"),
        ),
        out_specs=P(None, "section", None),
        check_vma=False,
    )
```

profile of v0, /device:TPU:0, one launch (start us, length us, event | category | flops | bytes accessed | tf_op | source)
XLA Modules:
  0.0 131.5 jit_solution(15690242384837333571)
XLA Ops:
  0.0 1.3 shard_map.75
  1.3 3.0 %collective-permute-start.48 = (bf16[1024,256]{1,0:T(8,128)(2,1)S(1)}, bf16[1024,256]{1,0:T(8,128)(2,1)S(1)}, u32[]{:S(2)}, u32[]{:S(2)}) collective-permute-start(bf16[1024,256]{1,0:T(8,128)(2,1)S(1)} %get-tuple-element.235), channel_id=1, source_target_pairs={{0,1},{1,0},{2,3},{3,2},{4,5},{5,4},{6,7},{7,6},{8,9},{9,8},{10,11... | collective-permute-start | bytes 1572872 | tf_op jit(solution)/shard_map/ppermute | solution.py:380
  4.3 1.5 %collective-permute-start.51 = (bf16[1024,256]{1,0:T(8,128)(2,1)S(1)}, bf16[1024,256]{1,0:T(8,128)(2,1)}, u32[]{:S(2)}, u32[]{:S(2)}) collective-permute-start(bf16[1024,256]{1,0:T(8,128)(2,1)S(1)} %get-tuple-element.236), channel_id=1, source_target_pairs={{0,2},{1,3},{2,0},{3,1},{4,6},{5,7},{6,4},{7,5},{8,10},{9,11},{10,... | collective-permute-start | bytes 1572872 | tf_op jit(solution)/shard_map/ppermute | solution.py:381
  5.8 0.7 fusion.6
  6.7 0.8 copy.11.own_col
  7.5 1.0 copy-done.1
  8.6 0.7 copy-done.2
  9.2 1.9 %shard_map.73 = bf16[8,72,512]{2,1,0:T(8,128)(2,1)} custom-call(s32[1,256]{1,0:T(1,128)S(1)} %bitcast.19, s32[256,1]{1,0:T(8,128)S(1)} %copy.11.own_col, bf16[8,256]{1,0:T(8,128)(2,1)S(1)} %stack.3.meta, f32[128,2,512]{2,1,0:T(2,128)S(1)} %copy-done.1), custom_call_target="tpu_custom_call" | custom-call | tf_op jit(solution)/shard_map/pallas_call | solution.py:405
  11.1 4.9 %all-to-all-start = ((bf16[8,72,512]{2,1,0:T(8,128)(2,1)}), bf16[8,72,512]{2,1,0:T(8,128)(2,1)S(1)}, u32[]{:S(2)}, u32[]{:S(2)}) async-start(bf16[8,72,512]{2,1,0:T(8,128)(2,1)} %shard_map.73), calls=%async_computation | async-start | bytes 1179648 | tf_op jit(solution)/shard_map/all_to_all | solution.py:408
  16.0 0.5 collective-permute-start.50
  16.5 0.5 collective-permute-start.49
  17.0 1.5 %collective-permute-start.52 = (bf16[1024,256]{1,0:T(8,128)(2,1)S(1)}, bf16[1024,256]{1,0:T(8,128)(2,1)}, u32[]{:S(2)}, u32[]{:S(2)}) collective-permute-start(bf16[1024,256]{1,0:T(8,128)(2,1)S(1)} %collective-permute-done.48), channel_id=1, source_target_pairs={{0,2},{1,3},{2,0},{3,1},{4,6},{5,7},{6,4},{7,5},{8,10},{9,11},{10,... | collective-permute-start | bytes 1572872 | tf_op jit(solution)/shard_map/ppermute | solution.py:381
  18.5 1.5 %collective-permute-start.53 = (bf16[1024,256]{1,0:T(8,128)(2,1)}, bf16[1024,256]{1,0:T(8,128)(2,1)}, u32[]{:S(2)}, u32[]{:S(2)}) collective-permute-start(bf16[1024,256]{1,0:T(8,128)(2,1)} %collective-permute-done.51), channel_id=1, source_target_pairs={{0,1},{1,0},{2,3},{3,2},{4,5},{5,4},{6,7},{7,6},{8,9},{9,8},{10,11... | collective-permute-start | bytes 1572872 | tf_op jit(solution)/shard_map/ppermute | solution.py:380
  20.0 12.7 %all-to-all-done.arrived = bf16[8,72,512]{2,1,0:T(8,128)(2,1)S(1)} async-done(((bf16[8,72,512]{2,1,0:T(8,128)(2,1)}), bf16[8,72,512]{2,1,0:T(8,128)(2,1)S(1)}, u32[]{:S(2)}, u32[]{:S(2)}) %all-to-all-start) | async-done | bytes 589856 | tf_op jit(solution)/shard_map/all_to_all | solution.py:408
  32.7 1.6 %shard_map.74 = (bf16[512,512]{1,0:T(8,128)(2,1)S(1)}, bf16[512,512]{1,0:T(8,128)(2,1)S(1)}, f32[128,8]{1,0:T(8,128)S(1)}, s32[1,512]{1,0:T(1,128)S(1)}, s32[1]{0:T(128)}) custom-call(s32[1]{0:T(128)} %bitcast.3.mp_ref, bf16[8,72,512]{2,1,0:T(8,128)(2,1)S(1)} %all-to-all-done.arrived, bf16[1024,512]{1,0:T(8,128)(2,1)S(1)} %copy-done), custom_call_target="tpu_custom_call" | custom-call | tf_op jit(solution)/shard_map/pallas_call | solution.py:409
  35.1 0.0 collective-permute-done.50
  35.1 0.0 collective-permute-done.49
  35.1 6.6 %collective-permute-done.52 = bf16[1024,256]{1,0:T(8,128)(2,1)} collective-permute-done((bf16[1024,256]{1,0:T(8,128)(2,1)S(1)}, bf16[1024,256]{1,0:T(8,128)(2,1)}, u32[]{:S(2)}, u32[]{:S(2)}) %collective-permute-start.52) | collective-permute-done | bytes 524320 | tf_op jit(solution)/shard_map/ppermute | solution.py:381
  41.7 0.2 collective-permute-done.53
  41.9 75.8 %conditional.1 = (f32[32,128]{1,0:T(8,128)S(1)}) conditional(s32[]{:T(128)} %bitcast.9, (bf16[512,512]{1,0:T(8,128)(2,1)S(1)}, bf16[512,512]{1,0:T(8,128)(2,1)S(1)}, s32[1]{0:T(128)}, bf16[2048,2048]{1,0:T(8,128)(2,1)}, bf16[2048,2048]{1,0:T(8,128)(2,1)}, /*index=5*/bf16[2048,256]{1,0:T(8,128)(2,1)}, ...), branch_computations={%region_0.1_spmd, %region_1.2_spmd, %region_2.3_spmd} | conditional | flops 17179869184 | bytes 125829872 | solution.py:425
  41.9 1.6 %collective-permute-start.17 = (bf16[384,512]{1,0:T(8,128)(2,1)S(1)}, bf16[384,512]{1,0:T(8,128)(2,1)S(1)}, u32[]{:S(2)}, u32[]{:S(2)}) collective-permute-start(bf16[384,512]{1,0:T(8,128)(2,1)S(1)} %slice.46.own), channel_id=1, source_target_pairs={{0,2},{1,3},{2,0},{3,1},{4,6},{5,7},{6,4},{7,5},{8,10},{9,11},{10,... | collective-permute-start | bytes 1179656 | tf_op jit(solution)/shard_map/cond/branch_1_fun/ppermute | solution.py:381
  43.5 0.5 collective-permute-start.16
  44.1 9.7 %collective-permute-done.17.py = bf16[384,512]{1,0:T(8,128)(2,1)S(1)} collective-permute-done((bf16[384,512]{1,0:T(8,128)(2,1)S(1)}, bf16[384,512]{1,0:T(8,128)(2,1)S(1)}, u32[]{:S(2)}, u32[]{:S(2)}) %collective-permute-start.17) | collective-permute-done | bytes 393248 | tf_op jit(solution)/shard_map/cond/branch_1_fun/ppermute | solution.py:381
  53.8 1.1 collective-permute-done.16.px
  55.0 0.6 collective-permute-start.19
  55.6 0.5 collective-permute-start.18
  56.1 1.6 %collective-permute-start.23 = (bf16[192,512]{1,0:T(8,128)(2,1)S(1)}, bf16[192,512]{1,0:T(8,128)(2,1)S(1)}, u32[]{:S(2)}, u32[]{:S(2)}) collective-permute-start(bf16[192,512]{1,0:T(8,128)(2,1)S(1)} %slice.66), channel_id=1, source_target_pairs={{0,1},{1,0},{2,3},{3,2},{4,5},{5,4},{6,7},{7,6},{8,9},{9,8},{10,11... | collective-permute-start | bytes 589832 | tf_op jit(solution)/shard_map/cond/branch_1_fun/ppermute | solution.py:380
  57.7 1.5 %collective-permute-start.22 = (bf16[192,512]{1,0:T(8,128)(2,1)S(1)}, bf16[192,512]{1,0:T(8,128)(2,1)S(1)}, u32[]{:S(2)}, u32[]{:S(2)}) collective-permute-start(bf16[192,512]{1,0:T(8,128)(2,1)S(1)} %slice.65), channel_id=1, source_target_pairs={{0,2},{1,3},{2,0},{3,1},{4,6},{5,7},{6,4},{7,5},{8,10},{9,11},{10,... | collective-permute-start | bytes 589832 | tf_op jit(solution)/shard_map/cond/branch_1_fun/ppermute | solution.py:381
  59.2 4.8 %branch_1_fun.9 = (f32[384,2048]{1,0:T(8,128)S(1)}, f32[384,1]{1,0:T(8,128)S(1)}) custom-call(s32[1]{0:T(128)} %get-tuple-element.135.mp_ref, bf16[384,512]{1,0:T(8,128)(2,1)S(1)} %slice.46.own, bf16[384,512]{1,0:T(8,128)(2,1)S(1)} %collective-permute-done.16.px, bf16[384,512]{1,0:T(8,128)(2,1)S(1)} %collective-permute-done.17.py, ...), custom_call_target="tpu_custom_call" | custom-call | flops 2415919104 | bytes 8388608 | tf_op jit(solution)/shard_map/cond/branch_1_fun/pallas_call | solution.py:302
  64.0 3.0 %collective-permute-done.19.py = bf16[384,512]{1,0:T(8,128)(2,1)S(1)} collective-permute-done((bf16[384,512]{1,0:T(8,128)(2,1)S(1)}, bf16[384,512]{1,0:T(8,128)(2,1)S(1)}, u32[]{:S(2)}, u32[]{:S(2)}) %collective-permute-start.19) | collective-permute-done | bytes 393248 | tf_op jit(solution)/shard_map/cond/branch_1_fun/ppermute | solution.py:381
  67.0 0.6 collective-permute-done.18.px
  67.7 0.6 collective-permute-start.21
  68.3 1.4 %collective-permute-start.20 = (bf16[192,512]{1,0:T(8,128)(2,1)S(1)}, bf16[192,512]{1,0:T(8,128)(2,1)S(1)}, u32[]{:S(2)}, u32[]{:S(2)}) collective-permute-start(bf16[192,512]{1,0:T(8,128)(2,1)S(1)} %slice.47), channel_id=1, source_target_pairs={{0,2},{1,3},{2,0},{3,1},{4,6},{5,7},{6,4},{7,5},{8,10},{9,11},{10,... | collective-permute-start | bytes 589832 | tf_op jit(solution)/shard_map/cond/branch_1_fun/ppermute | solution.py:381
  69.7 2.1 %collective-permute-done.23.db = bf16[192,512]{1,0:T(8,128)(2,1)S(1)} collective-permute-done((bf16[192,512]{1,0:T(8,128)(2,1)S(1)}, bf16[192,512]{1,0:T(8,128)(2,1)S(1)}, u32[]{:S(2)}, u32[]{:S(2)}) %collective-permute-start.23) | collective-permute-done | bytes 196640 | tf_op jit(solution)/shard_map/cond/branch_1_fun/ppermute | solution.py:380
  71.8 0.0 collective-permute-done.22.da
  71.8 2.5 %branch_1_fun.11 = (bf16[384,2048]{1,0:T(8,128)(2,1)S(1)}, bf16[96,2048]{1,0:T(8,128)(2,1)S(1)}) custom-call(s32[1]{0:T(128)} %get-tuple-element.135.mp_ref, f32[384,2048]{1,0:T(8,128)S(1)} %get-tuple-element.145.z, f32[384,1]{1,0:T(8,128)S(1)} %get-tuple-element.146.square, bf16[384,512]{1,0:T(8,128)(2,1)S(1)} %slice.46.own, ...), custom_call_target="tpu_custom_call" | custom-call | flops 805306368 | bytes 2097152 | tf_op jit(solution)/shard_map/cond/branch_1_fun/pallas_call | solution.py:315
  74.4 4.0 %branch_1_fun.12 = (bf16[192,1024]{1,0:T(8,128)(2,1)S(1)}, bf16[192,1024]{1,0:T(8,128)(2,1)S(1)}, bf16[192,1024]{1,0:T(8,128)(2,1)S(1)}, bf16[192,1024]{1,0:T(8,128)(2,1)S(1)}) custom-call(bf16[384,2048]{1,0:T(8,128)(2,1)S(1)} %get-tuple-element.149.hidden, bf16[2048,2048]{1,0:T(8,128)(2,1)S(1)} %bitcast.34), custom_call_target="tpu_custom_call" | custom-call | flops 3221225472 | bytes 8388608 | tf_op jit(solution)/shard_map/cond/branch_1_fun/pallas_call | solution.py:324
  78.4 0.6 collective-permute-start.24
  79.0 1.4 %collective-permute-start.25 = (bf16[192,1024]{1,0:T(8,128)(2,1)S(1)}, bf16[192,1024]{1,0:T(8,128)(2,1)S(1)}, u32[]{:S(2)}, u32[]{:S(2)}) collective-permute-start(bf16[192,1024]{1,0:T(8,128)(2,1)S(1)} %get-tuple-element.152), channel_id=1, source_target_pairs={{0,2},{1,3},{2,0},{3,1},{4,6},{5,7},{6,4},{7,5},{8,10},{9,11},{10,... | collective-permute-start | bytes 1179656 | tf_op jit(solution)/shard_map/cond/branch_1_fun/ppermute | solution.py:381
  80.4 0.0 collective-permute-done.21.db
  80.4 0.0 collective-permute-done.20.da
  80.4 5.1 %branch_1_fun.10 = (bf16[384,2048]{1,0:T(8,128)(2,1)S(1)}, bf16[96,2048]{1,0:T(8,128)(2,1)S(1)}) custom-call(s32[1]{0:T(128)} %get-tuple-element.135.mp_ref, bf16[384,512]{1,0:T(8,128)(2,1)S(1)} %slice.45.own, bf16[384,512]{1,0:T(8,128)(2,1)S(1)} %collective-permute-done.18.px, bf16[384,512]{1,0:T(8,128)(2,1)S(1)} %collective-permute-done.19.py, ...), custom_call_target="tpu_custom_call" | custom-call | flops 3221225472 | bytes 8388608 | tf_op jit(solution)/shard_map/cond/branch_1_fun/pallas_call | solution.py:293
  85.5 3.2 %collective-permute-done.24.got_a = bf16[192,1024]{1,0:T(8,128)(2,1)S(1)} collective-permute-done((bf16[192,1024]{1,0:T(8,128)(2,1)S(1)}, bf16[192,1024]{1,0:T(8,128)(2,1)S(1)}, u32[]{:S(2)}, u32[]{:S(2)}) %collective-permute-start.24) | collective-permute-done | bytes 393248 | tf_op jit(solution)/shard_map/cond/branch_1_fun/ppermute | solution.py:380
  88.8 0.9 collective-permute-done.25.got_b
  89.6 0.1 branch_1_fun.13
  89.7 3.9 %branch_1_fun.14 = (bf16[192,1024]{1,0:T(8,128)(2,1)S(1)}, bf16[192,1024]{1,0:T(8,128)(2,1)S(1)}, bf16[192,1024]{1,0:T(8,128)(2,1)S(1)}, bf16[192,1024]{1,0:T(8,128)(2,1)S(1)}) custom-call(bf16[384,2048]{1,0:T(8,128)(2,1)S(1)} %get-tuple-element.159.hidden, bf16[2048,2048]{1,0:T(8,128)(2,1)S(1)} %bitcast.34), custom_call_target="tpu_custom_call" | custom-call | flops 3221225472 | bytes 8388608 | tf_op jit(solution)/shard_map/cond/branch_1_fun/pallas_call | solution.py:324
  93.7 0.0 copy-start.8
  93.7 1.5 %collective-permute-start.26 = (bf16[192,1024]{1,0:T(8,128)(2,1)S(1)}, bf16[192,1024]{1,0:T(8,128)(2,1)S(1)}, u32[]{:S(2)}, u32[]{:S(2)}) collective-permute-start(bf16[192,1024]{1,0:T(8,128)(2,1)S(1)} %get-tuple-element.161), channel_id=1, source_target_pairs={{0,1},{1,0},{2,3},{3,2},{4,5},{5,4},{6,7},{7,6},{8,9},{9,8},{10,11... | collective-permute-start | bytes 1179656 | tf_op jit(solution)/shard_map/cond/branch_1_fun/ppermute | solution.py:380
  95.2 1.6 %collective-permute-start.27 = (bf16[192,1024]{1,0:T(8,128)(2,1)S(1)}, bf16[192,1024]{1,0:T(8,128)(2,1)S(1)}, u32[]{:S(2)}, u32[]{:S(2)}) collective-permute-start(bf16[192,1024]{1,0:T(8,128)(2,1)S(1)} %get-tuple-element.163), channel_id=1, source_target_pairs={{0,2},{1,3},{2,0},{3,1},{4,6},{5,7},{6,4},{7,5},{8,10},{9,11},{10,... | collective-permute-start | bytes 1179656 | tf_op jit(solution)/shard_map/cond/branch_1_fun/ppermute | solution.py:381
  96.9 0.5 collective-permute-start.31
  97.4 0.4 collective-permute-start.30
  97.8 5.2 %collective-permute-done.26.got_a = bf16[192,1024]{1,0:T(8,128)(2,1)S(1)} collective-permute-done((bf16[192,1024]{1,0:T(8,128)(2,1)S(1)}, bf16[192,1024]{1,0:T(8,128)(2,1)S(1)}, u32[]{:S(2)}, u32[]{:S(2)}) %collective-permute-start.26) | collective-permute-done | bytes 393248 | tf_op jit(solution)/shard_map/cond/branch_1_fun/ppermute | solution.py:380
  103.0 1.7 %collective-permute-done.27.got_b = bf16[192,1024]{1,0:T(8,128)(2,1)S(1)} collective-permute-done((bf16[192,1024]{1,0:T(8,128)(2,1)S(1)}, bf16[192,1024]{1,0:T(8,128)(2,1)S(1)}, u32[]{:S(2)}, u32[]{:S(2)}) %collective-permute-start.27) | collective-permute-done | bytes 393248 | tf_op jit(solution)/shard_map/cond/branch_1_fun/ppermute | solution.py:381
  104.8 0.1 branch_1_fun.15
  104.8 1.9 %collective-permute-start.28 = (bf16[96,1024]{1,0:T(8,128)(2,1)S(1)}, bf16[96,1024]{1,0:T(8,128)(2,1)S(1)}, u32[]{:S(2)}, u32[]{:S(2)}) collective-permute-start(bf16[96,1024]{1,0:T(8,128)(2,1)S(1)} %get-tuple-element.164), channel_id=1, source_target_pairs={{0,2},{1,3},{2,0},{3,1},{4,6},{5,7},{6,4},{7,5},{8,10},{9,11},{10,... | collective-permute-start | bytes 589832 | tf_op jit(solution)/shard_map/cond/branch_1_fun/ppermute | solution.py:381
  106.8 0.6 collective-permute-start.29
  107.3 1.6 %collective-permute-done.30.last_a = bf16[96,1024]{1,0:T(8,128)(2,1)S(1)} collective-permute-done((bf16[96,1024]{1,0:T(8,128)(2,1)S(1)}, bf16[96,1024]{1,0:T(8,128)(2,1)S(1)}, u32[]{:S(2)}, u32[]{:S(2)}) %collective-permute-start.30) | collective-permute-done | bytes 196640 | tf_op jit(solution)/shard_map/cond/branch_1_fun/ppermute | solution.py:381
  109.0 3.0 %branch_1_fun.16.rest_0_ = f32[8,64]{1,0:T(8,128)S(1)} custom-call(s32[1]{0:T(128)} %get-tuple-element.135.mp_ref, bf16[96,2048]{1,0:T(8,128)(2,1)S(1)} %get-tuple-element.175.mine, bf16[192,1024]{1,0:T(8,128)(2,1)S(1)} %get-tuple-element.154.keep_a, bf16[192,1024]{1,0:T(8,128)(2,1)S(1)} %collective-permute-done.24.got_a, ...), custom_call_target="tpu_custom_call" | custom-call | tf_op jit(solution)/shard_map/cond/branch_1_fun/pallas_call | solution.py:342
  112.0 1.2 collective-permute-done.28.last_a
  113.2 1.0 collective-permute-done.29.last_b
  114.2 3.0 %branch_1_fun.17 = f32[32,128]{1,0:T(8,128)S(1)} custom-call(s32[1]{0:T(128)} %get-tuple-element.135.mp_ref, bf16[96,2048]{1,0:T(8,128)(2,1)S(1)} %get-tuple-element.143.mine, bf16[192,1024]{1,0:T(8,128)(2,1)S(1)} %get-tuple-element.160.keep_a, bf16[192,1024]{1,0:T(8,128)(2,1)S(1)} %collective-permute-done.26.got_a, ...), custom_call_target="tpu_custom_call" | custom-call | tf_op jit(solution)/shard_map/cond/branch_1_fun/pallas_call | solution.py:342
  117.7 12.7 %all_to_all.16 = f32[32,1,128]{2,1,0:T(1,128)S(1)} all-to-all(f32[32,1,128]{2,1,0:T(1,128)S(1)} %bitcast.35), channel_id=1, replica_groups=mesh['section'=8,'mp'=4] {'section','mp'}, dimensions={0} | all-to-all | bytes 32768 | tf_op jit(solution)/shard_map/all_to_all | solution.py:426
  130.4 0.5 shard_map.76
  130.9 0.6 reshape.322
  (33 shorter events, 0.3 us)
Async XLA Ops:
  0.0 32.7 %copy-start = (bf16[1024,512]{1,0:T(8,128)(2,1)S(1)}, bf16[1024,512]{1,0:T(8,128)(2,1)}, u32[]{:S(2)}) copy-start(bf16[1024,512]{1,0:T(8,128)(2,1)} %embed.1) | copy-start | bytes 3145732
  1.3 15.7 %collective-permute-start.48 = (bf16[1024,256]{1,0:T(8,128)(2,1)S(1)}, bf16[1024,256]{1,0:T(8,128)(2,1)S(1)}, u32[]{:S(2)}, u32[]{:S(2)}) collective-permute-start(bf16[1024,256]{1,0:T(8,128)(2,1)S(1)} %get-tuple-element.235), channel_id=1, source_target_pairs={{0,1},{1,0},{2,3},{3,2},{4,5},{5,4},{6,7},{7,6},{8,9},{9,8},{10,11... | collective-permute-start | bytes 1572872 | tf_op jit(solution)/shard_map/ppermute | solution.py:380
  4.3 14.2 %collective-permute-start.51 = (bf16[1024,256]{1,0:T(8,128)(2,1)S(1)}, bf16[1024,256]{1,0:T(8,128)(2,1)}, u32[]{:S(2)}, u32[]{:S(2)}) collective-permute-start(bf16[1024,256]{1,0:T(8,128)(2,1)S(1)} %get-tuple-element.236), channel_id=1, source_target_pairs={{0,2},{1,3},{2,0},{3,1},{4,6},{5,7},{6,4},{7,5},{8,10},{9,11},{10,... | collective-permute-start | bytes 1572872 | tf_op jit(solution)/shard_map/ppermute | solution.py:381
  7.5 1.0 copy-start.1
  8.6 0.7 copy-start.2
  11.1 21.6 %all-to-all-start = ((bf16[8,72,512]{2,1,0:T(8,128)(2,1)}), bf16[8,72,512]{2,1,0:T(8,128)(2,1)S(1)}, u32[]{:S(2)}, u32[]{:S(2)}) async-start(bf16[8,72,512]{2,1,0:T(8,128)(2,1)} %shard_map.73), calls=%async_computation | async-start | bytes 1179648 | tf_op jit(solution)/shard_map/all_to_all | solution.py:408
  16.0 19.1 %collective-permute-start.50 = (bf16[1024,256]{1,0:T(8,128)(2,1)S(1)}, bf16[1024,256]{1,0:T(8,128)(2,1)}, u32[]{:S(2)}, u32[]{:S(2)}) collective-permute-start(bf16[1024,256]{1,0:T(8,128)(2,1)S(1)} %get-tuple-element.235), channel_id=1, source_target_pairs={{0,2},{1,3},{2,0},{3,1},{4,6},{5,7},{6,4},{7,5},{8,10},{9,11},{10,... | collective-permute-start | bytes 1572872 | tf_op jit(solution)/shard_map/ppermute | solution.py:381
  16.5 18.6 %collective-permute-start.49 = (bf16[1024,256]{1,0:T(8,128)(2,1)S(1)}, bf16[1024,256]{1,0:T(8,128)(2,1)}, u32[]{:S(2)}, u32[]{:S(2)}) collective-permute-start(bf16[1024,256]{1,0:T(8,128)(2,1)S(1)} %get-tuple-element.236), channel_id=1, source_target_pairs={{0,1},{1,0},{2,3},{3,2},{4,5},{5,4},{6,7},{7,6},{8,9},{9,8},{10,11... | collective-permute-start | bytes 1572872 | tf_op jit(solution)/shard_map/ppermute | solution.py:380
  17.0 24.6 %collective-permute-start.52 = (bf16[1024,256]{1,0:T(8,128)(2,1)S(1)}, bf16[1024,256]{1,0:T(8,128)(2,1)}, u32[]{:S(2)}, u32[]{:S(2)}) collective-permute-start(bf16[1024,256]{1,0:T(8,128)(2,1)S(1)} %collective-permute-done.48), channel_id=1, source_target_pairs={{0,2},{1,3},{2,0},{3,1},{4,6},{5,7},{6,4},{7,5},{8,10},{9,11},{10,... | collective-permute-start | bytes 1572872 | tf_op jit(solution)/shard_map/ppermute | solution.py:381
  18.5 23.3 %collective-permute-start.53 = (bf16[1024,256]{1,0:T(8,128)(2,1)}, bf16[1024,256]{1,0:T(8,128)(2,1)}, u32[]{:S(2)}, u32[]{:S(2)}) collective-permute-start(bf16[1024,256]{1,0:T(8,128)(2,1)} %collective-permute-done.51), channel_id=1, source_target_pairs={{0,1},{1,0},{2,3},{3,2},{4,5},{5,4},{6,7},{7,6},{8,9},{9,8},{10,11... | collective-permute-start | bytes 1572872 | tf_op jit(solution)/shard_map/ppermute | solution.py:380
  41.9 88.5 %copy-start.3 = (s32[128,2]{0,1:T(2,128)S(1)}, s32[128,2]{0,1:T(2,128)}, u32[]{:S(2)}) copy-start(s32[128,2]{0,1:T(2,128)} %param.10) | copy-start | bytes 3076
  41.9 11.9 %collective-permute-start.17 = (bf16[384,512]{1,0:T(8,128)(2,1)S(1)}, bf16[384,512]{1,0:T(8,128)(2,1)S(1)}, u32[]{:S(2)}, u32[]{:S(2)}) collective-permute-start(bf16[384,512]{1,0:T(8,128)(2,1)S(1)} %slice.46.own), channel_id=1, source_target_pairs={{0,2},{1,3},{2,0},{3,1},{4,6},{5,7},{6,4},{7,5},{8,10},{9,11},{10,... | collective-permute-start | bytes 1179656 | tf_op jit(solution)/shard_map/cond/branch_1_fun/ppermute | solution.py:381
  43.5 11.5 %collective-permute-start.16 = (bf16[384,512]{1,0:T(8,128)(2,1)S(1)}, bf16[384,512]{1,0:T(8,128)(2,1)S(1)}, u32[]{:S(2)}, u32[]{:S(2)}) collective-permute-start(bf16[384,512]{1,0:T(8,128)(2,1)S(1)} %slice.46.own), channel_id=1, source_target_pairs={{0,1},{1,0},{2,3},{3,2},{4,5},{5,4},{6,7},{7,6},{8,9},{9,8},{10,11... | collective-permute-start | bytes 1179656 | tf_op jit(solution)/shard_map/cond/branch_1_fun/ppermute | solution.py:380
  55.0 12.0 %collective-permute-start.19 = (bf16[384,512]{1,0:T(8,128)(2,1)S(1)}, bf16[384,512]{1,0:T(8,128)(2,1)S(1)}, u32[]{:S(2)}, u32[]{:S(2)}) collective-permute-start(bf16[384,512]{1,0:T(8,128)(2,1)S(1)} %slice.45.own), channel_id=1, source_target_pairs={{0,2},{1,3},{2,0},{3,1},{4,6},{5,7},{6,4},{7,5},{8,10},{9,11},{10,... | collective-permute-start | bytes 1179656 | tf_op jit(solution)/shard_map/cond/branch_1_fun/ppermute | solution.py:381
  55.6 12.1 %collective-permute-start.18 = (bf16[384,512]{1,0:T(8,128)(2,1)S(1)}, bf16[384,512]{1,0:T(8,128)(2,1)S(1)}, u32[]{:S(2)}, u32[]{:S(2)}) collective-permute-start(bf16[384,512]{1,0:T(8,128)(2,1)S(1)} %slice.45.own), channel_id=1, source_target_pairs={{0,1},{1,0},{2,3},{3,2},{4,5},{5,4},{6,7},{7,6},{8,9},{9,8},{10,11... | collective-permute-start | bytes 1179656 | tf_op jit(solution)/shard_map/cond/branch_1_fun/ppermute | solution.py:380
  56.1 15.7 %collective-permute-start.23 = (bf16[192,512]{1,0:T(8,128)(2,1)S(1)}, bf16[192,512]{1,0:T(8,128)(2,1)S(1)}, u32[]{:S(2)}, u32[]{:S(2)}) collective-permute-start(bf16[192,512]{1,0:T(8,128)(2,1)S(1)} %slice.66), channel_id=1, source_target_pairs={{0,1},{1,0},{2,3},{3,2},{4,5},{5,4},{6,7},{7,6},{8,9},{9,8},{10,11... | collective-permute-start | bytes 589832 | tf_op jit(solution)/shard_map/cond/branch_1_fun/ppermute | solution.py:380
  57.7 14.1 %collective-permute-start.22 = (bf16[192,512]{1,0:T(8,128)(2,1)S(1)}, bf16[192,512]{1,0:T(8,128)(2,1)S(1)}, u32[]{:S(2)}, u32[]{:S(2)}) collective-permute-start(bf16[192,512]{1,0:T(8,128)(2,1)S(1)} %slice.65), channel_id=1, source_target_pairs={{0,2},{1,3},{2,0},{3,1},{4,6},{5,7},{6,4},{7,5},{8,10},{9,11},{10,... | collective-permute-start | bytes 589832 | tf_op jit(solution)/shard_map/cond/branch_1_fun/ppermute | solution.py:381
  59.2 12.7 %copy-start.5 = (bf16[2048,2048]{1,0:T(8,128)(2,1)S(1)}, bf16[2048,2048]{1,0:T(8,128)(2,1)}, u32[]{:S(2)}) copy-start(bf16[2048,2048]{1,0:T(8,128)(2,1)} %get-tuple-element.139.w_in) | copy-start | bytes 25165828 | tf_op jit(solution)/shard_map/cond
  59.2 15.2 %slice-start.2 = ((s8[8388608]{0:T(1024)(128)(4,1)}), s8[4194304]{0:T(1024)(128)(4,1)S(1)}, s32[]{:S(2)}) async-start(s8[8388608]{0:T(1024)(128)(4,1)} %bitcast.33), calls=%async_computation.4 | async-start | bytes 8388608 | tf_op jit(solution)/shard_map/cond
  67.7 12.7 %collective-permute-start.21 = (bf16[192,512]{1,0:T(8,128)(2,1)S(1)}, bf16[192,512]{1,0:T(8,128)(2,1)S(1)}, u32[]{:S(2)}, u32[]{:S(2)}) collective-permute-start(bf16[192,512]{1,0:T(8,128)(2,1)S(1)} %slice.48), channel_id=1, source_target_pairs={{0,1},{1,0},{2,3},{3,2},{4,5},{5,4},{6,7},{7,6},{8,9},{9,8},{10,11... | collective-permute-start | bytes 589832 | tf_op jit(solution)/shard_map/cond/branch_1_fun/ppermute | solution.py:380
  68.3 12.1 %collective-permute-start.20 = (bf16[192,512]{1,0:T(8,128)(2,1)S(1)}, bf16[192,512]{1,0:T(8,128)(2,1)S(1)}, u32[]{:S(2)}, u32[]{:S(2)}) collective-permute-start(bf16[192,512]{1,0:T(8,128)(2,1)S(1)} %slice.47), channel_id=1, source_target_pairs={{0,2},{1,3},{2,0},{3,1},{4,6},{5,7},{6,4},{7,5},{8,10},{9,11},{10,... | collective-permute-start | bytes 589832 | tf_op jit(solution)/shard_map/cond/branch_1_fun/ppermute | solution.py:381
  71.8 2.6 %slice-start.3 = ((s8[8388608]{0:T(1024)(128)(4,1)}), s8[4194304]{0:T(1024)(128)(4,1)S(1)}, s32[]{:S(2)}) async-start(s8[8388608]{0:T(1024)(128)(4,1)} %bitcast.33), calls=%async_computation.5 | async-start | bytes 8388608 | tf_op jit(solution)/shard_map/cond
  78.4 10.4 %collective-permute-start.24 = (bf16[192,1024]{1,0:T(8,128)(2,1)S(1)}, bf16[192,1024]{1,0:T(8,128)(2,1)S(1)}, u32[]{:S(2)}, u32[]{:S(2)}) collective-permute-start(bf16[192,1024]{1,0:T(8,128)(2,1)S(1)} %get-tuple-element.151), channel_id=1, source_target_pairs={{0,1},{1,0},{2,3},{3,2},{4,5},{5,4},{6,7},{7,6},{8,9},{9,8},{10,11... | collective-permute-start | bytes 1179656 | tf_op jit(solution)/shard_map/cond/branch_1_fun/ppermute | solution.py:380
  79.0 10.7 %collective-permute-start.25 = (bf16[192,1024]{1,0:T(8,128)(2,1)S(1)}, bf16[192,1024]{1,0:T(8,128)(2,1)S(1)}, u32[]{:S(2)}, u32[]{:S(2)}) collective-permute-start(bf16[192,1024]{1,0:T(8,128)(2,1)S(1)} %get-tuple-element.152), channel_id=1, source_target_pairs={{0,2},{1,3},{2,0},{3,1},{4,6},{5,7},{6,4},{7,5},{8,10},{9,11},{10,... | collective-permute-start | bytes 1179656 | tf_op jit(solution)/shard_map/cond/branch_1_fun/ppermute | solution.py:381
  93.7 15.3 %copy-start.8 = (bf16[2048,256]{1,0:T(8,128)(2,1)S(1)}, bf16[2048,256]{1,0:T(8,128)(2,1)}, u32[]{:S(2)}) copy-start(bf16[2048,256]{1,0:T(8,128)(2,1)} %get-tuple-element.166.h0) | copy-start | bytes 3145732 | tf_op jit(solution)/shard_map/cond
  93.7 9.3 %collective-permute-start.26 = (bf16[192,1024]{1,0:T(8,128)(2,1)S(1)}, bf16[192,1024]{1,0:T(8,128)(2,1)S(1)}, u32[]{:S(2)}, u32[]{:S(2)}) collective-permute-start(bf16[192,1024]{1,0:T(8,128)(2,1)S(1)} %get-tuple-element.161), channel_id=1, source_target_pairs={{0,1},{1,0},{2,3},{3,2},{4,5},{5,4},{6,7},{7,6},{8,9},{9,8},{10,11... | collective-permute-start | bytes 1179656 | tf_op jit(solution)/shard_map/cond/branch_1_fun/ppermute | solution.py:380
  95.2 9.5 %collective-permute-start.27 = (bf16[192,1024]{1,0:T(8,128)(2,1)S(1)}, bf16[192,1024]{1,0:T(8,128)(2,1)S(1)}, u32[]{:S(2)}, u32[]{:S(2)}) collective-permute-start(bf16[192,1024]{1,0:T(8,128)(2,1)S(1)} %get-tuple-element.163), channel_id=1, source_target_pairs={{0,2},{1,3},{2,0},{3,1},{4,6},{5,7},{6,4},{7,5},{8,10},{9,11},{10,... | collective-permute-start | bytes 1179656 | tf_op jit(solution)/shard_map/cond/branch_1_fun/ppermute | solution.py:381
  96.9 10.4 %collective-permute-start.31 = (bf16[96,1024]{1,0:T(8,128)(2,1)S(1)}, bf16[96,1024]{1,0:T(8,128)(2,1)S(1)}, u32[]{:S(2)}, u32[]{:S(2)}) collective-permute-start(bf16[96,1024]{1,0:T(8,128)(2,1)S(1)} %get-tuple-element.176), channel_id=1, source_target_pairs={{0,1},{1,0},{2,3},{3,2},{4,5},{5,4},{6,7},{7,6},{8,9},{9,8},{10,11... | collective-permute-start | bytes 589832 | tf_op jit(solution)/shard_map/cond/branch_1_fun/ppermute | solution.py:380
  97.4 11.5 %collective-permute-start.30 = (bf16[96,1024]{1,0:T(8,128)(2,1)S(1)}, bf16[96,1024]{1,0:T(8,128)(2,1)S(1)}, u32[]{:S(2)}, u32[]{:S(2)}) collective-permute-start(bf16[96,1024]{1,0:T(8,128)(2,1)S(1)} %get-tuple-element.158), channel_id=1, source_target_pairs={{0,2},{1,3},{2,0},{3,1},{4,6},{5,7},{6,4},{7,5},{8,10},{9,11},{10,... | collective-permute-start | bytes 589832 | tf_op jit(solution)/shard_map/cond/branch_1_fun/ppermute | solution.py:381
  104.8 8.3 %collective-permute-start.28 = (bf16[96,1024]{1,0:T(8,128)(2,1)S(1)}, bf16[96,1024]{1,0:T(8,128)(2,1)S(1)}, u32[]{:S(2)}, u32[]{:S(2)}) collective-permute-start(bf16[96,1024]{1,0:T(8,128)(2,1)S(1)} %get-tuple-element.164), channel_id=1, source_target_pairs={{0,2},{1,3},{2,0},{3,1},{4,6},{5,7},{6,4},{7,5},{8,10},{9,11},{10,... | collective-permute-start | bytes 589832 | tf_op jit(solution)/shard_map/cond/branch_1_fun/ppermute | solution.py:381
  106.8 7.4 %collective-permute-start.29 = (bf16[96,1024]{1,0:T(8,128)(2,1)S(1)}, bf16[96,1024]{1,0:T(8,128)(2,1)S(1)}, u32[]{:S(2)}, u32[]{:S(2)}) collective-permute-start(bf16[96,1024]{1,0:T(8,128)(2,1)S(1)} %get-tuple-element.165), channel_id=1, source_target_pairs={{0,1},{1,0},{2,3},{3,2},{4,5},{5,4},{6,7},{7,6},{8,9},{9,8},{10,11... | collective-permute-start | bytes 589832 | tf_op jit(solution)/shard_map/cond/branch_1_fun/ppermute | solution.py:380
where the time goes:
time: 132 us
  waiting for transfers between devices  51 us (39%)
  Pallas kernels  32 us (24%)
  starting transfers between devices  30.4 us (23%)
  blocking collectives  12.7 us (10%)
  local copies, waits for them, and re-layouts  4.03 us (3%)
    ppermute x11, waiting for transfers between devices, plane_plan(): over_y = lambda v: lax.ppermute(v, 'mp', [(i, i ^ 2) for i in range(4)])  24.7 us
    ppermute x11, starting transfers between devices, plane_plan(): over_y = lambda v: lax.ppermute(v, 'mp', [(i, i ^ 2) for i in range(4)])  14 us
    ppermute x11, waiting for transfers between devices, plane_plan(): over_x = lambda v: lax.ppermute(v, 'mp', [(i, i ^ 1) for i in range(4)])  13.6 us
    all_to_all x1, waiting for transfers between devices, plane_plan(): lax.all_to_all(packed, 'section', split_axis=0, concat_axis=0, tiled=True)  12.7 us
    all_to_all x1, blocking collectives, plane_plan(): lax.all_to_all(sent, ('section', 'mp'), split_axis=0, concat_axis=0, tile...  12.7 us
    ppermute x11, starting transfers between devices, plane_plan(): over_x = lambda v: lax.ppermute(v, 'mp', [(i, i ^ 1) for i in range(4)])  11.5 us
    pallas_call x2, Pallas kernels, to_parts(): call(functools.partial(part_kernel, size, TILE), (shape(h, width // 2),)...  7.9 us
    pallas_call x2, Pallas kernels, score(): call(functools.partial(score_kernel, sections, cap, step_idx), shape(4 *...  6.06 us
  transfers between devices with their start and end apart: 23, of which 15 were waited for; matrix products, arithmetic and copies ran while one was open for 1% of the time, Pallas kernels for 18%

commit v1 on v0

--- a/solution.py
+++ b/solution.py
@@ -33,21 +33,43 @@
     return lax.dot_general(left, right, (((1,), (1,)), ((), ())), preferred_element_type=f32)
 
 
-def slots_row(own_row, own_col):
+def slots_row(own_row):
     rows = own_row.shape[1]
-    earlier = (own_col == own_row) & (iota((rows, rows), 0) < iota((rows, rows), 1))
+    lower, upper = iota((rows, rows), 0), iota((rows, rows), 1)
+    own_col = jnp.sum(jnp.where(lower == upper, own_row, 0), axis=1, keepdims=True)
+    earlier = (own_col == own_row) & (lower < upper)
     return jnp.sum(earlier.astype(jnp.int32), axis=0, keepdims=True)
 
 
-def pack_kernel(sections, cap, own_row, own_col, meta, state, out):
-    games, _, feat = state.shape
+def owners_row(pair):
+    return jnp.concatenate([pair[0:1, :], pair[1:2, :]], axis=1)
+
+
+def pack_kernel(sections, cap, agents, acts, state, out, agents_here, acts_here, state_here, done):
+    copies = [
+        pltpu.make_async_copy(far, here, done.at[i])
+        for i, (far, here) in enumerate(((agents, agents_here), (acts, acts_here), (state, state_here)))
+    ]
+    for copy in copies:
+        copy.start()
+    games, _, feat = state_here.shape
     rows = 2 * games
-    dest = own_row[...] * cap + slots_row(own_row[...], own_col[...])
+    copies[0].wait()
+    own_row = owners_row(agents_here)
+    dest = own_row * cap + slots_row(own_row)
     select = (iota((sections * cap, rows), 0) == dest).astype(bf16)
-    first = jnp.dot(select[:, :games], state[:, 0, :].astype(bf16), preferred_element_type=f32)
-    second = jnp.dot(select[:, games:], state[:, 1, :].astype(bf16), preferred_element_type=f32)
-    packed = (first + second).astype(bf16)
-    notes = nt_dot(meta[...], select).astype(bf16)
+    copies[1].wait()
+    first, second = (acts_here[0, p : p + 1, :] for p in range(2))
+    mine0 = jnp.concatenate([first, second], axis=1)
+    other0 = jnp.concatenate([second, first], axis=1)
+    mine1 = jnp.concatenate([acts_here[1, 0:1, :], acts_here[1, 1:2, :]], axis=1)
+    digits = [v for a in (mine0, other0, mine1) for v in (a // DIGIT, a % DIGIT)]
+    meta = jnp.concatenate(digits + [jnp.zeros_like(mine0), jnp.ones_like(mine0)], axis=0).astype(f32).astype(bf16)
+    notes = nt_dot(meta, select).astype(bf16)
+    copies[2].wait()
+    packed = jnp.dot(select[:, :games], state_here[:, 0, :].astype(bf16), preferred_element_type=f32)
+    packed = packed + jnp.dot(select[:, games:], state_here[:, 1, :].astype(bf16), preferred_element_type=f32)
+    packed = packed.astype(bf16)
     for s in range(sections):
         out[s, :cap, :] = packed[s * cap : (s + 1) * cap]
         out[s, cap:, :] = jnp.zeros((META, feat), bf16)
@@ -116,7 +138,16 @@
         hidden[:, cols] = jax.nn.gelu(z * scale[...]).astype(bf16)
 
 
-def near_kernel(size, tile, mp_ref, own, px, py, w_in, z, square, chunks, w_here, arrived):
+def near_kernel(size, tile, mp_ref, own, px, py, w_in, *rest):
+    *ends, chunks, w_here, arrived, halved = rest
+    halves = []
+    if len(ends) == 6:
+        first, second, z, square, left, right = ends
+        h = left.shape[0]
+        halves.append(pltpu.make_async_copy(first.at[pl.ds(0, h)], left, halved.at[0]))
+        halves.append(pltpu.make_async_copy(second.at[pl.ds(h, h)], right, halved.at[1]))
+    else:
+        z, square = ends
     feat = own.shape[1]
     group = size // 4
     m = mp_ref[0]
@@ -130,6 +161,8 @@
     for t in range(tiles):
         for k in range(3):
             fetch(k, t).start()
+    for copy in halves:
+        copy.start()
     total = jnp.zeros((size, 1), f32)
     for k, src in enumerate((own, px, py)):
         for j in range(4):
@@ -144,6 +177,9 @@
         for k in range(3):
             fetch(k, t).wait()
         z[:, cols] = sum(jnp.dot(chunks[k], w_here[k, :, cols], preferred_element_type=f32) for k in range(3))
+
+    for copy in halves:
+        copy.wait()
 
 
 def far_kernel(size, tile, mp_ref, z, square, own, px, py, da, db, w_in, hidden, mine, chunk, scale):
@@ -191,7 +227,7 @@
     out_b[...] = (keep_b[...].astype(f32) + got_b[...].astype(f32)).astype(bf16)
 
 
-def score_kernel(sections, cap, step_idx, mp_ref, mine, keep_a, got_a, last_a, keep_b, got_b, last_b, h0, h1_top, h1_bottom, h2_top, h2_bottom, h3_top, h3_bottom, notes, place, *rest):
+def score_kernel(sections, cap, step_idx, mp_ref, mine, keep_a, got_a, last_a, keep_b, got_b, last_b, h0, h1, h2, h3_top, h3_bottom, notes, place, *rest):
     earlier, out = rest[:-1], rest[-1]
     group, width = mine.shape
     half = width // 2
@@ -209,7 +245,7 @@
     c = 4 * step_idx
     chosen = (notes[:, c : c + 1] * DIGIT + notes[:, c + 1 : c + 2]).astype(jnp.int32)
     logits = []
-    heads = ((h0[:half], h0[half:]), (h1_top[...], h1_bottom[...]), (h2_top[...], h2_bottom[...]), (h3_top[...], h3_bottom[...]))
+    heads = ((h0[:half], h0[half:]), (h1[:half], h1[half:]), (h2[:half], h2[half:]), (h3_top[...], h3_bottom[...]))
     for top, bottom in heads:
         logits.append(
             jnp.dot(na, top, preferred_element_type=f32) + jnp.dot(nb, bottom, preferred_element_type=f32)
@@ -234,26 +270,16 @@
         out[4 * s : 4 * s + 4, :] = jnp.broadcast_to(row, (4, 2 * cap))
 
 
-def return_kernel(sections, cap, own_row, own_col, got, out):
+def return_kernel(sections, cap, agents, got, out):
+    own_row = owners_row(agents)
     rows = own_row.shape[1]
-    dest = own_row[...] * cap + slots_row(own_row[...], own_col[...])
+    dest = own_row * cap + slots_row(own_row)
     pick = (iota((sections * cap, rows), 0) == dest).astype(f32)
-    agents = [jnp.sum(got[4 * a : 4 * a + 4, :], axis=0, keepdims=True) for a in range(sections)]
-    steps = [jnp.concatenate([v[:, t * cap : (t + 1) * cap] for v in agents], axis=1) for t in range(STEPS)]
+    sums = [jnp.sum(got[4 * a : 4 * a + 4, :], axis=0, keepdims=True) for a in range(sections)]
+    steps = [jnp.concatenate([v[:, t * cap : (t + 1) * cap] for v in sums], axis=1) for t in range(STEPS)]
     steps = jnp.concatenate(steps + [jnp.zeros((8 - STEPS, sections * cap), f32)], axis=0)
     found = jnp.dot(steps, pick, precision=lax.Precision.HIGHEST, preferred_element_type=f32)
     out[...] = found[:STEPS]
-
-
-def halves_kernel(source, top, bottom, done):
-    h = top.shape[0]
-    copies = [
-        pltpu.make_async_copy(source.at[pl.ds(i * h, h)], half, done.at[i]) for i, half in enumerate((top, bottom))
-    ]
-    for copy in copies:
-        copy.start()
-    for copy in copies:
-        copy.wait()
 
 
 def call(kernel, outs, cost=None, **kw):
@@ -271,6 +297,7 @@
 
 
 SMEM_SPEC = pl.BlockSpec(memory_space=pltpu.SMEM)
+HBM_SPEC = pl.BlockSpec(memory_space=pltpu.HBM)
 VMEM_SPEC = pl.BlockSpec(memory_space=pltpu.VMEM)
 
 
@@ -298,18 +325,22 @@
             scratch_shapes=[pltpu.VMEM((size, width), bf16), pltpu.VMEM((size, 1), f32)],
         )(m, x, *near_x, *far_x, w_in)
 
-    def to_near(x, near_x):
+    def to_near(x, near_x, *wholes):
+        halves = tuple(shape(v.shape[0] // 2, v.shape[1]) for v in wholes)
+        any_spec = pl.BlockSpec(memory_space=pl.ANY)
         return call(
             functools.partial(near_kernel, size, TILE),
-            (shape(size, inner, dtype=f32), shape(size, 1, dtype=f32)),
+            (shape(size, inner, dtype=f32), shape(size, 1, dtype=f32)) + halves,
             cost=pl.CostEstimate(flops=3 * flops // 4, bytes_accessed=2 * width * inner, transcendentals=0),
-            in_specs=[SMEM_SPEC] + [VMEM_SPEC] * 3 + [pl.BlockSpec(memory_space=pl.ANY)],
+            in_specs=[SMEM_SPEC] + [VMEM_SPEC] * 3 + [any_spec] * (1 + len(wholes)),
+            out_specs=(VMEM_SPEC,) * 2 + (any_spec,) * len(halves),
             scratch_shapes=[
                 pltpu.VMEM((3, size, feat), bf16),
                 pltpu.VMEM((3, feat, inner), bf16),
                 pltpu.SemaphoreType.DMA((3, inner // TILE)),
+                pltpu.SemaphoreType.DMA((2,)),
             ],
-        )(m, x, *near_x, w_in)
+        )(m, x, *near_x, w_in, *wholes)
 
     def finish_hidden(z, square, x, near_x, far_x):
         return call(
@@ -342,16 +373,18 @@
         return call(
             functools.partial(score_kernel, sections, cap, step_idx),
             shape(4 * sections, 2 * cap, dtype=f32) if earlier else shape(sections, cap, dtype=f32),
-            in_specs=[SMEM_SPEC] + [VMEM_SPEC] * (9 + len(heads) + len(earlier)),
-        )(m, *pieces, *heads, notes, place, *earlier)
+            in_specs=[SMEM_SPEC] + [VMEM_SPEC] * (14 + len(earlier)),
+        )(m, *pieces, head_own, head_x, head_y, *head_far, notes, place, *earlier)
 
     x0, x1, notes = x0[:size], x1[:size], notes[:group]
     near0 = near(x0)
     far0 = far(*near0)
-    z0, square0 = to_near(x0, near0)
+    head_own, head_x, head_y = heads
+    z0, square0, left, right = to_near(x0, near0, head_x, head_y)
     x1, *near0 = lax.optimization_barrier((x1, *near0))
     near1 = near(x1)
-    z0, *near1 = lax.optimization_barrier((z0, *near1))
+    z0, left, right, *near1 = lax.optimization_barrier((z0, left, right, *near1))
+    head_far = over_y(left), over_x(right)
     hidden0, mine0 = finish_hidden(z0, square0, x0, near0, far0)
     far1 = far(*near1)
     send_a0, send_b0, keep_a0, keep_b0 = to_parts(hidden0)
@@ -363,6 +396,7 @@
     hidden1, fold_a0 = lax.optimization_barrier((hidden1, fold_a0))
     send_a1, send_b1, keep_a1, keep_b1 = to_parts(hidden1)
     got_a1, got_b1 = over_x(send_a1), over_y(send_b1)
+    got_a1, *head_far = lax.optimization_barrier((got_a1, *head_far))
     fold_a1, fold_b1 = fold(keep_a1, got_a1, keep_b1, got_b1)
     last_a1, last_b1 = over_y(fold_a1), over_x(fold_b1)
     first = score(0, (mine0, keep_a0, got_a0, last_a0, keep_b0, got_b0, last_b0))
@@ -380,31 +414,24 @@
     over_x = lambda v: lax.ppermute(v, "mp", [(i, i ^ 1) for i in range(4)])
     over_y = lambda v: lax.ppermute(v, "mp", [(i, i ^ 2) for i in range(4)])
 
-    own_row = matches.T.reshape(1, rows)
-    own_col = own_row.reshape(rows, 1)
+    agents = matches.T
     acts = actions.transpose(0, 2, 1)
-    mine0, other0, mine1 = acts[0].reshape(rows), acts[0, ::-1].reshape(rows), acts[1].reshape(rows)
-    notes = jnp.stack(
-        [
-            mine0 // DIGIT, mine0 % DIGIT, other0 // DIGIT, other0 % DIGIT,
-            mine1 // DIGIT, mine1 % DIGIT, jnp.zeros_like(mine0), jnp.ones_like(mine0),
-        ]
-    ).astype(bf16)
 
     head_own = head[0]
-    rows_half = head_own.shape[0] // 2
-    top, bottom = call(
-        halves_kernel,
-        (shape(rows_half, head_own.shape[1]),) * 2,
-        in_specs=[pl.BlockSpec(memory_space=pl.ANY)],
-        scratch_shapes=[pltpu.SemaphoreType.DMA((2,))],
-    )(head_own)
-    x_top, y_bottom = over_x(top), over_y(bottom)
-    others = (x_top, over_x(bottom), over_y(top), y_bottom, over_y(x_top), over_x(y_bottom))
-
-    packed = call(functools.partial(pack_kernel, sections, cap), shape(sections, cap + META, feat))(
-        own_row, own_col, notes, state
-    )
+    head_x, head_y = over_x(head_own), over_y(head_own)
+    others = (head_x, head_y)
+
+    packed = call(
+        functools.partial(pack_kernel, sections, cap),
+        shape(sections, cap + META, feat),
+        in_specs=[HBM_SPEC] * 3,
+        scratch_shapes=[
+            pltpu.VMEM(agents.shape, jnp.int32),
+            pltpu.VMEM(acts.shape, jnp.int32),
+            pltpu.VMEM(state.shape, f32),
+            pltpu.SemaphoreType.DMA((3,)),
+        ],
+    )(agents, acts, state)
     arrived = lax.all_to_all(packed, "section", split_axis=0, concat_axis=0, tiled=True)
     x0, x1, notes_c, place, count = call(
         functools.partial(unpack_kernel, sections, cap),
@@ -424,7 +451,7 @@
     ]
     sent = lax.switch(count[0], branches, m, x0, x1, notes_c, place, w_in[0, 0], w_out[0, 0], *heads)
     back = lax.all_to_all(sent, ("section", "mp"), split_axis=0, concat_axis=0, tiled=True)
-    logp = call(functools.partial(return_kernel, sections, cap), shape(STEPS, rows, dtype=f32))(own_row, own_col, back)
+    logp = call(functools.partial(return_kernel, sections, cap), shape(STEPS, rows, dtype=f32))(agents, back)
     return logp.reshape(STEPS, 2, games).transpose(0, 2, 1)
 
 

time: 132 us -> 118 us (0.89)
  waiting for transfers between devices: 51 us -> 40 us
  blocking collectives: 12.7 us -> 20.7 us
  Pallas kernels: 32 us -> 24.9 us
  starting transfers between devices: 30.4 us -> 25.4 us
    ppermute x11 -> x10, waiting for transfers between devices: 24.7 us -> 9.03 us  [plane_plan(): over_y = lambda v: lax.ppermute(v, 'mp', [(i, i ^ 2) for i in range(4)])]
    all_to_all x1, blocking collectives: 12.7 us -> 20.7 us  [plane_plan(): lax.all_to_all(sent, ('section', 'mp'), split_axis=0, concat_axis=0, tile...]
    all_to_all x1, waiting for transfers between devices: 12.7 us -> 16.8 us  [plane_plan(): lax.all_to_all(packed, 'section', split_axis=0, concat_axis=0, tiled=True)]
    ppermute x11 -> x10, starting transfers between devices: 14 us -> 10.5 us  [plane_plan(): over_y = lambda v: lax.ppermute(v, 'mp', [(i, i ^ 2) for i in range(4)])]
    pallas_call x2, Pallas kernels: 7.9 us -> 5.72 us  [to_parts(): call(functools.partial(part_kernel, size, TILE), (shape(h, width // 2),)...]
    ppermute x11 -> x10, starting transfers between devices: 11.5 us -> 10 us  [plane_plan(): over_x = lambda v: lax.ppermute(v, 'mp', [(i, i ^ 1) for i in range(4)])]
    pallas_call x1, Pallas kernels: 5.14 us -> 3.69 us  [to_hidden(): call(functools.partial(hidden_kernel, size, TILE), (shape(size, inner), s...]
    cond x8 -> x6, local copies, waits for them, and re-layouts: 0.02 us -> 1.44 us
  transfers between devices with their start and end apart: 23 -> 21, of which waited for: 15 -> 8; matrix products, arithmetic and copies ran while one was open for 1% -> 0% of each run, Pallas kernels for 18% -> 19%
where the time goes in v1:
time: 118 us; the launch traced here: 117 us
  waiting for transfers between devices  40 us (34%)
  starting transfers between devices  25.4 us (22%)
  Pallas kernels  24.9 us (21%)
  blocking collectives  20.7 us (18%)
  local copies, waits for them, and re-layouts  4.53 us (4%)
    all_to_all x1, blocking collectives, plane_plan(): lax.all_to_all(sent, ('section', 'mp'), split_axis=0, concat_axis=0, tile...  20.7 us
    all_to_all x1, waiting for transfers between devices, plane_plan(): lax.all_to_all(packed, 'section', split_axis=0, concat_axis=0, tiled=True)  16.8 us
    ppermute x10, waiting for transfers between devices, plane_plan(): over_x = lambda v: lax.ppermute(v, 'mp', [(i, i ^ 1) for i in range(4)])  14.2 us
    ppermute x10, starting transfers between devices, plane_plan(): over_y = lambda v: lax.ppermute(v, 'mp', [(i, i ^ 2) for i in range(4)])  10.5 us
    ppermute x10, starting transfers between devices, plane_plan(): over_x = lambda v: lax.ppermute(v, 'mp', [(i, i ^ 1) for i in range(4)])  10 us
    ppermute x10, waiting for transfers between devices, plane_plan(): over_y = lambda v: lax.ppermute(v, 'mp', [(i, i ^ 2) for i in range(4)])  9.03 us
    pallas_call x2, Pallas kernels, to_parts(): call(functools.partial(part_kernel, size, TILE), (shape(h, width // 2),)...  5.72 us
    pallas_call x2, Pallas kernels, score(): call(functools.partial(score_kernel, sections, cap, step_idx), shape(4 *...  5.07 us
  transfers between devices with their start and end apart: 21, of which 8 were waited for; matrix products, arithmetic and copies ran while one was open for 0% of the time, Pallas kernels for 19%

profile of v1, /device:TPU:0, one launch (start us, length us, event | category | flops | bytes accessed | tf_op | source)
XLA Modules:
  0.0 117.2 jit_solution(14887927313056149938)
XLA Ops:
  0.0 3.0 %collective-permute-start.55 = (bf16[2048,256]{1,0:T(8,128)(2,1)}, bf16[2048,256]{1,0:T(8,128)(2,1)S(1)}, u32[]{:S(2)}, u32[]{:S(2)}) collective-permute-start(bf16[2048,256]{1,0:T(8,128)(2,1)} %bitcast.17), channel_id=1, source_target_pairs={{0,2},{1,3},{2,0},{3,1},{4,6},{5,7},{6,4},{7,5},{8,10},{9,11},{10,... | collective-permute-start | bytes 3145736 | tf_op jit(solution)/shard_map/ppermute | solution.py:415
  3.0 1.5 %collective-permute-start.54 = (bf16[2048,256]{1,0:T(8,128)(2,1)}, bf16[2048,256]{1,0:T(8,128)(2,1)}, u32[]{:S(2)}, u32[]{:S(2)}) collective-permute-start(bf16[2048,256]{1,0:T(8,128)(2,1)} %bitcast.18), channel_id=1, source_target_pairs={{0,1},{1,0},{2,3},{3,2},{4,5},{5,4},{6,7},{7,6},{8,9},{9,8},{10,11... | collective-permute-start | bytes 3145736 | tf_op jit(solution)/shard_map/ppermute | solution.py:414
  4.5 1.0 copy-done.1
  5.5 0.7 copy-done.2
  6.2 0.7 copy-done.4
  6.9 2.1 %shard_map.73 = bf16[8,72,512]{2,1,0:T(8,128)(2,1)} custom-call(s32[2,128]{1,0:T(2,128)S(1)} %bitcast.11, s32[2,2,128]{2,1,0:T(2,128)S(1)} %bitcast.13, f32[128,2,512]{2,1,0:T(2,128)S(1)} %copy-done.1), custom_call_target="tpu_custom_call" | custom-call | tf_op jit(solution)/shard_map/pallas_call | solution.py:424
  9.0 4.9 %all-to-all-start = ((bf16[8,72,512]{2,1,0:T(8,128)(2,1)}), bf16[8,72,512]{2,1,0:T(8,128)(2,1)S(1)}, u32[]{:S(2)}, u32[]{:S(2)}) async-start(bf16[8,72,512]{2,1,0:T(8,128)(2,1)} %shard_map.73), calls=%async_computation | async-start | bytes 1179648 | tf_op jit(solution)/shard_map/all_to_all | solution.py:435
  13.9 16.8 %all-to-all-done.arrived = bf16[8,72,512]{2,1,0:T(8,128)(2,1)S(1)} async-done(((bf16[8,72,512]{2,1,0:T(8,128)(2,1)}), bf16[8,72,512]{2,1,0:T(8,128)(2,1)S(1)}, u32[]{:S(2)}, u32[]{:S(2)}) %all-to-all-start) | async-done | bytes 589856 | tf_op jit(solution)/shard_map/all_to_all | solution.py:435
  30.6 1.6 %shard_map.74 = (bf16[512,512]{1,0:T(8,128)(2,1)S(1)}, bf16[512,512]{1,0:T(8,128)(2,1)S(1)}, f32[128,8]{1,0:T(8,128)S(1)}, s32[1,512]{1,0:T(1,128)S(1)}, s32[1]{0:T(128)}) custom-call(s32[1]{0:T(128)} %bitcast.1.mp_ref, bf16[8,72,512]{2,1,0:T(8,128)(2,1)S(1)} %all-to-all-done.arrived, bf16[1024,512]{1,0:T(8,128)(2,1)S(1)} %copy-done), custom_call_target="tpu_custom_call" | custom-call | tf_op jit(solution)/shard_map/pallas_call | solution.py:436
  32.9 0.0 collective-permute-done.55
  32.9 0.0 collective-permute-done.54
  32.9 0.0 copy-start.3
  32.9 62.5 %conditional.1 = (f32[32,128]{1,0:T(8,128)S(1)}) conditional(s32[]{:T(128)} %bitcast.3, (bf16[512,512]{1,0:T(8,128)(2,1)S(1)}, bf16[512,512]{1,0:T(8,128)(2,1)S(1)}, s32[1]{0:T(128)}, bf16[2048,2048]{1,0:T(8,128)(2,1)}, bf16[2048,256]{1,0:T(8,128)(2,1)}, /*index=5*/bf16[2048,256]{1,0:T(8,128)(2,1)S(1)}, ...), branch_computations={%region_0.0_spmd, %region_1.0_spmd, %region_2.0_spmd} | conditional | flops 17179869184 | bytes 130024256 | solution.py:452
  33.6 0.6 collective-permute-start.37
  34.2 0.5 collective-permute-start.36
  34.7 8.2 %collective-permute-done.37.py = bf16[256,512]{1,0:T(8,128)(2,1)S(1)} collective-permute-done((bf16[256,512]{1,0:T(8,128)(2,1)S(1)}, bf16[256,512]{1,0:T(8,128)(2,1)S(1)}, u32[]{:S(2)}, u32[]{:S(2)}) %collective-permute-start.37) | collective-permute-done | bytes 262176 | tf_op jit(solution)/shard_map/cond/branch_2_fun/ppermute | solution.py:415
  42.9 0.5 collective-permute-done.36.px
  43.4 1.5 %collective-permute-start.39 = (bf16[256,512]{1,0:T(8,128)(2,1)S(1)}, bf16[256,512]{1,0:T(8,128)(2,1)S(1)}, u32[]{:S(2)}, u32[]{:S(2)}) collective-permute-start(bf16[256,512]{1,0:T(8,128)(2,1)S(1)} %slice.47.own), channel_id=1, source_target_pairs={{0,2},{1,3},{2,0},{3,1},{4,6},{5,7},{6,4},{7,5},{8,10},{9,11},{10,... | collective-permute-start | bytes 786440 | tf_op jit(solution)/shard_map/cond/branch_2_fun/ppermute | solution.py:415
  44.9 0.5 collective-permute-start.38
  45.5 1.5 %collective-permute-start.43 = (bf16[128,512]{1,0:T(8,128)(2,1)S(1)}, bf16[128,512]{1,0:T(8,128)(2,1)S(1)}, u32[]{:S(2)}, u32[]{:S(2)}) collective-permute-start(bf16[128,512]{1,0:T(8,128)(2,1)S(1)} %slice.59), channel_id=1, source_target_pairs={{0,1},{1,0},{2,3},{3,2},{4,5},{5,4},{6,7},{7,6},{8,9},{9,8},{10,11... | collective-permute-start | bytes 393224 | tf_op jit(solution)/shard_map/cond/branch_2_fun/ppermute | solution.py:414
  47.1 0.6 collective-permute-start.42
  47.6 4.0 %branch_2_fun.9 = (f32[256,2048]{1,0:T(8,128)S(1)}, f32[256,1]{1,0:T(8,128)S(1)}, bf16[1024,256]{1,0:T(8,128)(2,1)S(1)}, bf16[1024,256]{1,0:T(8,128)(2,1)S(1)}) custom-call(s32[1]{0:T(128)} %get-tuple-element.159.mp_ref, bf16[256,512]{1,0:T(8,128)(2,1)S(1)} %slice.48.own, bf16[256,512]{1,0:T(8,128)(2,1)S(1)} %collective-permute-done.36.px, ...), custom_call_target="tpu_custom_call" | custom-call | flops 1610612736 | bytes 8388608 | tf_op jit(solution)/shard_map/cond/branch_2_fun/pallas_call | solution.py:331
  51.7 0.8 collective-permute-done.39.py
  52.5 1.6 %collective-permute-done.38.px = bf16[256,512]{1,0:T(8,128)(2,1)S(1)} collective-permute-done((bf16[256,512]{1,0:T(8,128)(2,1)S(1)}, bf16[256,512]{1,0:T(8,128)(2,1)S(1)}, u32[]{:S(2)}, u32[]{:S(2)}) %collective-permute-start.38) | collective-permute-done | bytes 262176 | tf_op jit(solution)/shard_map/cond/branch_2_fun/ppermute | solution.py:414
  54.1 0.6 collective-permute-start.41
  54.7 0.5 collective-permute-start.40
  55.2 1.7 %collective-permute-done.43.db = bf16[128,512]{1,0:T(8,128)(2,1)S(1)} collective-permute-done((bf16[128,512]{1,0:T(8,128)(2,1)S(1)}, bf16[128,512]{1,0:T(8,128)(2,1)S(1)}, u32[]{:S(2)}, u32[]{:S(2)}) %collective-permute-start.43) | collective-permute-done | bytes 131104 | tf_op jit(solution)/shard_map/cond/branch_2_fun/ppermute | solution.py:414
  56.9 0.0 collective-permute-done.42.da
  56.9 1.9 %branch_2_fun.11 = (bf16[256,2048]{1,0:T(8,128)(2,1)S(1)}, bf16[64,2048]{1,0:T(8,128)(2,1)S(1)}) custom-call(s32[1]{0:T(128)} %get-tuple-element.159.mp_ref, f32[256,2048]{1,0:T(8,128)S(1)} %get-tuple-element.173.z, f32[256,1]{1,0:T(8,128)S(1)} %get-tuple-element.174.square, bf16[256,512]{1,0:T(8,128)(2,1)S(1)} %slice.48.own, ...), custom_call_target="tpu_custom_call" | custom-call | flops 536870912 | bytes 2097152 | tf_op jit(solution)/shard_map/cond/branch_2_fun/pallas_call | solution.py:346
  58.9 1.4 %copy-done.11 = bf16[2048,2048]{1,0:T(8,128)(2,1)S(1)} copy-done((bf16[2048,2048]{1,0:T(8,128)(2,1)S(1)}, bf16[2048,2048]{1,0:T(8,128)(2,1)}, u32[]{:S(2)}) %copy-start.11) | copy-done | bytes 8388632 | tf_op jit(solution)/shard_map/cond
  60.3 2.9 %branch_2_fun.12 = (bf16[128,1024]{1,0:T(8,128)(2,1)S(1)}, bf16[128,1024]{1,0:T(8,128)(2,1)S(1)}, bf16[128,1024]{1,0:T(8,128)(2,1)S(1)}, bf16[128,1024]{1,0:T(8,128)(2,1)S(1)}) custom-call(bf16[256,2048]{1,0:T(8,128)(2,1)S(1)} %get-tuple-element.177.hidden, bf16[2048,2048]{1,0:T(8,128)(2,1)S(1)} %copy-done.11), custom_call_target="tpu_custom_call" | custom-call | flops 2147483648 | bytes 8388608 | tf_op jit(solution)/shard_map/cond/branch_2_fun/pallas_call | solution.py:355
  63.2 0.6 collective-permute-start.44
  63.8 0.8 collective-permute-start.45
  64.6 1.2 %collective-permute-start.47 = (bf16[1024,256]{1,0:T(8,128)(2,1)S(1)}, bf16[1024,256]{1,0:T(8,128)(2,1)S(1)}, u32[]{:S(2)}, u32[]{:S(2)}) collective-permute-start(bf16[1024,256]{1,0:T(8,128)(2,1)S(1)} %get-tuple-element.190), channel_id=1, source_target_pairs={{0,2},{1,3},{2,0},{3,1},{4,6},{5,7},{6,4},{7,5},{8,10},{9,11},{10,... | collective-permute-start | bytes 1572872 | tf_op jit(solution)/shard_map/cond/branch_2_fun/ppermute | solution.py:415
  65.8 0.0 collective-permute-done.41.db
  65.8 1.5 %collective-permute-start.48 = (bf16[1024,256]{1,0:T(8,128)(2,1)S(1)}, bf16[1024,256]{1,0:T(8,128)(2,1)S(1)}, u32[]{:S(2)}, u32[]{:S(2)}) collective-permute-start(bf16[1024,256]{1,0:T(8,128)(2,1)S(1)} %get-tuple-element.191), channel_id=1, source_target_pairs={{0,1},{1,0},{2,3},{3,2},{4,5},{5,4},{6,7},{7,6},{8,9},{9,8},{10,11... | collective-permute-start | bytes 1572872 | tf_op jit(solution)/shard_map/cond/branch_2_fun/ppermute | solution.py:414
  67.3 0.0 collective-permute-done.40.da
  67.3 3.7 %branch_2_fun.10 = (bf16[256,2048]{1,0:T(8,128)(2,1)S(1)}, bf16[64,2048]{1,0:T(8,128)(2,1)S(1)}) custom-call(s32[1]{0:T(128)} %get-tuple-element.159.mp_ref, bf16[256,512]{1,0:T(8,128)(2,1)S(1)} %slice.47.own, bf16[256,512]{1,0:T(8,128)(2,1)S(1)} %collective-permute-done.38.px, bf16[256,512]{1,0:T(8,128)(2,1)S(1)} %collective-permute-done.39.py, ...), custom_call_target="tpu_custom_call" | custom-call | flops 2147483648 | bytes 8388608 | tf_op jit(solution)/shard_map/cond/branch_2_fun/pallas_call | solution.py:320
  71.0 0.0 collective-permute-done.44.got_a
  71.0 0.0 collective-permute-done.45.got_b
  71.0 0.1 branch_2_fun.13
  71.1 0.0 copy-start.10
  71.1 2.9 %branch_2_fun.14 = (bf16[128,1024]{1,0:T(8,128)(2,1)S(1)}, bf16[128,1024]{1,0:T(8,128)(2,1)S(1)}, bf16[128,1024]{1,0:T(8,128)(2,1)S(1)}, bf16[128,1024]{1,0:T(8,128)(2,1)S(1)}) custom-call(bf16[256,2048]{1,0:T(8,128)(2,1)S(1)} %get-tuple-element.187.hidden, bf16[2048,2048]{1,0:T(8,128)(2,1)S(1)} %copy-done.11), custom_call_target="tpu_custom_call" | custom-call | flops 2147483648 | bytes 8388608 | tf_op jit(solution)/shard_map/cond/branch_2_fun/pallas_call | solution.py:355
  73.9 0.7 collective-permute-start.46
  74.6 0.7 collective-permute-start.49
  75.4 1.3 %collective-permute-start.52 = (bf16[64,1024]{1,0:T(8,128)(2,1)S(1)}, bf16[64,1024]{1,0:T(8,128)(2,1)S(1)}, u32[]{:S(2)}, u32[]{:S(2)}) collective-permute-start(bf16[64,1024]{1,0:T(8,128)(2,1)S(1)} %get-tuple-element.186), channel_id=1, source_target_pairs={{0,2},{1,3},{2,0},{3,1},{4,6},{5,7},{6,4},{7,5},{8,10},{9,11},{10,... | collective-permute-start | bytes 393224 | tf_op jit(solution)/shard_map/cond/branch_2_fun/ppermute | solution.py:415
  76.7 6.9 %collective-permute-done.46.got_a = bf16[128,1024]{1,0:T(8,128)(2,1)S(1)} collective-permute-done((bf16[128,1024]{1,0:T(8,128)(2,1)S(1)}, bf16[128,1024]{1,0:T(8,128)(2,1)S(1)}, u32[]{:S(2)}, u32[]{:S(2)}) %collective-permute-start.46) | collective-permute-done | bytes 262176 | tf_op jit(solution)/shard_map/cond/branch_2_fun/ppermute | solution.py:414
  83.6 2.0 %collective-permute-start.53 = (bf16[64,1024]{1,0:T(8,128)(2,1)S(1)}, bf16[64,1024]{1,0:T(8,128)(2,1)S(1)}, u32[]{:S(2)}, u32[]{:S(2)}) collective-permute-start(bf16[64,1024]{1,0:T(8,128)(2,1)S(1)} %get-tuple-element.203), channel_id=1, source_target_pairs={{0,1},{1,0},{2,3},{3,2},{4,5},{5,4},{6,7},{7,6},{8,9},{9,8},{10,11... | collective-permute-start | bytes 393224 | tf_op jit(solution)/shard_map/cond/branch_2_fun/ppermute | solution.py:414
  85.5 0.0 collective-permute-done.47.h3_top
  85.5 0.0 collective-permute-done.48.h3_bottom
  85.6 0.0 collective-permute-done.49.got_b
  85.6 0.1 branch_2_fun.15
  85.6 0.3 collective-permute-start.50
  86.0 0.6 collective-permute-start.51
  86.5 3.5 %collective-permute-done.53.last_b = bf16[64,1024]{1,0:T(8,128)(2,1)S(1)} collective-permute-done((bf16[64,1024]{1,0:T(8,128)(2,1)S(1)}, bf16[64,1024]{1,0:T(8,128)(2,1)S(1)}, u32[]{:S(2)}, u32[]{:S(2)}) %collective-permute-start.53) | collective-permute-done | bytes 131104 | tf_op jit(solution)/shard_map/cond/branch_2_fun/ppermute | solution.py:414
  90.0 0.0 collective-permute-done.52.last_a
  90.0 0.0 copy-done.10
  90.0 2.5 %branch_2_fun.16.rest_0_ = f32[8,64]{1,0:T(8,128)S(1)} custom-call(s32[1]{0:T(128)} %get-tuple-element.159.mp_ref, bf16[64,2048]{1,0:T(8,128)(2,1)S(1)} %get-tuple-element.202.mine, bf16[128,1024]{1,0:T(8,128)(2,1)S(1)} %get-tuple-element.182.keep_a, bf16[128,1024]{1,0:T(8,128)(2,1)S(1)} %collective-permute-done.44.got_a, ...), custom_call_target="tpu_custom_call" | custom-call | tf_op jit(solution)/shard_map/cond/branch_2_fun/pallas_call | solution.py:373
  92.6 0.0 collective-permute-done.50.last_a
  92.6 0.0 collective-permute-done.51.last_b
  92.6 2.5 %branch_2_fun.17 = f32[32,128]{1,0:T(8,128)S(1)} custom-call(s32[1]{0:T(128)} %get-tuple-element.159.mp_ref, bf16[64,2048]{1,0:T(8,128)(2,1)S(1)} %get-tuple-element.171.mine, bf16[128,1024]{1,0:T(8,128)(2,1)S(1)} %get-tuple-element.188.keep_a, bf16[128,1024]{1,0:T(8,128)(2,1)S(1)} %collective-permute-done.46.got_a, ...), custom_call_target="tpu_custom_call" | custom-call | tf_op jit(solution)/shard_map/cond/branch_2_fun/pallas_call | solution.py:373
  95.3 20.7 %all_to_all.16 = f32[32,1,128]{2,1,0:T(1,128)S(1)} all-to-all(f32[32,1,128]{2,1,0:T(1,128)S(1)} %bitcast.29), channel_id=1, replica_groups=mesh['section'=8,'mp'=4] {'section','mp'}, dimensions={0} | all-to-all | bytes 32768 | tf_op jit(solution)/shard_map/all_to_all | solution.py:453
  116.1 0.6 shard_map.75
  116.6 0.6 reshape.12
  (16 shorter events, 0.1 us)
Async XLA Ops:
  0.0 30.6 %copy-start = (bf16[1024,512]{1,0:T(8,128)(2,1)S(1)}, bf16[1024,512]{1,0:T(8,128)(2,1)}, u32[]{:S(2)}) copy-start(bf16[1024,512]{1,0:T(8,128)(2,1)} %embed.1) | copy-start | bytes 3145732
  0.0 32.9 %collective-permute-start.55 = (bf16[2048,256]{1,0:T(8,128)(2,1)}, bf16[2048,256]{1,0:T(8,128)(2,1)S(1)}, u32[]{:S(2)}, u32[]{:S(2)}) collective-permute-start(bf16[2048,256]{1,0:T(8,128)(2,1)} %bitcast.17), channel_id=1, source_target_pairs={{0,2},{1,3},{2,0},{3,1},{4,6},{5,7},{6,4},{7,5},{8,10},{9,11},{10,... | collective-permute-start | bytes 3145736 | tf_op jit(solution)/shard_map/ppermute | solution.py:415
  3.0 29.9 %collective-permute-start.54 = (bf16[2048,256]{1,0:T(8,128)(2,1)}, bf16[2048,256]{1,0:T(8,128)(2,1)}, u32[]{:S(2)}, u32[]{:S(2)}) collective-permute-start(bf16[2048,256]{1,0:T(8,128)(2,1)} %bitcast.18), channel_id=1, source_target_pairs={{0,1},{1,0},{2,3},{3,2},{4,5},{5,4},{6,7},{7,6},{8,9},{9,8},{10,11... | collective-permute-start | bytes 3145736 | tf_op jit(solution)/shard_map/ppermute | solution.py:414
  4.5 1.0 copy-start.1
  5.5 0.7 copy-start.2
  6.2 0.7 copy-start.4
  9.0 21.6 %all-to-all-start = ((bf16[8,72,512]{2,1,0:T(8,128)(2,1)}), bf16[8,72,512]{2,1,0:T(8,128)(2,1)S(1)}, u32[]{:S(2)}, u32[]{:S(2)}) async-start(bf16[8,72,512]{2,1,0:T(8,128)(2,1)} %shard_map.73), calls=%async_computation | async-start | bytes 1179648 | tf_op jit(solution)/shard_map/all_to_all | solution.py:435
  32.9 83.2 %copy-start.3 = (s32[128,2]{0,1:T(2,128)S(1)}, s32[128,2]{0,1:T(2,128)}, u32[]{:S(2)}) copy-start(s32[128,2]{0,1:T(2,128)} %param.10) | copy-start | bytes 3076
  33.6 9.3 %collective-permute-start.37 = (bf16[256,512]{1,0:T(8,128)(2,1)S(1)}, bf16[256,512]{1,0:T(8,128)(2,1)S(1)}, u32[]{:S(2)}, u32[]{:S(2)}) collective-permute-start(bf16[256,512]{1,0:T(8,128)(2,1)S(1)} %slice.48.own), channel_id=1, source_target_pairs={{0,2},{1,3},{2,0},{3,1},{4,6},{5,7},{6,4},{7,5},{8,10},{9,11},{10,... | collective-permute-start | bytes 786440 | tf_op jit(solution)/shard_map/cond/branch_2_fun/ppermute | solution.py:415
  34.2 9.2 %collective-permute-start.36 = (bf16[256,512]{1,0:T(8,128)(2,1)S(1)}, bf16[256,512]{1,0:T(8,128)(2,1)S(1)}, u32[]{:S(2)}, u32[]{:S(2)}) collective-permute-start(bf16[256,512]{1,0:T(8,128)(2,1)S(1)} %slice.48.own), channel_id=1, source_target_pairs={{0,1},{1,0},{2,3},{3,2},{4,5},{5,4},{6,7},{7,6},{8,9},{9,8},{10,11... | collective-permute-start | bytes 786440 | tf_op jit(solution)/shard_map/cond/branch_2_fun/ppermute | solution.py:414
  43.4 9.1 %collective-permute-start.39 = (bf16[256,512]{1,0:T(8,128)(2,1)S(1)}, bf16[256,512]{1,0:T(8,128)(2,1)S(1)}, u32[]{:S(2)}, u32[]{:S(2)}) collective-permute-start(bf16[256,512]{1,0:T(8,128)(2,1)S(1)} %slice.47.own), channel_id=1, source_target_pairs={{0,2},{1,3},{2,0},{3,1},{4,6},{5,7},{6,4},{7,5},{8,10},{9,11},{10,... | collective-permute-start | bytes 786440 | tf_op jit(solution)/shard_map/cond/branch_2_fun/ppermute | solution.py:415
  44.9 9.1 %collective-permute-start.38 = (bf16[256,512]{1,0:T(8,128)(2,1)S(1)}, bf16[256,512]{1,0:T(8,128)(2,1)S(1)}, u32[]{:S(2)}, u32[]{:S(2)}) collective-permute-start(bf16[256,512]{1,0:T(8,128)(2,1)S(1)} %slice.47.own), channel_id=1, source_target_pairs={{0,1},{1,0},{2,3},{3,2},{4,5},{5,4},{6,7},{7,6},{8,9},{9,8},{10,11... | collective-permute-start | bytes 786440 | tf_op jit(solution)/shard_map/cond/branch_2_fun/ppermute | solution.py:414
  45.5 11.4 %collective-permute-start.43 = (bf16[128,512]{1,0:T(8,128)(2,1)S(1)}, bf16[128,512]{1,0:T(8,128)(2,1)S(1)}, u32[]{:S(2)}, u32[]{:S(2)}) collective-permute-start(bf16[128,512]{1,0:T(8,128)(2,1)S(1)} %slice.59), channel_id=1, source_target_pairs={{0,1},{1,0},{2,3},{3,2},{4,5},{5,4},{6,7},{7,6},{8,9},{9,8},{10,11... | collective-permute-start | bytes 393224 | tf_op jit(solution)/shard_map/cond/branch_2_fun/ppermute | solution.py:414
  47.1 9.8 %collective-permute-start.42 = (bf16[128,512]{1,0:T(8,128)(2,1)S(1)}, bf16[128,512]{1,0:T(8,128)(2,1)S(1)}, u32[]{:S(2)}, u32[]{:S(2)}) collective-permute-start(bf16[128,512]{1,0:T(8,128)(2,1)S(1)} %slice.58), channel_id=1, source_target_pairs={{0,2},{1,3},{2,0},{3,1},{4,6},{5,7},{6,4},{7,5},{8,10},{9,11},{10,... | collective-permute-start | bytes 393224 | tf_op jit(solution)/shard_map/cond/branch_2_fun/ppermute | solution.py:415
  47.6 9.3 %copy-start.7 = (bf16[2048,2048]{1,0:T(8,128)(2,1)S(1)}, bf16[2048,2048]{1,0:T(8,128)(2,1)}, u32[]{:S(2)}) copy-start(bf16[2048,2048]{1,0:T(8,128)(2,1)} %get-tuple-element.163.w_in) | copy-start | bytes 25165828 | tf_op jit(solution)/shard_map/cond
  54.1 11.7 %collective-permute-start.41 = (bf16[128,512]{1,0:T(8,128)(2,1)S(1)}, bf16[128,512]{1,0:T(8,128)(2,1)S(1)}, u32[]{:S(2)}, u32[]{:S(2)}) collective-permute-start(bf16[128,512]{1,0:T(8,128)(2,1)S(1)} %slice.50), channel_id=1, source_target_pairs={{0,1},{1,0},{2,3},{3,2},{4,5},{5,4},{6,7},{7,6},{8,9},{9,8},{10,11... | collective-permute-start | bytes 393224 | tf_op jit(solution)/shard_map/cond/branch_2_fun/ppermute | solution.py:414
  54.7 12.5 %collective-permute-start.40 = (bf16[128,512]{1,0:T(8,128)(2,1)S(1)}, bf16[128,512]{1,0:T(8,128)(2,1)S(1)}, u32[]{:S(2)}, u32[]{:S(2)}) collective-permute-start(bf16[128,512]{1,0:T(8,128)(2,1)S(1)} %slice.49), channel_id=1, source_target_pairs={{0,2},{1,3},{2,0},{3,1},{4,6},{5,7},{6,4},{7,5},{8,10},{9,11},{10,... | collective-permute-start | bytes 393224 | tf_op jit(solution)/shard_map/cond/branch_2_fun/ppermute | solution.py:415
  56.9 3.4 %copy-start.11 = (bf16[2048,2048]{1,0:T(8,128)(2,1)S(1)}, bf16[2048,2048]{1,0:T(8,128)(2,1)}, u32[]{:S(2)}) copy-start(bf16[2048,2048]{1,0:T(8,128)(2,1)} %get-tuple-element.178.w_out) | copy-start | bytes 25165828 | tf_op jit(solution)/shard_map/cond
  63.2 7.8 %collective-permute-start.44 = (bf16[128,1024]{1,0:T(8,128)(2,1)S(1)}, bf16[128,1024]{1,0:T(8,128)(2,1)S(1)}, u32[]{:S(2)}, u32[]{:S(2)}) collective-permute-start(bf16[128,1024]{1,0:T(8,128)(2,1)S(1)} %get-tuple-element.179), channel_id=1, source_target_pairs={{0,1},{1,0},{2,3},{3,2},{4,5},{5,4},{6,7},{7,6},{8,9},{9,8},{10,11... | collective-permute-start | bytes 786440 | tf_op jit(solution)/shard_map/cond/branch_2_fun/ppermute | solution.py:414
  63.8 7.2 %collective-permute-start.45 = (bf16[128,1024]{1,0:T(8,128)(2,1)S(1)}, bf16[128,1024]{1,0:T(8,128)(2,1)S(1)}, u32[]{:S(2)}, u32[]{:S(2)}) collective-permute-start(bf16[128,1024]{1,0:T(8,128)(2,1)S(1)} %get-tuple-element.180), channel_id=1, source_target_pairs={{0,2},{1,3},{2,0},{3,1},{4,6},{5,7},{6,4},{7,5},{8,10},{9,11},{10,... | collective-permute-start | bytes 786440 | tf_op jit(solution)/shard_map/cond/branch_2_fun/ppermute | solution.py:415
  64.6 21.0 %collective-permute-start.47 = (bf16[1024,256]{1,0:T(8,128)(2,1)S(1)}, bf16[1024,256]{1,0:T(8,128)(2,1)S(1)}, u32[]{:S(2)}, u32[]{:S(2)}) collective-permute-start(bf16[1024,256]{1,0:T(8,128)(2,1)S(1)} %get-tuple-element.190), channel_id=1, source_target_pairs={{0,2},{1,3},{2,0},{3,1},{4,6},{5,7},{6,4},{7,5},{8,10},{9,11},{10,... | collective-permute-start | bytes 1572872 | tf_op jit(solution)/shard_map/cond/branch_2_fun/ppermute | solution.py:415
  65.8 19.8 %collective-permute-start.48 = (bf16[1024,256]{1,0:T(8,128)(2,1)S(1)}, bf16[1024,256]{1,0:T(8,128)(2,1)S(1)}, u32[]{:S(2)}, u32[]{:S(2)}) collective-permute-start(bf16[1024,256]{1,0:T(8,128)(2,1)S(1)} %get-tuple-element.191), channel_id=1, source_target_pairs={{0,1},{1,0},{2,3},{3,2},{4,5},{5,4},{6,7},{7,6},{8,9},{9,8},{10,11... | collective-permute-start | bytes 1572872 | tf_op jit(solution)/shard_map/cond/branch_2_fun/ppermute | solution.py:414
  71.1 19.0 %copy-start.10 = (bf16[2048,256]{1,0:T(8,128)(2,1)S(1)}, bf16[2048,256]{1,0:T(8,128)(2,1)}, u32[]{:S(2)}) copy-start(bf16[2048,256]{1,0:T(8,128)(2,1)} %get-tuple-element.197.h0) | copy-start | bytes 3145732 | tf_op jit(solution)/shard_map/cond
  73.9 9.6 %collective-permute-start.46 = (bf16[128,1024]{1,0:T(8,128)(2,1)S(1)}, bf16[128,1024]{1,0:T(8,128)(2,1)S(1)}, u32[]{:S(2)}, u32[]{:S(2)}) collective-permute-start(bf16[128,1024]{1,0:T(8,128)(2,1)S(1)} %get-tuple-element.189), channel_id=1, source_target_pairs={{0,1},{1,0},{2,3},{3,2},{4,5},{5,4},{6,7},{7,6},{8,9},{9,8},{10,11... | collective-permute-start | bytes 786440 | tf_op jit(solution)/shard_map/cond/branch_2_fun/ppermute | solution.py:414
  74.6 10.9 %collective-permute-start.49 = (bf16[128,1024]{1,0:T(8,128)(2,1)S(1)}, bf16[128,1024]{1,0:T(8,128)(2,1)S(1)}, u32[]{:S(2)}, u32[]{:S(2)}) collective-permute-start(bf16[128,1024]{1,0:T(8,128)(2,1)S(1)} %get-tuple-element.194), channel_id=1, source_target_pairs={{0,2},{1,3},{2,0},{3,1},{4,6},{5,7},{6,4},{7,5},{8,10},{9,11},{10,... | collective-permute-start | bytes 786440 | tf_op jit(solution)/shard_map/cond/branch_2_fun/ppermute | solution.py:415
  75.4 14.6 %collective-permute-start.52 = (bf16[64,1024]{1,0:T(8,128)(2,1)S(1)}, bf16[64,1024]{1,0:T(8,128)(2,1)S(1)}, u32[]{:S(2)}, u32[]{:S(2)}) collective-permute-start(bf16[64,1024]{1,0:T(8,128)(2,1)S(1)} %get-tuple-element.186), channel_id=1, source_target_pairs={{0,2},{1,3},{2,0},{3,1},{4,6},{5,7},{6,4},{7,5},{8,10},{9,11},{10,... | collective-permute-start | bytes 393224 | tf_op jit(solution)/shard_map/cond/branch_2_fun/ppermute | solution.py:415
  83.6 6.4 %collective-permute-start.53 = (bf16[64,1024]{1,0:T(8,128)(2,1)S(1)}, bf16[64,1024]{1,0:T(8,128)(2,1)S(1)}, u32[]{:S(2)}, u32[]{:S(2)}) collective-permute-start(bf16[64,1024]{1,0:T(8,128)(2,1)S(1)} %get-tuple-element.203), channel_id=1, source_target_pairs={{0,1},{1,0},{2,3},{3,2},{4,5},{5,4},{6,7},{7,6},{8,9},{9,8},{10,11... | collective-permute-start | bytes 393224 | tf_op jit(solution)/shard_map/cond/branch_2_fun/ppermute | solution.py:414
  85.6 6.9 %collective-permute-start.50 = (bf16[64,1024]{1,0:T(8,128)(2,1)S(1)}, bf16[64,1024]{1,0:T(8,128)(2,1)S(1)}, u32[]{:S(2)}, u32[]{:S(2)}) collective-permute-start(bf16[64,1024]{1,0:T(8,128)(2,1)S(1)} %get-tuple-element.195), channel_id=1, source_target_pairs={{0,2},{1,3},{2,0},{3,1},{4,6},{5,7},{6,4},{7,5},{8,10},{9,11},{10,... | collective-permute-start | bytes 393224 | tf_op jit(solution)/shard_map/cond/branch_2_fun/ppermute | solution.py:415
  86.0 6.6 %collective-permute-start.51 = (bf16[64,1024]{1,0:T(8,128)(2,1)S(1)}, bf16[64,1024]{1,0:T(8,128)(2,1)S(1)}, u32[]{:S(2)}, u32[]{:S(2)}) collective-permute-start(bf16[64,1024]{1,0:T(8,128)(2,1)S(1)} %get-tuple-element.196), channel_id=1, source_target_pairs={{0,1},{1,0},{2,3},{3,2},{4,5},{5,4},{6,7},{7,6},{8,9},{9,8},{10,11... | collective-permute-start | bytes 393224 | tf_op jit(solution)/shard_map/cond/branch_2_fun/ppermute | solution.py:414

commit v2 on v1

--- a/solution.py
+++ b/solution.py
@@ -10,7 +10,7 @@
 STEPS = 2
 META = 8
 DIGIT = 32
-SHARES = ((1, 1), (3, 4), (1, 2))
+SHARES = ((1, 1), (5, 8), (3, 8))
 TILE = 512
 VMEM = 20 * 1024 * 1024
 
@@ -279,14 +279,16 @@
     steps = [jnp.concatenate([v[:, t * cap : (t + 1) * cap] for v in sums], axis=1) for t in range(STEPS)]
     steps = jnp.concatenate(steps + [jnp.zeros((8 - STEPS, sections * cap), f32)], axis=0)
     found = jnp.dot(steps, pick, precision=lax.Precision.HIGHEST, preferred_element_type=f32)
-    out[...] = found[:STEPS]
-
-
-def call(kernel, outs, cost=None, **kw):
+    for t in range(STEPS):
+        for p in range(2):
+            out[t, p : p + 1, :] = found[t : t + 1, p * rows // 2 : (p + 1) * rows // 2]
+
+
+def call(kernel, outs, cost=None, grant=VMEM, **kw):
     return pl.pallas_call(
         kernel,
         out_shape=outs,
-        compiler_params=pltpu.CompilerParams(vmem_limit_bytes=VMEM),
+        compiler_params=pltpu.CompilerParams(vmem_limit_bytes=grant),
         cost_estimate=cost,
         **kw,
     )
@@ -390,10 +392,8 @@
     send_a0, send_b0, keep_a0, keep_b0 = to_parts(hidden0)
     got_a0, got_b0 = over_x(send_a0), over_y(send_b0)
     hidden1, mine1 = to_hidden(x1, near1, far1)
-    hidden1, got_a0, got_b0 = lax.optimization_barrier((hidden1, got_a0, got_b0))
     fold_a0, fold_b0 = fold(keep_a0, got_a0, keep_b0, got_b0)
     last_a0, last_b0 = over_y(fold_a0), over_x(fold_b0)
-    hidden1, fold_a0 = lax.optimization_barrier((hidden1, fold_a0))
     send_a1, send_b1, keep_a1, keep_b1 = to_parts(hidden1)
     got_a1, got_b1 = over_x(send_a1), over_y(send_b1)
     got_a1, *head_far = lax.optimization_barrier((got_a1, *head_far))
@@ -424,6 +424,7 @@
     packed = call(
         functools.partial(pack_kernel, sections, cap),
         shape(sections, cap + META, feat),
+        grant=60 * 1024 * 1024,
         in_specs=[HBM_SPEC] * 3,
         scratch_shapes=[
             pltpu.VMEM(agents.shape, jnp.int32),
@@ -451,8 +452,8 @@
     ]
     sent = lax.switch(count[0], branches, m, x0, x1, notes_c, place, w_in[0, 0], w_out[0, 0], *heads)
     back = lax.all_to_all(sent, ("section", "mp"), split_axis=0, concat_axis=0, tiled=True)
-    logp = call(functools.partial(return_kernel, sections, cap), shape(STEPS, rows, dtype=f32))(agents, back)
-    return logp.reshape(STEPS, 2, games).transpose(0, 2, 1)
+    logp = call(functools.partial(return_kernel, sections, cap), shape(STEPS, 2, games, dtype=f32))(agents, back)
+    return logp.transpose(0, 2, 1)
 
 
 def general_plan(matches, actions, state, embed, w_in, w_out, head):

time: 118 us -> 120 us (1.017)
  blocking collectives: 20.7 us -> 27.6 us
  local copies, waits for them, and re-layouts: 4.53 us -> 0.12 us
  Pallas kernels: 24.9 us -> 28.7 us
  waiting for transfers between devices: 40 us -> 36.8 us
    all_to_all x1, blocking collectives: 20.7 us -> 27.6 us  [plane_plan(): lax.all_to_all(sent, ('section', 'mp'), split_axis=0, concat_axis=0, tile...]
    ppermute x10, waiting for transfers between devices: 9.03 us -> 4.56 us  [plane_plan(): over_y = lambda v: lax.ppermute(v, 'mp', [(i, i ^ 2) for i in range(4)])]
    unnamed x10 -> x4, local copies, waits for them, and re-layouts: 2.41 us -> 0.01 us
    cond x6 -> x8, local copies, waits for them, and re-layouts: 1.44 us -> 0.02 us
    ppermute x10, waiting for transfers between devices: 14.2 us -> 15.5 us  [plane_plan(): over_x = lambda v: lax.ppermute(v, 'mp', [(i, i ^ 1) for i in range(4)])]
    ppermute x10, starting transfers between devices: 10.5 us -> 9.28 us  [plane_plan(): over_y = lambda v: lax.ppermute(v, 'mp', [(i, i ^ 2) for i in range(4)])]
  transfers between devices with their start and end apart: 21 -> 21, of which waited for: 8 -> 7; matrix products, arithmetic and copies ran while one was open for 0% -> 0% of each run, Pallas kernels for 19% -> 21%
where the time goes in v2:
time: 120 us; the launch traced here: 119 us
  waiting for transfers between devices  36.8 us (31%)
  Pallas kernels  28.7 us (24%)
  blocking collectives  27.6 us (23%)
  starting transfers between devices  24.3 us (20%)
    all_to_all x1, blocking collectives, plane_plan(): lax.all_to_all(sent, ('section', 'mp'), split_axis=0, concat_axis=0, tile...  27.6 us
    all_to_all x1, waiting for transfers between devices, plane_plan(): lax.all_to_all(packed, 'section', split_axis=0, concat_axis=0, tiled=True)  16.8 us
    ppermute x10, waiting for transfers between devices, plane_plan(): over_x = lambda v: lax.ppermute(v, 'mp', [(i, i ^ 1) for i in range(4)])  15.5 us
    ppermute x10, starting transfers between devices, plane_plan(): over_x = lambda v: lax.ppermute(v, 'mp', [(i, i ^ 1) for i in range(4)])  10.1 us
    ppermute x10, starting transfers between devices, plane_plan(): over_y = lambda v: lax.ppermute(v, 'mp', [(i, i ^ 2) for i in range(4)])  9.28 us
    pallas_call x2, Pallas kernels, to_parts(): call(functools.partial(part_kernel, size, TILE), (shape(h, width // 2),)...  6.81 us
    pallas_call x2, Pallas kernels, score(): call(functools.partial(score_kernel, sections, cap, step_idx), shape(4 *...  5.15 us
    all_to_all x1, starting transfers between devices, plane_plan(): lax.all_to_all(packed, 'section', split_axis=0, concat_axis=0, tiled=True)  4.89 us
  transfers between devices with their start and end apart: 21, of which 7 were waited for; matrix products, arithmetic and copies ran while one was open for 0% of the time, Pallas kernels for 21%

profile of v2, /device:TPU:0, one launch (start us, length us, event | category | flops | bytes accessed | tf_op | source)
XLA Modules:
  0.0 119.3 jit_solution(10990073115145546739)
XLA Ops:
  0.0 2.9 %collective-permute-start.54 = (bf16[2048,256]{1,0:T(8,128)(2,1)}, bf16[2048,256]{1,0:T(8,128)(2,1)S(1)}, u32[]{:S(2)}, u32[]{:S(2)}) collective-permute-start(bf16[2048,256]{1,0:T(8,128)(2,1)} %bitcast.16), channel_id=1, source_target_pairs={{0,1},{1,0},{2,3},{3,2},{4,5},{5,4},{6,7},{7,6},{8,9},{9,8},{10,11... | collective-permute-start | bytes 3145736 | tf_op jit(solution)/shard_map/ppermute | solution.py:414
  2.9 1.5 %collective-permute-start.55 = (bf16[2048,256]{1,0:T(8,128)(2,1)}, bf16[2048,256]{1,0:T(8,128)(2,1)}, u32[]{:S(2)}, u32[]{:S(2)}) collective-permute-start(bf16[2048,256]{1,0:T(8,128)(2,1)} %bitcast.17), channel_id=1, source_target_pairs={{0,2},{1,3},{2,0},{3,1},{4,6},{5,7},{6,4},{7,5},{8,10},{9,11},{10,... | collective-permute-start | bytes 3145736 | tf_op jit(solution)/shard_map/ppermute | solution.py:415
  4.5 2.8 %shard_map.73 = bf16[8,72,512]{2,1,0:T(8,128)(2,1)} custom-call(s32[2,128]{1,0:T(2,128)} %bitcast.11, s32[2,2,128]{2,1,0:T(2,128)} %bitcast.29, f32[128,2,512]{2,1,0:T(2,128)} %state.1), custom_call_target="tpu_custom_call" | custom-call | tf_op jit(solution)/shard_map/pallas_call | solution.py:424
  7.2 4.9 %all-to-all-start = ((bf16[8,72,512]{2,1,0:T(8,128)(2,1)}), bf16[8,72,512]{2,1,0:T(8,128)(2,1)S(1)}, u32[]{:S(2)}, u32[]{:S(2)}) async-start(bf16[8,72,512]{2,1,0:T(8,128)(2,1)} %shard_map.73), calls=%async_computation | async-start | bytes 1179648 | tf_op jit(solution)/shard_map/all_to_all | solution.py:436
  12.1 16.8 %all-to-all-done.arrived = bf16[8,72,512]{2,1,0:T(8,128)(2,1)S(1)} async-done(((bf16[8,72,512]{2,1,0:T(8,128)(2,1)}), bf16[8,72,512]{2,1,0:T(8,128)(2,1)S(1)}, u32[]{:S(2)}, u32[]{:S(2)}) %all-to-all-start) | async-done | bytes 589856 | tf_op jit(solution)/shard_map/all_to_all | solution.py:436
  28.9 0.0 copy-done
  28.9 1.6 %shard_map.74 = (bf16[512,512]{1,0:T(8,128)(2,1)S(1)}, bf16[512,512]{1,0:T(8,128)(2,1)S(1)}, f32[128,8]{1,0:T(8,128)S(1)}, s32[1,512]{1,0:T(1,128)S(1)}, s32[1]{0:T(128)}) custom-call(s32[1]{0:T(128)} %bitcast.1.mp_ref, bf16[8,72,512]{2,1,0:T(8,128)(2,1)S(1)} %all-to-all-done.arrived, bf16[1024,512]{1,0:T(8,128)(2,1)S(1)} %copy-done), custom_call_target="tpu_custom_call" | custom-call | tf_op jit(solution)/shard_map/pallas_call | solution.py:437
  31.1 0.0 collective-permute-done.54
  31.2 0.0 collective-permute-done.55
  31.2 0.0 copy-start.1
  31.2 59.4 %conditional.1 = (f32[32,128]{1,0:T(8,128)S(1)}) conditional(s32[]{:T(128)} %bitcast.3, (bf16[512,512]{1,0:T(8,128)(2,1)S(1)}, bf16[512,512]{1,0:T(8,128)(2,1)S(1)}, s32[1]{0:T(128)}, bf16[2048,2048]{1,0:T(8,128)(2,1)}, bf16[2048,256]{1,0:T(8,128)(2,1)S(1)}, /*index=5*/bf16[2048,256]{1,0:T(8,128)(2,1)}, ...), branch_computations={%region_0.0_spmd, %region_1.0_spmd, %region_2.0_spmd} | conditional | flops 17179869184 | bytes 130024256 | solution.py:453
  31.6 0.6 collective-permute-start.18
  32.2 0.5 collective-permute-start.19
  32.8 7.1 %collective-permute-done.18.px = bf16[320,512]{1,0:T(8,128)(2,1)S(1)} collective-permute-done((bf16[320,512]{1,0:T(8,128)(2,1)S(1)}, bf16[320,512]{1,0:T(8,128)(2,1)S(1)}, u32[]{:S(2)}, u32[]{:S(2)}) %collective-permute-start.18) | collective-permute-done | bytes 327712 | tf_op jit(solution)/shard_map/cond/branch_1_fun/ppermute | solution.py:414
  39.9 0.2 collective-permute-done.19.py
  40.1 1.5 %collective-permute-start.20 = (bf16[320,512]{1,0:T(8,128)(2,1)S(1)}, bf16[320,512]{1,0:T(8,128)(2,1)S(1)}, u32[]{:S(2)}, u32[]{:S(2)}) collective-permute-start(bf16[320,512]{1,0:T(8,128)(2,1)S(1)} %slice.40.own), channel_id=1, source_target_pairs={{0,1},{1,0},{2,3},{3,2},{4,5},{5,4},{6,7},{7,6},{8,9},{9,8},{10,11... | collective-permute-start | bytes 983048 | tf_op jit(solution)/shard_map/cond/branch_1_fun/ppermute | solution.py:414
  41.6 0.5 collective-permute-start.21
  42.1 1.6 %collective-permute-start.30 = (bf16[160,512]{1,0:T(8,128)(2,1)S(1)}, bf16[160,512]{1,0:T(8,128)(2,1)S(1)}, u32[]{:S(2)}, u32[]{:S(2)}) collective-permute-start(bf16[160,512]{1,0:T(8,128)(2,1)S(1)} %slice.56), channel_id=1, source_target_pairs={{0,2},{1,3},{2,0},{3,1},{4,6},{5,7},{6,4},{7,5},{8,10},{9,11},{10,... | collective-permute-start | bytes 491528 | tf_op jit(solution)/shard_map/cond/branch_1_fun/ppermute | solution.py:415
  43.7 0.6 collective-permute-start.31
  44.3 4.5 %branch_1_fun.9 = (f32[320,2048]{1,0:T(8,128)S(1)}, f32[320,1]{1,0:T(8,128)S(1)}, bf16[1024,256]{1,0:T(8,128)(2,1)S(1)}, bf16[1024,256]{1,0:T(8,128)(2,1)S(1)}) custom-call(s32[1]{0:T(128)} %get-tuple-element.110.mp_ref, bf16[320,512]{1,0:T(8,128)(2,1)S(1)} %slice.41.own, bf16[320,512]{1,0:T(8,128)(2,1)S(1)} %collective-permute-done.18.px, ...), custom_call_target="tpu_custom_call" | custom-call | flops 2013265920 | bytes 8388608 | tf_op jit(solution)/shard_map/cond/branch_1_fun/pallas_call | solution.py:333
  48.8 0.0 collective-permute-done.20.px
  48.8 1.5 %collective-permute-done.21.py = bf16[320,512]{1,0:T(8,128)(2,1)S(1)} collective-permute-done((bf16[320,512]{1,0:T(8,128)(2,1)S(1)}, bf16[320,512]{1,0:T(8,128)(2,1)S(1)}, u32[]{:S(2)}, u32[]{:S(2)}) %collective-permute-start.21) | collective-permute-done | bytes 327712 | tf_op jit(solution)/shard_map/cond/branch_1_fun/ppermute | solution.py:415
  50.3 0.2 collective-permute-start.22
  50.5 0.5 collective-permute-start.23
  51.0 2.8 %collective-permute-done.30.da = bf16[160,512]{1,0:T(8,128)(2,1)S(1)} collective-permute-done((bf16[160,512]{1,0:T(8,128)(2,1)S(1)}, bf16[160,512]{1,0:T(8,128)(2,1)S(1)}, u32[]{:S(2)}, u32[]{:S(2)}) %collective-permute-start.30) | collective-permute-done | bytes 163872 | tf_op jit(solution)/shard_map/cond/branch_1_fun/ppermute | solution.py:415
  53.8 0.0 collective-permute-done.31.db
  53.8 0.0 copy-done.3
  53.8 2.2 %branch_1_fun.13 = (bf16[320,2048]{1,0:T(8,128)(2,1)S(1)}, bf16[80,2048]{1,0:T(8,128)(2,1)S(1)}) custom-call(s32[1]{0:T(128)} %get-tuple-element.110.mp_ref, f32[320,2048]{1,0:T(8,128)S(1)} %get-tuple-element.139.z, f32[320,1]{1,0:T(8,128)S(1)} %get-tuple-element.140.square, bf16[320,512]{1,0:T(8,128)(2,1)S(1)} %slice.41.own, ...), custom_call_target="tpu_custom_call" | custom-call | flops 671088640 | bytes 2097152 | tf_op jit(solution)/shard_map/cond/branch_1_fun/pallas_call | solution.py:348
  56.1 0.0 slice-done.2
  56.1 0.0 slice-done.3
  56.1 3.4 %branch_1_fun.14 = (bf16[160,1024]{1,0:T(8,128)(2,1)S(1)}, bf16[160,1024]{1,0:T(8,128)(2,1)S(1)}, bf16[160,1024]{1,0:T(8,128)(2,1)S(1)}, bf16[160,1024]{1,0:T(8,128)(2,1)S(1)}) custom-call(bf16[320,2048]{1,0:T(8,128)(2,1)S(1)} %get-tuple-element.144.hidden, bf16[2048,2048]{1,0:T(8,128)(2,1)S(1)} %bitcast.27), custom_call_target="tpu_custom_call" | custom-call | flops 2684354560 | bytes 8388608 | tf_op jit(solution)/shard_map/cond/branch_1_fun/pallas_call | solution.py:357
  59.5 0.1 collective-permute-start.32
  59.6 0.7 collective-permute-start.33
  60.3 1.4 %collective-permute-start.25 = (bf16[1024,256]{1,0:T(8,128)(2,1)S(1)}, bf16[1024,256]{1,0:T(8,128)(2,1)S(1)}, u32[]{:S(2)}, u32[]{:S(2)}) collective-permute-start(bf16[1024,256]{1,0:T(8,128)(2,1)S(1)} %get-tuple-element.127), channel_id=1, source_target_pairs={{0,2},{1,3},{2,0},{3,1},{4,6},{5,7},{6,4},{7,5},{8,10},{9,11},{10,... | collective-permute-start | bytes 1572872 | tf_op jit(solution)/shard_map/cond/branch_1_fun/ppermute | solution.py:415
  61.7 0.0 collective-permute-done.22.da
  61.7 1.9 %collective-permute-start.26 = (bf16[1024,256]{1,0:T(8,128)(2,1)S(1)}, bf16[1024,256]{1,0:T(8,128)(2,1)S(1)}, u32[]{:S(2)}, u32[]{:S(2)}) collective-permute-start(bf16[1024,256]{1,0:T(8,128)(2,1)S(1)} %get-tuple-element.128), channel_id=1, source_target_pairs={{0,1},{1,0},{2,3},{3,2},{4,5},{5,4},{6,7},{7,6},{8,9},{9,8},{10,11... | collective-permute-start | bytes 1572872 | tf_op jit(solution)/shard_map/cond/branch_1_fun/ppermute | solution.py:414
  63.6 0.0 collective-permute-done.23.db
  63.6 4.4 %branch_1_fun.10 = (bf16[320,2048]{1,0:T(8,128)(2,1)S(1)}, bf16[80,2048]{1,0:T(8,128)(2,1)S(1)}) custom-call(s32[1]{0:T(128)} %get-tuple-element.110.mp_ref, bf16[320,512]{1,0:T(8,128)(2,1)S(1)} %slice.40.own, bf16[320,512]{1,0:T(8,128)(2,1)S(1)} %collective-permute-done.20.px, bf16[320,512]{1,0:T(8,128)(2,1)S(1)} %collective-permute-done.21.py, ...), custom_call_target="tpu_custom_call" | custom-call | flops 2684354560 | bytes 8388608 | tf_op jit(solution)/shard_map/cond/branch_1_fun/pallas_call | solution.py:322
  68.0 3.4 %branch_1_fun.11 = (bf16[160,1024]{1,0:T(8,128)(2,1)S(1)}, bf16[160,1024]{1,0:T(8,128)(2,1)S(1)}, bf16[160,1024]{1,0:T(8,128)(2,1)S(1)}, bf16[160,1024]{1,0:T(8,128)(2,1)S(1)}) custom-call(bf16[320,2048]{1,0:T(8,128)(2,1)S(1)} %get-tuple-element.123.hidden, bf16[2048,2048]{1,0:T(8,128)(2,1)S(1)} %bitcast.27), custom_call_target="tpu_custom_call" | custom-call | flops 2684354560 | bytes 8388608 | tf_op jit(solution)/shard_map/cond/branch_1_fun/pallas_call | solution.py:357
  71.4 0.0 copy-start.6
  71.5 0.1 collective-permute-start.24
  71.6 0.0 collective-permute-done.32.got_a
  71.6 0.6 collective-permute-start.27
  72.2 0.0 collective-permute-done.33.got_b
  72.2 0.1 branch_1_fun.15
  72.3 1.5 %collective-permute-start.34 = (bf16[80,1024]{1,0:T(8,128)(2,1)S(1)}, bf16[80,1024]{1,0:T(8,128)(2,1)S(1)}, u32[]{:S(2)}, u32[]{:S(2)}) collective-permute-start(bf16[80,1024]{1,0:T(8,128)(2,1)S(1)} %get-tuple-element.149), channel_id=1, source_target_pairs={{0,2},{1,3},{2,0},{3,1},{4,6},{5,7},{6,4},{7,5},{8,10},{9,11},{10,... | collective-permute-start | bytes 491528 | tf_op jit(solution)/shard_map/cond/branch_1_fun/ppermute | solution.py:415
  73.8 5.8 %collective-permute-done.24.got_a = bf16[160,1024]{1,0:T(8,128)(2,1)S(1)} collective-permute-done((bf16[160,1024]{1,0:T(8,128)(2,1)S(1)}, bf16[160,1024]{1,0:T(8,128)(2,1)S(1)}, u32[]{:S(2)}, u32[]{:S(2)}) %collective-permute-start.24) | collective-permute-done | bytes 327712 | tf_op jit(solution)/shard_map/cond/branch_1_fun/ppermute | solution.py:414
  79.6 0.4 collective-permute-start.35
  80.0 0.0 collective-permute-done.25.h3_top
  80.0 0.0 collective-permute-done.26.h3_bottom
  80.0 0.0 collective-permute-done.27.got_b
  80.0 0.1 branch_1_fun.12
  80.1 0.8 collective-permute-start.28
  80.9 1.4 %collective-permute-start.29 = (bf16[80,1024]{1,0:T(8,128)(2,1)S(1)}, bf16[80,1024]{1,0:T(8,128)(2,1)S(1)}, u32[]{:S(2)}, u32[]{:S(2)}) collective-permute-start(bf16[80,1024]{1,0:T(8,128)(2,1)S(1)} %get-tuple-element.133), channel_id=1, source_target_pairs={{0,1},{1,0},{2,3},{3,2},{4,5},{5,4},{6,7},{7,6},{8,9},{9,8},{10,11... | collective-permute-start | bytes 491528 | tf_op jit(solution)/shard_map/cond/branch_1_fun/ppermute | solution.py:414
  82.3 0.0 collective-permute-done.34.last_a
  82.3 2.6 %collective-permute-done.35.last_b = bf16[80,1024]{1,0:T(8,128)(2,1)S(1)} collective-permute-done((bf16[80,1024]{1,0:T(8,128)(2,1)S(1)}, bf16[80,1024]{1,0:T(8,128)(2,1)S(1)}, u32[]{:S(2)}, u32[]{:S(2)}) %collective-permute-start.35) | collective-permute-done | bytes 163872 | tf_op jit(solution)/shard_map/cond/branch_1_fun/ppermute | solution.py:414
  84.9 0.0 copy-done.6
  84.9 2.6 %branch_1_fun.16.rest_0_ = f32[8,64]{1,0:T(8,128)S(1)} custom-call(s32[1]{0:T(128)} %get-tuple-element.110.mp_ref, bf16[80,2048]{1,0:T(8,128)(2,1)S(1)} %get-tuple-element.143.mine, bf16[160,1024]{1,0:T(8,128)(2,1)S(1)} %get-tuple-element.145.keep_a, bf16[160,1024]{1,0:T(8,128)(2,1)S(1)} %collective-permute-done.32.got_a, ...), custom_call_target="tpu_custom_call" | custom-call | tf_op jit(solution)/shard_map/cond/branch_1_fun/pallas_call | solution.py:375
  87.4 0.0 collective-permute-done.28.last_a
  87.4 0.0 collective-permute-done.29.last_b
  87.5 2.6 %branch_1_fun.17 = f32[32,128]{1,0:T(8,128)S(1)} custom-call(s32[1]{0:T(128)} %get-tuple-element.110.mp_ref, bf16[80,2048]{1,0:T(8,128)(2,1)S(1)} %get-tuple-element.122.mine, bf16[160,1024]{1,0:T(8,128)(2,1)S(1)} %get-tuple-element.125.keep_a, bf16[160,1024]{1,0:T(8,128)(2,1)S(1)} %collective-permute-done.24.got_a, ...), custom_call_target="tpu_custom_call" | custom-call | tf_op jit(solution)/shard_map/cond/branch_1_fun/pallas_call | solution.py:375
  90.5 27.6 %all_to_all.16 = f32[32,1,128]{2,1,0:T(1,128)S(1)} all-to-all(f32[32,1,128]{2,1,0:T(1,128)S(1)} %bitcast.28), channel_id=1, replica_groups=mesh['section'=8,'mp'=4] {'section','mp'}, dimensions={0} | all-to-all | bytes 32768 | tf_op jit(solution)/shard_map/all_to_all | solution.py:454
  118.1 0.0 copy-done.1
  118.1 1.1 shard_map.75
  (12 shorter events, 0.1 us)
Async XLA Ops:
  0.0 28.9 %copy-start = (bf16[1024,512]{1,0:T(8,128)(2,1)S(1)}, bf16[1024,512]{1,0:T(8,128)(2,1)}, u32[]{:S(2)}) copy-start(bf16[1024,512]{1,0:T(8,128)(2,1)} %embed.1) | copy-start | bytes 3145732
  0.0 31.1 %collective-permute-start.54 = (bf16[2048,256]{1,0:T(8,128)(2,1)}, bf16[2048,256]{1,0:T(8,128)(2,1)S(1)}, u32[]{:S(2)}, u32[]{:S(2)}) collective-permute-start(bf16[2048,256]{1,0:T(8,128)(2,1)} %bitcast.16), channel_id=1, source_target_pairs={{0,1},{1,0},{2,3},{3,2},{4,5},{5,4},{6,7},{7,6},{8,9},{9,8},{10,11... | collective-permute-start | bytes 3145736 | tf_op jit(solution)/shard_map/ppermute | solution.py:414
  2.9 28.2 %collective-permute-start.55 = (bf16[2048,256]{1,0:T(8,128)(2,1)}, bf16[2048,256]{1,0:T(8,128)(2,1)}, u32[]{:S(2)}, u32[]{:S(2)}) collective-permute-start(bf16[2048,256]{1,0:T(8,128)(2,1)} %bitcast.17), channel_id=1, source_target_pairs={{0,2},{1,3},{2,0},{3,1},{4,6},{5,7},{6,4},{7,5},{8,10},{9,11},{10,... | collective-permute-start | bytes 3145736 | tf_op jit(solution)/shard_map/ppermute | solution.py:415
  7.2 21.7 %all-to-all-start = ((bf16[8,72,512]{2,1,0:T(8,128)(2,1)}), bf16[8,72,512]{2,1,0:T(8,128)(2,1)S(1)}, u32[]{:S(2)}, u32[]{:S(2)}) async-start(bf16[8,72,512]{2,1,0:T(8,128)(2,1)} %shard_map.73), calls=%async_computation | async-start | bytes 1179648 | tf_op jit(solution)/shard_map/all_to_all | solution.py:436
  31.2 86.9 %copy-start.1 = (s32[128,2]{0,1:T(2,128)S(1)}, s32[128,2]{0,1:T(2,128)}, u32[]{:S(2)}) copy-start(s32[128,2]{0,1:T(2,128)} %param.10) | copy-start | bytes 3076
  31.6 8.2 %collective-permute-start.18 = (bf16[320,512]{1,0:T(8,128)(2,1)S(1)}, bf16[320,512]{1,0:T(8,128)(2,1)S(1)}, u32[]{:S(2)}, u32[]{:S(2)}) collective-permute-start(bf16[320,512]{1,0:T(8,128)(2,1)S(1)} %slice.41.own), channel_id=1, source_target_pairs={{0,1},{1,0},{2,3},{3,2},{4,5},{5,4},{6,7},{7,6},{8,9},{9,8},{10,11... | collective-permute-start | bytes 983048 | tf_op jit(solution)/shard_map/cond/branch_1_fun/ppermute | solution.py:414
  32.2 7.9 %collective-permute-start.19 = (bf16[320,512]{1,0:T(8,128)(2,1)S(1)}, bf16[320,512]{1,0:T(8,128)(2,1)S(1)}, u32[]{:S(2)}, u32[]{:S(2)}) collective-permute-start(bf16[320,512]{1,0:T(8,128)(2,1)S(1)} %slice.41.own), channel_id=1, source_target_pairs={{0,2},{1,3},{2,0},{3,1},{4,6},{5,7},{6,4},{7,5},{8,10},{9,11},{10,... | collective-permute-start | bytes 983048 | tf_op jit(solution)/shard_map/cond/branch_1_fun/ppermute | solution.py:415
  40.1 8.7 %collective-permute-start.20 = (bf16[320,512]{1,0:T(8,128)(2,1)S(1)}, bf16[320,512]{1,0:T(8,128)(2,1)S(1)}, u32[]{:S(2)}, u32[]{:S(2)}) collective-permute-start(bf16[320,512]{1,0:T(8,128)(2,1)S(1)} %slice.40.own), channel_id=1, source_target_pairs={{0,1},{1,0},{2,3},{3,2},{4,5},{5,4},{6,7},{7,6},{8,9},{9,8},{10,11... | collective-permute-start | bytes 983048 | tf_op jit(solution)/shard_map/cond/branch_1_fun/ppermute | solution.py:414
  41.6 8.7 %collective-permute-start.21 = (bf16[320,512]{1,0:T(8,128)(2,1)S(1)}, bf16[320,512]{1,0:T(8,128)(2,1)S(1)}, u32[]{:S(2)}, u32[]{:S(2)}) collective-permute-start(bf16[320,512]{1,0:T(8,128)(2,1)S(1)} %slice.40.own), channel_id=1, source_target_pairs={{0,2},{1,3},{2,0},{3,1},{4,6},{5,7},{6,4},{7,5},{8,10},{9,11},{10,... | collective-permute-start | bytes 983048 | tf_op jit(solution)/shard_map/cond/branch_1_fun/ppermute | solution.py:415
  42.1 11.7 %collective-permute-start.30 = (bf16[160,512]{1,0:T(8,128)(2,1)S(1)}, bf16[160,512]{1,0:T(8,128)(2,1)S(1)}, u32[]{:S(2)}, u32[]{:S(2)}) collective-permute-start(bf16[160,512]{1,0:T(8,128)(2,1)S(1)} %slice.56), channel_id=1, source_target_pairs={{0,2},{1,3},{2,0},{3,1},{4,6},{5,7},{6,4},{7,5},{8,10},{9,11},{10,... | collective-permute-start | bytes 491528 | tf_op jit(solution)/shard_map/cond/branch_1_fun/ppermute | solution.py:415
  43.7 10.1 %collective-permute-start.31 = (bf16[160,512]{1,0:T(8,128)(2,1)S(1)}, bf16[160,512]{1,0:T(8,128)(2,1)S(1)}, u32[]{:S(2)}, u32[]{:S(2)}) collective-permute-start(bf16[160,512]{1,0:T(8,128)(2,1)S(1)} %slice.57), channel_id=1, source_target_pairs={{0,1},{1,0},{2,3},{3,2},{4,5},{5,4},{6,7},{7,6},{8,9},{9,8},{10,11... | collective-permute-start | bytes 491528 | tf_op jit(solution)/shard_map/cond/branch_1_fun/ppermute | solution.py:414
  44.3 9.5 %copy-start.3 = (bf16[2048,2048]{1,0:T(8,128)(2,1)S(1)}, bf16[2048,2048]{1,0:T(8,128)(2,1)}, u32[]{:S(2)}) copy-start(bf16[2048,2048]{1,0:T(8,128)(2,1)} %get-tuple-element.114.w_in) | copy-start | bytes 25165828 | tf_op jit(solution)/shard_map/cond
  44.3 11.7 %slice-start.2 = ((s8[8388608]{0:T(1024)(128)(4,1)}), s8[4194304]{0:T(1024)(128)(4,1)S(1)}, s32[]{:S(2)}) async-start(s8[8388608]{0:T(1024)(128)(4,1)} %bitcast.26), calls=%async_computation.4 | async-start | bytes 8388608 | tf_op jit(solution)/shard_map/cond
  50.3 11.4 %collective-permute-start.22 = (bf16[160,512]{1,0:T(8,128)(2,1)S(1)}, bf16[160,512]{1,0:T(8,128)(2,1)S(1)}, u32[]{:S(2)}, u32[]{:S(2)}) collective-permute-start(bf16[160,512]{1,0:T(8,128)(2,1)S(1)} %slice.42), channel_id=1, source_target_pairs={{0,2},{1,3},{2,0},{3,1},{4,6},{5,7},{6,4},{7,5},{8,10},{9,11},{10,... | collective-permute-start | bytes 491528 | tf_op jit(solution)/shard_map/cond/branch_1_fun/ppermute | solution.py:415
  50.5 13.1 %collective-permute-start.23 = (bf16[160,512]{1,0:T(8,128)(2,1)S(1)}, bf16[160,512]{1,0:T(8,128)(2,1)S(1)}, u32[]{:S(2)}, u32[]{:S(2)}) collective-permute-start(bf16[160,512]{1,0:T(8,128)(2,1)S(1)} %slice.43), channel_id=1, source_target_pairs={{0,1},{1,0},{2,3},{3,2},{4,5},{5,4},{6,7},{7,6},{8,9},{9,8},{10,11... | collective-permute-start | bytes 491528 | tf_op jit(solution)/shard_map/cond/branch_1_fun/ppermute | solution.py:414
  53.8 2.3 %slice-start.3 = ((s8[8388608]{0:T(1024)(128)(4,1)}), s8[4194304]{0:T(1024)(128)(4,1)S(1)}, s32[]{:S(2)}) async-start(s8[8388608]{0:T(1024)(128)(4,1)} %bitcast.26), calls=%async_computation.5 | async-start | bytes 8388608 | tf_op jit(solution)/shard_map/cond
  59.5 12.1 %collective-permute-start.32 = (bf16[160,1024]{1,0:T(8,128)(2,1)S(1)}, bf16[160,1024]{1,0:T(8,128)(2,1)S(1)}, u32[]{:S(2)}, u32[]{:S(2)}) collective-permute-start(bf16[160,1024]{1,0:T(8,128)(2,1)S(1)} %get-tuple-element.146), channel_id=1, source_target_pairs={{0,1},{1,0},{2,3},{3,2},{4,5},{5,4},{6,7},{7,6},{8,9},{9,8},{10,11... | collective-permute-start | bytes 983048 | tf_op jit(solution)/shard_map/cond/branch_1_fun/ppermute | solution.py:414
  59.6 12.7 %collective-permute-start.33 = (bf16[160,1024]{1,0:T(8,128)(2,1)S(1)}, bf16[160,1024]{1,0:T(8,128)(2,1)S(1)}, u32[]{:S(2)}, u32[]{:S(2)}) collective-permute-start(bf16[160,1024]{1,0:T(8,128)(2,1)S(1)} %get-tuple-element.148), channel_id=1, source_target_pairs={{0,2},{1,3},{2,0},{3,1},{4,6},{5,7},{6,4},{7,5},{8,10},{9,11},{10,... | collective-permute-start | bytes 983048 | tf_op jit(solution)/shard_map/cond/branch_1_fun/ppermute | solution.py:415
  60.3 19.7 %collective-permute-start.25 = (bf16[1024,256]{1,0:T(8,128)(2,1)S(1)}, bf16[1024,256]{1,0:T(8,128)(2,1)S(1)}, u32[]{:S(2)}, u32[]{:S(2)}) collective-permute-start(bf16[1024,256]{1,0:T(8,128)(2,1)S(1)} %get-tuple-element.127), channel_id=1, source_target_pairs={{0,2},{1,3},{2,0},{3,1},{4,6},{5,7},{6,4},{7,5},{8,10},{9,11},{10,... | collective-permute-start | bytes 1572872 | tf_op jit(solution)/shard_map/cond/branch_1_fun/ppermute | solution.py:415
  61.7 18.3 %collective-permute-start.26 = (bf16[1024,256]{1,0:T(8,128)(2,1)S(1)}, bf16[1024,256]{1,0:T(8,128)(2,1)S(1)}, u32[]{:S(2)}, u32[]{:S(2)}) collective-permute-start(bf16[1024,256]{1,0:T(8,128)(2,1)S(1)} %get-tuple-element.128), channel_id=1, source_target_pairs={{0,1},{1,0},{2,3},{3,2},{4,5},{5,4},{6,7},{7,6},{8,9},{9,8},{10,11... | collective-permute-start | bytes 1572872 | tf_op jit(solution)/shard_map/cond/branch_1_fun/ppermute | solution.py:414
  71.4 13.4 %copy-start.6 = (bf16[2048,256]{1,0:T(8,128)(2,1)S(1)}, bf16[2048,256]{1,0:T(8,128)(2,1)}, u32[]{:S(2)}) copy-start(bf16[2048,256]{1,0:T(8,128)(2,1)} %get-tuple-element.134.h0) | copy-start | bytes 3145732 | tf_op jit(solution)/shard_map/cond
  71.5 8.1 %collective-permute-start.24 = (bf16[160,1024]{1,0:T(8,128)(2,1)S(1)}, bf16[160,1024]{1,0:T(8,128)(2,1)S(1)}, u32[]{:S(2)}, u32[]{:S(2)}) collective-permute-start(bf16[160,1024]{1,0:T(8,128)(2,1)S(1)} %get-tuple-element.126), channel_id=1, source_target_pairs={{0,1},{1,0},{2,3},{3,2},{4,5},{5,4},{6,7},{7,6},{8,9},{9,8},{10,11... | collective-permute-start | bytes 983048 | tf_op jit(solution)/shard_map/cond/branch_1_fun/ppermute | solution.py:414
  71.6 8.4 %collective-permute-start.27 = (bf16[160,1024]{1,0:T(8,128)(2,1)S(1)}, bf16[160,1024]{1,0:T(8,128)(2,1)S(1)}, u32[]{:S(2)}, u32[]{:S(2)}) collective-permute-start(bf16[160,1024]{1,0:T(8,128)(2,1)S(1)} %get-tuple-element.131), channel_id=1, source_target_pairs={{0,2},{1,3},{2,0},{3,1},{4,6},{5,7},{6,4},{7,5},{8,10},{9,11},{10,... | collective-permute-start | bytes 983048 | tf_op jit(solution)/shard_map/cond/branch_1_fun/ppermute | solution.py:415
  72.3 10.0 %collective-permute-start.34 = (bf16[80,1024]{1,0:T(8,128)(2,1)S(1)}, bf16[80,1024]{1,0:T(8,128)(2,1)S(1)}, u32[]{:S(2)}, u32[]{:S(2)}) collective-permute-start(bf16[80,1024]{1,0:T(8,128)(2,1)S(1)} %get-tuple-element.149), channel_id=1, source_target_pairs={{0,2},{1,3},{2,0},{3,1},{4,6},{5,7},{6,4},{7,5},{8,10},{9,11},{10,... | collective-permute-start | bytes 491528 | tf_op jit(solution)/shard_map/cond/branch_1_fun/ppermute | solution.py:415
  79.6 5.3 %collective-permute-start.35 = (bf16[80,1024]{1,0:T(8,128)(2,1)S(1)}, bf16[80,1024]{1,0:T(8,128)(2,1)S(1)}, u32[]{:S(2)}, u32[]{:S(2)}) collective-permute-start(bf16[80,1024]{1,0:T(8,128)(2,1)S(1)} %get-tuple-element.150), channel_id=1, source_target_pairs={{0,1},{1,0},{2,3},{3,2},{4,5},{5,4},{6,7},{7,6},{8,9},{9,8},{10,11... | collective-permute-start | bytes 491528 | tf_op jit(solution)/shard_map/cond/branch_1_fun/ppermute | solution.py:414
  80.1 7.4 %collective-permute-start.28 = (bf16[80,1024]{1,0:T(8,128)(2,1)S(1)}, bf16[80,1024]{1,0:T(8,128)(2,1)S(1)}, u32[]{:S(2)}, u32[]{:S(2)}) collective-permute-start(bf16[80,1024]{1,0:T(8,128)(2,1)S(1)} %get-tuple-element.132), channel_id=1, source_target_pairs={{0,2},{1,3},{2,0},{3,1},{4,6},{5,7},{6,4},{7,5},{8,10},{9,11},{10,... | collective-permute-start | bytes 491528 | tf_op jit(solution)/shard_map/cond/branch_1_fun/ppermute | solution.py:415
  80.9 6.6 %collective-permute-start.29 = (bf16[80,1024]{1,0:T(8,128)(2,1)S(1)}, bf16[80,1024]{1,0:T(8,128)(2,1)S(1)}, u32[]{:S(2)}, u32[]{:S(2)}) collective-permute-start(bf16[80,1024]{1,0:T(8,128)(2,1)S(1)} %get-tuple-element.133), channel_id=1, source_target_pairs={{0,1},{1,0},{2,3},{3,2},{4,5},{5,4},{6,7},{7,6},{8,9},{9,8},{10,11... | collective-permute-start | bytes 491528 | tf_op jit(solution)/shard_map/cond/branch_1_fun/ppermute | solution.py:414

commit v3 on v2

--- a/solution.py
+++ b/solution.py
@@ -222,9 +222,8 @@
                 ref[(i % 2) * group : (i % 2 + 1) * group, cols] = part[j * group : (j + 1) * group]
 
 
-def fold_kernel(keep_a, got_a, keep_b, got_b, out_a, out_b):
-    out_a[...] = (keep_a[...].astype(f32) + got_a[...].astype(f32)).astype(bf16)
-    out_b[...] = (keep_b[...].astype(f32) + got_b[...].astype(f32)).astype(bf16)
+def fold_kernel(keep, got, out):
+    out[...] = (keep[...].astype(f32) + got[...].astype(f32)).astype(bf16)
 
 
 def score_kernel(sections, cap, step_idx, mp_ref, mine, keep_a, got_a, last_a, keep_b, got_b, last_b, h0, h1, h2, h3_top, h3_bottom, notes, place, *rest):
@@ -360,16 +359,15 @@
             cost=pl.CostEstimate(flops=flops, bytes_accessed=2 * width * inner, transcendentals=0),
         )(hidden, w_out)
 
-    def fold(keep_a, got_a, keep_b, got_b):
+    def fold(keep, got):
         second = pl.BlockSpec((group, width // 2), lambda i: (1, 0))
-        whole = pl.BlockSpec((group, width // 2), lambda i: (0, 0))
         return call(
             fold_kernel,
-            (shape(group, width // 2),) * 2,
+            shape(group, width // 2),
             grid=(1,),
-            in_specs=[second] * 4,
-            out_specs=(whole,) * 2,
-        )(keep_a, got_a, keep_b, got_b)
+            in_specs=[second] * 2,
+            out_specs=pl.BlockSpec((group, width // 2), lambda i: (0, 0)),
+        )(keep, got)
 
     def score(step_idx, pieces, *earlier):
         return call(
@@ -392,12 +390,12 @@
     send_a0, send_b0, keep_a0, keep_b0 = to_parts(hidden0)
     got_a0, got_b0 = over_x(send_a0), over_y(send_b0)
     hidden1, mine1 = to_hidden(x1, near1, far1)
-    fold_a0, fold_b0 = fold(keep_a0, got_a0, keep_b0, got_b0)
+    fold_a0, fold_b0 = fold(keep_a0, got_a0), fold(keep_b0, got_b0)
     last_a0, last_b0 = over_y(fold_a0), over_x(fold_b0)
     send_a1, send_b1, keep_a1, keep_b1 = to_parts(hidden1)
     got_a1, got_b1 = over_x(send_a1), over_y(send_b1)
     got_a1, *head_far = lax.optimization_barrier((got_a1, *head_far))
-    fold_a1, fold_b1 = fold(keep_a1, got_a1, keep_b1, got_b1)
+    fold_a1, fold_b1 = fold(keep_a1, got_a1), fold(keep_b1, got_b1)
     last_a1, last_b1 = over_y(fold_a1), over_x(fold_b1)
     first = score(0, (mine0, keep_a0, got_a0, last_a0, keep_b0, got_b0, last_b0))
     return score(1, (mine1, keep_a1, got_a1, last_a1, keep_b1, got_b1, last_b1), first)

time: 120 us -> 120 us (level)
  blocking collectives: 27.6 us -> 8.87 us
  waiting for transfers between devices: 36.8 us -> 47.8 us
  Pallas kernels: 28.7 us -> 36.3 us
  starting transfers between devices: 24.3 us -> 25.9 us
    all_to_all x1, blocking collectives: 27.6 us -> 8.87 us  [plane_plan(): lax.all_to_all(sent, ('section', 'mp'), split_axis=0, concat_axis=0, tile...]
    ppermute x10, waiting for transfers between devices: 15.5 us -> 21.2 us  [plane_plan(): over_x = lambda v: lax.ppermute(v, 'mp', [(i, i ^ 1) for i in range(4)])]
    ppermute x10, waiting for transfers between devices: 4.56 us -> 9.78 us  [plane_plan(): over_y = lambda v: lax.ppermute(v, 'mp', [(i, i ^ 2) for i in range(4)])]
    pallas_call x2, Pallas kernels: 6.81 us -> 10.1 us  [to_parts(): call(functools.partial(part_kernel, size, TILE), (shape(h, width // 2),)...]
    ppermute x10, starting transfers between devices: 10.1 us -> 12.6 us  [plane_plan(): over_x = lambda v: lax.ppermute(v, 'mp', [(i, i ^ 1) for i in range(4)])]
    pallas_call x1, Pallas kernels: 4.4 us -> 6.58 us  [to_hidden(): call(functools.partial(hidden_kernel, size, TILE), (shape(size, inner), s...]
  transfers between devices with their start and end apart: 21 -> 21, of which waited for: 7 -> 11; matrix products, arithmetic and copies ran while one was open for 0% -> 0% of each run, Pallas kernels for 21% -> 27%
where the time goes in v3:
time: 120 us
  waiting for transfers between devices  47.8 us (40%)
  Pallas kernels  36.3 us (30%)
  starting transfers between devices  25.9 us (22%)
  blocking collectives  8.87 us (7%)
    ppermute x10, waiting for transfers between devices, plane_plan(): over_x = lambda v: lax.ppermute(v, 'mp', [(i, i ^ 1) for i in range(4)])  21.2 us
    all_to_all x1, waiting for transfers between devices, plane_plan(): lax.all_to_all(packed, 'section', split_axis=0, concat_axis=0, tiled=True)  16.8 us
    ppermute x10, starting transfers between devices, plane_plan(): over_x = lambda v: lax.ppermute(v, 'mp', [(i, i ^ 1) for i in range(4)])  12.6 us
    pallas_call x2, Pallas kernels, to_parts(): call(functools.partial(part_kernel, size, TILE), (shape(h, width // 2),)...  10.1 us
    ppermute x10, waiting for transfers between devices, plane_plan(): over_y = lambda v: lax.ppermute(v, 'mp', [(i, i ^ 2) for i in range(4)])  9.78 us
    all_to_all x1, blocking collectives, plane_plan(): lax.all_to_all(sent, ('section', 'mp'), split_axis=0, concat_axis=0, tile...  8.87 us
    ppermute x10, starting transfers between devices, plane_plan(): over_y = lambda v: lax.ppermute(v, 'mp', [(i, i ^ 2) for i in range(4)])  8.44 us
    pallas_call x1, Pallas kernels, to_hidden(): call(functools.partial(hidden_kernel, size, TILE), (shape(size, inner), s...  6.58 us
  transfers between devices with their start and end apart: 21, of which 11 were waited for; matrix products, arithmetic and copies ran while one was open for 0% of the time, Pallas kernels for 27%

profile of v3, /device:TPU:0, one launch (start us, length us, event | category | flops | bytes accessed | tf_op | source)
XLA Modules:
  0.0 120.2 jit_solution(1576971315697840753)
XLA Ops:
  0.0 2.9 %collective-permute-start.54 = (bf16[2048,256]{1,0:T(8,128)(2,1)}, bf16[2048,256]{1,0:T(8,128)(2,1)S(1)}, u32[]{:S(2)}, u32[]{:S(2)}) collective-permute-start(bf16[2048,256]{1,0:T(8,128)(2,1)} %bitcast.16), channel_id=1, source_target_pairs={{0,1},{1,0},{2,3},{3,2},{4,5},{5,4},{6,7},{7,6},{8,9},{9,8},{10,11... | collective-permute-start | bytes 3145736 | tf_op jit(solution)/shard_map/ppermute | solution.py:412
  2.9 1.5 %collective-permute-start.55 = (bf16[2048,256]{1,0:T(8,128)(2,1)}, bf16[2048,256]{1,0:T(8,128)(2,1)}, u32[]{:S(2)}, u32[]{:S(2)}) collective-permute-start(bf16[2048,256]{1,0:T(8,128)(2,1)} %bitcast.17), channel_id=1, source_target_pairs={{0,2},{1,3},{2,0},{3,1},{4,6},{5,7},{6,4},{7,5},{8,10},{9,11},{10,... | collective-permute-start | bytes 3145736 | tf_op jit(solution)/shard_map/ppermute | solution.py:413
  4.5 2.8 %shard_map.73 = bf16[8,72,512]{2,1,0:T(8,128)(2,1)} custom-call(s32[2,128]{1,0:T(2,128)} %bitcast.11, s32[2,2,128]{2,1,0:T(2,128)} %bitcast.29, f32[128,2,512]{2,1,0:T(2,128)} %state.1), custom_call_target="tpu_custom_call" | custom-call | tf_op jit(solution)/shard_map/pallas_call | solution.py:422
  7.2 4.9 %all-to-all-start = ((bf16[8,72,512]{2,1,0:T(8,128)(2,1)}), bf16[8,72,512]{2,1,0:T(8,128)(2,1)S(1)}, u32[]{:S(2)}, u32[]{:S(2)}) async-start(bf16[8,72,512]{2,1,0:T(8,128)(2,1)} %shard_map.73), calls=%async_computation | async-start | bytes 1179648 | tf_op jit(solution)/shard_map/all_to_all | solution.py:434
  12.1 16.8 %all-to-all-done.arrived = bf16[8,72,512]{2,1,0:T(8,128)(2,1)S(1)} async-done(((bf16[8,72,512]{2,1,0:T(8,128)(2,1)}), bf16[8,72,512]{2,1,0:T(8,128)(2,1)S(1)}, u32[]{:S(2)}, u32[]{:S(2)}) %all-to-all-start) | async-done | bytes 589856 | tf_op jit(solution)/shard_map/all_to_all | solution.py:434
  28.9 0.0 copy-done
  28.9 1.6 %shard_map.74 = (bf16[512,512]{1,0:T(8,128)(2,1)S(1)}, bf16[512,512]{1,0:T(8,128)(2,1)S(1)}, f32[128,8]{1,0:T(8,128)S(1)}, s32[1,512]{1,0:T(1,128)S(1)}, s32[1]{0:T(128)}) custom-call(s32[1]{0:T(128)} %bitcast.1.mp_ref, bf16[8,72,512]{2,1,0:T(8,128)(2,1)S(1)} %all-to-all-done.arrived, bf16[1024,512]{1,0:T(8,128)(2,1)S(1)} %copy-done), custom_call_target="tpu_custom_call" | custom-call | tf_op jit(solution)/shard_map/pallas_call | solution.py:435
  31.1 0.0 collective-permute-done.54
  31.1 0.0 collective-permute-done.55
  31.1 0.0 copy-start.1
  31.1 79.0 %conditional.1 = (f32[32,128]{1,0:T(8,128)S(1)}) conditional(s32[]{:T(128)} %bitcast.3, (bf16[512,512]{1,0:T(8,128)(2,1)S(1)}, bf16[512,512]{1,0:T(8,128)(2,1)S(1)}, s32[1]{0:T(128)}, bf16[2048,2048]{1,0:T(8,128)(2,1)}, bf16[2048,256]{1,0:T(8,128)(2,1)S(1)}, /*index=5*/bf16[2048,256]{1,0:T(8,128)(2,1)}, ...), branch_computations={%region_0.0_spmd, %region_1.0_spmd, %region_2.0_spmd} | conditional | flops 17179869184 | bytes 130024256 | solution.py:451
  31.3 0.6 collective-permute-start
  31.9 0.5 collective-permute-start.1
  32.5 10.9 %collective-permute-done.px = bf16[512,512]{1,0:T(8,128)(2,1)S(1)} collective-permute-done((bf16[512,512]{1,0:T(8,128)(2,1)S(1)}, bf16[512,512]{1,0:T(8,128)(2,1)S(1)}, u32[]{:S(2)}, u32[]{:S(2)}) %collective-permute-start) | collective-permute-done | bytes 524320 | tf_op jit(solution)/shard_map/cond/branch_0_fun/ppermute | solution.py:412
  43.4 0.0 collective-permute-done.1.py
  43.4 1.7 %collective-permute-start.2 = (bf16[512,512]{1,0:T(8,128)(2,1)S(1)}, bf16[512,512]{1,0:T(8,128)(2,1)S(1)}, u32[]{:S(2)}, u32[]{:S(2)}) collective-permute-start(bf16[512,512]{1,0:T(8,128)(2,1)S(1)} %get-tuple-element.72.own), channel_id=1, source_target_pairs={{0,1},{1,0},{2,3},{3,2},{4,5},{5,4},{6,7},{7,6},{8,9},{9,8},{10,11... | collective-permute-start | bytes 1572872 | tf_op jit(solution)/shard_map/cond/branch_0_fun/ppermute | solution.py:412
  45.1 0.5 collective-permute-start.3
  45.7 1.6 %collective-permute-start.12 = (bf16[256,512]{1,0:T(8,128)(2,1)S(1)}, bf16[256,512]{1,0:T(8,128)(2,1)S(1)}, u32[]{:S(2)}, u32[]{:S(2)}) collective-permute-start(bf16[256,512]{1,0:T(8,128)(2,1)S(1)} %slice.54), channel_id=1, source_target_pairs={{0,2},{1,3},{2,0},{3,1},{4,6},{5,7},{6,4},{7,5},{8,10},{9,11},{10,... | collective-permute-start | bytes 786440 | tf_op jit(solution)/shard_map/cond/branch_0_fun/ppermute | solution.py:413
  47.3 0.4 collective-permute-start.13
  47.6 5.6 %branch_0_fun.11 = (f32[512,2048]{1,0:T(8,128)S(1)}, f32[512,1]{1,0:T(8,128)S(1)}, bf16[1024,256]{1,0:T(8,128)(2,1)S(1)}, bf16[1024,256]{1,0:T(8,128)(2,1)S(1)}) custom-call(s32[1]{0:T(128)} %get-tuple-element.68.mp_ref, bf16[512,512]{1,0:T(8,128)(2,1)S(1)} %get-tuple-element.71.own, bf16[512,512]{1,0:T(8,128)(2,1)S(1)} %collective-permute-done.px, ...), custom_call_target="tpu_custom_call" | custom-call | flops 3221225472 | bytes 8388608 | tf_op jit(solution)/shard_map/cond/branch_0_fun/pallas_call | solution.py:332
  53.3 3.9 %collective-permute-done.2.px = bf16[512,512]{1,0:T(8,128)(2,1)S(1)} collective-permute-done((bf16[512,512]{1,0:T(8,128)(2,1)S(1)}, bf16[512,512]{1,0:T(8,128)(2,1)S(1)}, u32[]{:S(2)}, u32[]{:S(2)}) %collective-permute-start.2) | collective-permute-done | bytes 524320 | tf_op jit(solution)/shard_map/cond/branch_0_fun/ppermute | solution.py:412
  57.2 2.7 %collective-permute-done.3.py = bf16[512,512]{1,0:T(8,128)(2,1)S(1)} collective-permute-done((bf16[512,512]{1,0:T(8,128)(2,1)S(1)}, bf16[512,512]{1,0:T(8,128)(2,1)S(1)}, u32[]{:S(2)}, u32[]{:S(2)}) %collective-permute-start.3) | collective-permute-done | bytes 524320 | tf_op jit(solution)/shard_map/cond/branch_0_fun/ppermute | solution.py:413
  59.9 0.1 collective-permute-start.4
  60.0 0.0 slice-start
  60.0 0.9 collective-permute-start.5
  60.9 4.6 %collective-permute-done.12.da = bf16[256,512]{1,0:T(8,128)(2,1)S(1)} collective-permute-done((bf16[256,512]{1,0:T(8,128)(2,1)S(1)}, bf16[256,512]{1,0:T(8,128)(2,1)S(1)}, u32[]{:S(2)}, u32[]{:S(2)}) %collective-permute-start.12) | collective-permute-done | bytes 262176 | tf_op jit(solution)/shard_map/cond/branch_0_fun/ppermute | solution.py:413
  65.5 0.0 collective-permute-done.13.db
  65.5 0.0 copy-done.2
  65.5 3.1 %branch_0_fun.16 = (bf16[512,2048]{1,0:T(8,128)(2,1)S(1)}, bf16[128,2048]{1,0:T(8,128)(2,1)S(1)}) custom-call(s32[1]{0:T(128)} %get-tuple-element.68.mp_ref, f32[512,2048]{1,0:T(8,128)S(1)} %get-tuple-element.96.z, f32[512,1]{1,0:T(8,128)S(1)} %get-tuple-element.97.square, bf16[512,512]{1,0:T(8,128)(2,1)S(1)} %get-tuple-element.71.own, ...), custom_call_target="tpu_custom_call" | custom-call | flops 1073741824 | bytes 2097152 | tf_op jit(solution)/shard_map/cond/branch_0_fun/pallas_call | solution.py:347
  68.6 5.0 %branch_0_fun.17 = (bf16[256,1024]{1,0:T(8,128)(2,1)S(1)}, bf16[256,1024]{1,0:T(8,128)(2,1)S(1)}, bf16[256,1024]{1,0:T(8,128)(2,1)S(1)}, bf16[256,1024]{1,0:T(8,128)(2,1)S(1)}) custom-call(bf16[512,2048]{1,0:T(8,128)(2,1)S(1)} %get-tuple-element.101.hidden, bf16[2048,2048]{1,0:T(8,128)(2,1)S(1)} %bitcast.25), custom_call_target="tpu_custom_call" | custom-call | flops 4294967296 | bytes 8388608 | tf_op jit(solution)/shard_map/cond/branch_0_fun/pallas_call | solution.py:356
  73.6 0.1 collective-permute-start.16
  73.7 0.8 collective-permute-start.14
  74.6 1.5 %collective-permute-start.7 = (bf16[1024,256]{1,0:T(8,128)(2,1)S(1)}, bf16[1024,256]{1,0:T(8,128)(2,1)S(1)}, u32[]{:S(2)}, u32[]{:S(2)}) collective-permute-start(bf16[1024,256]{1,0:T(8,128)(2,1)S(1)} %get-tuple-element.86), channel_id=1, source_target_pairs={{0,2},{1,3},{2,0},{3,1},{4,6},{5,7},{6,4},{7,5},{8,10},{9,11},{10,... | collective-permute-start | bytes 1572872 | tf_op jit(solution)/shard_map/cond/branch_0_fun/ppermute | solution.py:413
  76.1 0.0 collective-permute-done.4.da
  76.1 1.7 %collective-permute-start.8 = (bf16[1024,256]{1,0:T(8,128)(2,1)S(1)}, bf16[1024,256]{1,0:T(8,128)(2,1)S(1)}, u32[]{:S(2)}, u32[]{:S(2)}) collective-permute-start(bf16[1024,256]{1,0:T(8,128)(2,1)S(1)} %get-tuple-element.87), channel_id=1, source_target_pairs={{0,1},{1,0},{2,3},{3,2},{4,5},{5,4},{6,7},{7,6},{8,9},{9,8},{10,11... | collective-permute-start | bytes 1572872 | tf_op jit(solution)/shard_map/cond/branch_0_fun/ppermute | solution.py:412
  77.8 0.0 collective-permute-done.5.db
  77.8 6.6 %branch_0_fun.12 = (bf16[512,2048]{1,0:T(8,128)(2,1)S(1)}, bf16[128,2048]{1,0:T(8,128)(2,1)S(1)}) custom-call(s32[1]{0:T(128)} %get-tuple-element.68.mp_ref, bf16[512,512]{1,0:T(8,128)(2,1)S(1)} %get-tuple-element.72.own, bf16[512,512]{1,0:T(8,128)(2,1)S(1)} %collective-permute-done.2.px, bf16[512,512]{1,0:T(8,128)(2,1)S(1)} %collective-permute-done.3.py, ...), custom_call_target="tpu_custom_call" | custom-call | flops 4294967296 | bytes 8388608 | tf_op jit(solution)/shard_map/cond/branch_0_fun/pallas_call | solution.py:321
  84.4 5.0 %branch_0_fun.13 = (bf16[256,1024]{1,0:T(8,128)(2,1)S(1)}, bf16[256,1024]{1,0:T(8,128)(2,1)S(1)}, bf16[256,1024]{1,0:T(8,128)(2,1)S(1)}, bf16[256,1024]{1,0:T(8,128)(2,1)S(1)}) custom-call(bf16[512,2048]{1,0:T(8,128)(2,1)S(1)} %get-tuple-element.82.hidden, bf16[2048,2048]{1,0:T(8,128)(2,1)S(1)} %bitcast.25), custom_call_target="tpu_custom_call" | custom-call | flops 4294967296 | bytes 8388608 | tf_op jit(solution)/shard_map/cond/branch_0_fun/pallas_call | solution.py:356
  89.4 0.4 collective-permute-start.6
  89.8 0.0 collective-permute-done.16.got.got_b
  89.8 0.5 collective-permute-start.10
  90.3 0.1 branch_0_fun.19
  90.4 0.0 copy-start.5
  90.4 0.0 collective-permute-done.14.got.got_a
  90.4 1.3 %collective-permute-start.17 = (bf16[128,1024]{1,0:T(8,128)(2,1)S(1)}, bf16[128,1024]{1,0:T(8,128)(2,1)S(1)}, u32[]{:S(2)}, u32[]{:S(2)}) collective-permute-start(bf16[128,1024]{1,0:T(8,128)(2,1)S(1)} %branch_0_fun.19), channel_id=1, source_target_pairs={{0,1},{1,0},{2,3},{3,2},{4,5},{5,4},{6,7},{7,6},{8,9},{9,8},{10,11... | collective-permute-start | bytes 786440 | tf_op jit(solution)/shard_map/cond/branch_0_fun/ppermute | solution.py:412
  91.7 0.1 branch_0_fun.18
  91.8 0.0 collective-permute-done.7.h3_top
  91.8 2.0 %collective-permute-start.15 = (bf16[128,1024]{1,0:T(8,128)(2,1)S(1)}, bf16[128,1024]{1,0:T(8,128)(2,1)S(1)}, u32[]{:S(2)}, u32[]{:S(2)}) collective-permute-start(bf16[128,1024]{1,0:T(8,128)(2,1)S(1)} %branch_0_fun.18), channel_id=1, source_target_pairs={{0,2},{1,3},{2,0},{3,1},{4,6},{5,7},{6,4},{7,5},{8,10},{9,11},{10,... | collective-permute-start | bytes 786440 | tf_op jit(solution)/shard_map/cond/branch_0_fun/ppermute | solution.py:413
  93.8 0.0 collective-permute-done.8.h3_bottom
  93.8 4.8 %collective-permute-done.6.got.got_a = bf16[256,1024]{1,0:T(8,128)(2,1)S(1)} collective-permute-done((bf16[256,1024]{1,0:T(8,128)(2,1)S(1)}, bf16[256,1024]{1,0:T(8,128)(2,1)S(1)}, u32[]{:S(2)}, u32[]{:S(2)}) %collective-permute-start.6) | collective-permute-done | bytes 524320 | tf_op jit(solution)/shard_map/cond/branch_0_fun/ppermute | solution.py:412
  98.6 0.3 collective-permute-done.10.got.got_b
  99.0 0.1 branch_0_fun.15
  99.0 1.8 %collective-permute-start.11 = (bf16[128,1024]{1,0:T(8,128)(2,1)S(1)}, bf16[128,1024]{1,0:T(8,128)(2,1)S(1)}, u32[]{:S(2)}, u32[]{:S(2)}) collective-permute-start(bf16[128,1024]{1,0:T(8,128)(2,1)S(1)} %branch_0_fun.15), channel_id=1, source_target_pairs={{0,1},{1,0},{2,3},{3,2},{4,5},{5,4},{6,7},{7,6},{8,9},{9,8},{10,11... | collective-permute-start | bytes 786440 | tf_op jit(solution)/shard_map/cond/branch_0_fun/ppermute | solution.py:412
  100.8 0.1 branch_0_fun.14
  100.9 0.1 collective-permute-start.9
  101.0 0.4 collective-permute-done.17.last_b
  101.5 0.3 collective-permute-done.15.last_a
  101.8 2.6 %branch_0_fun.20.rest_0_ = f32[8,64]{1,0:T(8,128)S(1)} custom-call(s32[1]{0:T(128)} %get-tuple-element.68.mp_ref, bf16[128,2048]{1,0:T(8,128)(2,1)S(1)} %get-tuple-element.100.mine, bf16[256,1024]{1,0:T(8,128)(2,1)S(1)} %get-tuple-element.102.keep.keep_a, bf16[256,1024]{1,0:T(8,128)(2,1)S(1)} %collective-permute-done.14.got.got_a, ...), custom_call_target="tpu_custom_call" | custom-call | tf_op jit(solution)/shard_map/cond/branch_0_fun/pallas_call | solution.py:373
  104.4 1.1 collective-permute-done.11.last_b
  105.5 1.8 %collective-permute-done.9.last_a = bf16[128,1024]{1,0:T(8,128)(2,1)S(1)} collective-permute-done((bf16[128,1024]{1,0:T(8,128)(2,1)S(1)}, bf16[128,1024]{1,0:T(8,128)(2,1)S(1)}, u32[]{:S(2)}, u32[]{:S(2)}) %collective-permute-start.9) | collective-permute-done | bytes 262176 | tf_op jit(solution)/shard_map/cond/branch_0_fun/ppermute | solution.py:413
  107.3 2.6 %branch_0_fun.21 = f32[32,128]{1,0:T(8,128)S(1)} custom-call(s32[1]{0:T(128)} %get-tuple-element.68.mp_ref, bf16[128,2048]{1,0:T(8,128)(2,1)S(1)} %get-tuple-element.81.mine, bf16[256,1024]{1,0:T(8,128)(2,1)S(1)} %get-tuple-element.84.keep.keep_a, bf16[256,1024]{1,0:T(8,128)(2,1)S(1)} %collective-permute-done.6.got.got_a, ...), custom_call_target="tpu_custom_call" | custom-call | tf_op jit(solution)/shard_map/cond/branch_0_fun/pallas_call | solution.py:373
  110.1 8.9 %all_to_all.16 = f32[32,1,128]{2,1,0:T(1,128)S(1)} all-to-all(f32[32,1,128]{2,1,0:T(1,128)S(1)} %bitcast.28), channel_id=1, replica_groups=mesh['section'=8,'mp'=4] {'section','mp'}, dimensions={0} | all-to-all | bytes 32768 | tf_op jit(solution)/shard_map/all_to_all | solution.py:452
  119.0 0.0 copy-done.1
  119.0 1.1 shard_map.75
  (11 shorter events, 0.1 us)
Async XLA Ops:
  0.0 28.9 %copy-start = (bf16[1024,512]{1,0:T(8,128)(2,1)S(1)}, bf16[1024,512]{1,0:T(8,128)(2,1)}, u32[]{:S(2)}) copy-start(bf16[1024,512]{1,0:T(8,128)(2,1)} %embed.1) | copy-start | bytes 3145732
  0.0 31.1 %collective-permute-start.54 = (bf16[2048,256]{1,0:T(8,128)(2,1)}, bf16[2048,256]{1,0:T(8,128)(2,1)S(1)}, u32[]{:S(2)}, u32[]{:S(2)}) collective-permute-start(bf16[2048,256]{1,0:T(8,128)(2,1)} %bitcast.16), channel_id=1, source_target_pairs={{0,1},{1,0},{2,3},{3,2},{4,5},{5,4},{6,7},{7,6},{8,9},{9,8},{10,11... | collective-permute-start | bytes 3145736 | tf_op jit(solution)/shard_map/ppermute | solution.py:412
  2.9 28.2 %collective-permute-start.55 = (bf16[2048,256]{1,0:T(8,128)(2,1)}, bf16[2048,256]{1,0:T(8,128)(2,1)}, u32[]{:S(2)}, u32[]{:S(2)}) collective-permute-start(bf16[2048,256]{1,0:T(8,128)(2,1)} %bitcast.17), channel_id=1, source_target_pairs={{0,2},{1,3},{2,0},{3,1},{4,6},{5,7},{6,4},{7,5},{8,10},{9,11},{10,... | collective-permute-start | bytes 3145736 | tf_op jit(solution)/shard_map/ppermute | solution.py:413
  7.2 21.7 %all-to-all-start = ((bf16[8,72,512]{2,1,0:T(8,128)(2,1)}), bf16[8,72,512]{2,1,0:T(8,128)(2,1)S(1)}, u32[]{:S(2)}, u32[]{:S(2)}) async-start(bf16[8,72,512]{2,1,0:T(8,128)(2,1)} %shard_map.73), calls=%async_computation | async-start | bytes 1179648 | tf_op jit(solution)/shard_map/all_to_all | solution.py:434
  31.1 87.9 %copy-start.1 = (s32[128,2]{0,1:T(2,128)S(1)}, s32[128,2]{0,1:T(2,128)}, u32[]{:S(2)}) copy-start(s32[128,2]{0,1:T(2,128)} %param.10) | copy-start | bytes 3076
  31.3 12.0 %collective-permute-start = (bf16[512,512]{1,0:T(8,128)(2,1)S(1)}, bf16[512,512]{1,0:T(8,128)(2,1)S(1)}, u32[]{:S(2)}, u32[]{:S(2)}) collective-permute-start(bf16[512,512]{1,0:T(8,128)(2,1)S(1)} %get-tuple-element.71.own), channel_id=1, source_target_pairs={{0,1},{1,0},{2,3},{3,2},{4,5},{5,4},{6,7},{7,6},{8,9},{9,8},{10,11... | collective-permute-start | bytes 1572872 | tf_op jit(solution)/shard_map/cond/branch_0_fun/ppermute | solution.py:412
  31.9 11.4 %collective-permute-start.1 = (bf16[512,512]{1,0:T(8,128)(2,1)S(1)}, bf16[512,512]{1,0:T(8,128)(2,1)S(1)}, u32[]{:S(2)}, u32[]{:S(2)}) collective-permute-start(bf16[512,512]{1,0:T(8,128)(2,1)S(1)} %get-tuple-element.71.own), channel_id=1, source_target_pairs={{0,2},{1,3},{2,0},{3,1},{4,6},{5,7},{6,4},{7,5},{8,10},{9,11},{10,... | collective-permute-start | bytes 1572872 | tf_op jit(solution)/shard_map/cond/branch_0_fun/ppermute | solution.py:413
  43.4 13.8 %collective-permute-start.2 = (bf16[512,512]{1,0:T(8,128)(2,1)S(1)}, bf16[512,512]{1,0:T(8,128)(2,1)S(1)}, u32[]{:S(2)}, u32[]{:S(2)}) collective-permute-start(bf16[512,512]{1,0:T(8,128)(2,1)S(1)} %get-tuple-element.72.own), channel_id=1, source_target_pairs={{0,1},{1,0},{2,3},{3,2},{4,5},{5,4},{6,7},{7,6},{8,9},{9,8},{10,11... | collective-permute-start | bytes 1572872 | tf_op jit(solution)/shard_map/cond/branch_0_fun/ppermute | solution.py:412
  45.1 14.7 %collective-permute-start.3 = (bf16[512,512]{1,0:T(8,128)(2,1)S(1)}, bf16[512,512]{1,0:T(8,128)(2,1)S(1)}, u32[]{:S(2)}, u32[]{:S(2)}) collective-permute-start(bf16[512,512]{1,0:T(8,128)(2,1)S(1)} %get-tuple-element.72.own), channel_id=1, source_target_pairs={{0,2},{1,3},{2,0},{3,1},{4,6},{5,7},{6,4},{7,5},{8,10},{9,11},{10,... | collective-permute-start | bytes 1572872 | tf_op jit(solution)/shard_map/cond/branch_0_fun/ppermute | solution.py:413
  45.7 19.8 %collective-permute-start.12 = (bf16[256,512]{1,0:T(8,128)(2,1)S(1)}, bf16[256,512]{1,0:T(8,128)(2,1)S(1)}, u32[]{:S(2)}, u32[]{:S(2)}) collective-permute-start(bf16[256,512]{1,0:T(8,128)(2,1)S(1)} %slice.54), channel_id=1, source_target_pairs={{0,2},{1,3},{2,0},{3,1},{4,6},{5,7},{6,4},{7,5},{8,10},{9,11},{10,... | collective-permute-start | bytes 786440 | tf_op jit(solution)/shard_map/cond/branch_0_fun/ppermute | solution.py:413
  47.3 18.2 %collective-permute-start.13 = (bf16[256,512]{1,0:T(8,128)(2,1)S(1)}, bf16[256,512]{1,0:T(8,128)(2,1)S(1)}, u32[]{:S(2)}, u32[]{:S(2)}) collective-permute-start(bf16[256,512]{1,0:T(8,128)(2,1)S(1)} %slice.55), channel_id=1, source_target_pairs={{0,1},{1,0},{2,3},{3,2},{4,5},{5,4},{6,7},{7,6},{8,9},{9,8},{10,11... | collective-permute-start | bytes 786440 | tf_op jit(solution)/shard_map/cond/branch_0_fun/ppermute | solution.py:412
  47.6 17.9 %copy-start.2 = (bf16[2048,2048]{1,0:T(8,128)(2,1)S(1)}, bf16[2048,2048]{1,0:T(8,128)(2,1)}, u32[]{:S(2)}) copy-start(bf16[2048,2048]{1,0:T(8,128)(2,1)} %get-tuple-element.73.w_in) | copy-start | bytes 25165828 | tf_op jit(solution)/shard_map/cond
  59.9 16.2 %collective-permute-start.4 = (bf16[256,512]{1,0:T(8,128)(2,1)S(1)}, bf16[256,512]{1,0:T(8,128)(2,1)S(1)}, u32[]{:S(2)}, u32[]{:S(2)}) collective-permute-start(bf16[256,512]{1,0:T(8,128)(2,1)S(1)} %slice.36), channel_id=1, source_target_pairs={{0,2},{1,3},{2,0},{3,1},{4,6},{5,7},{6,4},{7,5},{8,10},{9,11},{10,... | collective-permute-start | bytes 786440 | tf_op jit(solution)/shard_map/cond/branch_0_fun/ppermute | solution.py:413
  60.0 8.6 %slice-start = ((s8[8388608]{0:T(1024)(128)(4,1)}), s8[4194304]{0:T(1024)(128)(4,1)S(1)}, s32[]{:S(2)}) async-start(s8[8388608]{0:T(1024)(128)(4,1)} %bitcast.24), calls=%async_computation.2 | async-start | bytes 8388608 | tf_op jit(solution)/shard_map/cond
  60.0 17.8 %collective-permute-start.5 = (bf16[256,512]{1,0:T(8,128)(2,1)S(1)}, bf16[256,512]{1,0:T(8,128)(2,1)S(1)}, u32[]{:S(2)}, u32[]{:S(2)}) collective-permute-start(bf16[256,512]{1,0:T(8,128)(2,1)S(1)} %slice.37), channel_id=1, source_target_pairs={{0,1},{1,0},{2,3},{3,2},{4,5},{5,4},{6,7},{7,6},{8,9},{9,8},{10,11... | collective-permute-start | bytes 786440 | tf_op jit(solution)/shard_map/cond/branch_0_fun/ppermute | solution.py:412
  65.5 3.1 %slice-start.1 = ((s8[8388608]{0:T(1024)(128)(4,1)}), s8[4194304]{0:T(1024)(128)(4,1)S(1)}, s32[]{:S(2)}) async-start(s8[8388608]{0:T(1024)(128)(4,1)} %bitcast.24), calls=%async_computation.3 | async-start | bytes 8388608 | tf_op jit(solution)/shard_map/cond
  73.6 16.1 %collective-permute-start.16 = (bf16[256,1024]{1,0:T(8,128)(2,1)S(1)}, bf16[256,1024]{1,0:T(8,128)(2,1)S(1)}, u32[]{:S(2)}, u32[]{:S(2)}) collective-permute-start(bf16[256,1024]{1,0:T(8,128)(2,1)S(1)} %get-tuple-element.105), channel_id=1, source_target_pairs={{0,2},{1,3},{2,0},{3,1},{4,6},{5,7},{6,4},{7,5},{8,10},{9,11},{10,... | collective-permute-start | bytes 1572872 | tf_op jit(solution)/shard_map/cond/branch_0_fun/ppermute | solution.py:413
  73.7 16.7 %collective-permute-start.14 = (bf16[256,1024]{1,0:T(8,128)(2,1)S(1)}, bf16[256,1024]{1,0:T(8,128)(2,1)S(1)}, u32[]{:S(2)}, u32[]{:S(2)}) collective-permute-start(bf16[256,1024]{1,0:T(8,128)(2,1)S(1)} %get-tuple-element.103), channel_id=1, source_target_pairs={{0,1},{1,0},{2,3},{3,2},{4,5},{5,4},{6,7},{7,6},{8,9},{9,8},{10,11... | collective-permute-start | bytes 1572872 | tf_op jit(solution)/shard_map/cond/branch_0_fun/ppermute | solution.py:412
  74.6 17.2 %collective-permute-start.7 = (bf16[1024,256]{1,0:T(8,128)(2,1)S(1)}, bf16[1024,256]{1,0:T(8,128)(2,1)S(1)}, u32[]{:S(2)}, u32[]{:S(2)}) collective-permute-start(bf16[1024,256]{1,0:T(8,128)(2,1)S(1)} %get-tuple-element.86), channel_id=1, source_target_pairs={{0,2},{1,3},{2,0},{3,1},{4,6},{5,7},{6,4},{7,5},{8,10},{9,11},{10,... | collective-permute-start | bytes 1572872 | tf_op jit(solution)/shard_map/cond/branch_0_fun/ppermute | solution.py:413
  76.1 17.8 %collective-permute-start.8 = (bf16[1024,256]{1,0:T(8,128)(2,1)S(1)}, bf16[1024,256]{1,0:T(8,128)(2,1)S(1)}, u32[]{:S(2)}, u32[]{:S(2)}) collective-permute-start(bf16[1024,256]{1,0:T(8,128)(2,1)S(1)} %get-tuple-element.87), channel_id=1, source_target_pairs={{0,1},{1,0},{2,3},{3,2},{4,5},{5,4},{6,7},{7,6},{8,9},{9,8},{10,11... | collective-permute-start | bytes 1572872 | tf_op jit(solution)/shard_map/cond/branch_0_fun/ppermute | solution.py:412
  89.4 9.2 %collective-permute-start.6 = (bf16[256,1024]{1,0:T(8,128)(2,1)S(1)}, bf16[256,1024]{1,0:T(8,128)(2,1)S(1)}, u32[]{:S(2)}, u32[]{:S(2)}) collective-permute-start(bf16[256,1024]{1,0:T(8,128)(2,1)S(1)} %get-tuple-element.85), channel_id=1, source_target_pairs={{0,1},{1,0},{2,3},{3,2},{4,5},{5,4},{6,7},{7,6},{8,9},{9,8},{10,11... | collective-permute-start | bytes 1572872 | tf_op jit(solution)/shard_map/cond/branch_0_fun/ppermute | solution.py:412
  89.8 9.2 %collective-permute-start.10 = (bf16[256,1024]{1,0:T(8,128)(2,1)S(1)}, bf16[256,1024]{1,0:T(8,128)(2,1)S(1)}, u32[]{:S(2)}, u32[]{:S(2)}) collective-permute-start(bf16[256,1024]{1,0:T(8,128)(2,1)S(1)} %get-tuple-element.90), channel_id=1, source_target_pairs={{0,2},{1,3},{2,0},{3,1},{4,6},{5,7},{6,4},{7,5},{8,10},{9,11},{10,... | collective-permute-start | bytes 1572872 | tf_op jit(solution)/shard_map/cond/branch_0_fun/ppermute | solution.py:413
  90.4 11.4 %copy-start.5 = (bf16[2048,256]{1,0:T(8,128)(2,1)S(1)}, bf16[2048,256]{1,0:T(8,128)(2,1)}, u32[]{:S(2)}) copy-start(bf16[2048,256]{1,0:T(8,128)(2,1)} %get-tuple-element.91.h0) | copy-start | bytes 3145732 | tf_op jit(solution)/shard_map/cond
  90.4 11.1 %collective-permute-start.17 = (bf16[128,1024]{1,0:T(8,128)(2,1)S(1)}, bf16[128,1024]{1,0:T(8,128)(2,1)S(1)}, u32[]{:S(2)}, u32[]{:S(2)}) collective-permute-start(bf16[128,1024]{1,0:T(8,128)(2,1)S(1)} %branch_0_fun.19), channel_id=1, source_target_pairs={{0,1},{1,0},{2,3},{3,2},{4,5},{5,4},{6,7},{7,6},{8,9},{9,8},{10,11... | collective-permute-start | bytes 786440 | tf_op jit(solution)/shard_map/cond/branch_0_fun/ppermute | solution.py:412
  91.8 10.0 %collective-permute-start.15 = (bf16[128,1024]{1,0:T(8,128)(2,1)S(1)}, bf16[128,1024]{1,0:T(8,128)(2,1)S(1)}, u32[]{:S(2)}, u32[]{:S(2)}) collective-permute-start(bf16[128,1024]{1,0:T(8,128)(2,1)S(1)} %branch_0_fun.18), channel_id=1, source_target_pairs={{0,2},{1,3},{2,0},{3,1},{4,6},{5,7},{6,4},{7,5},{8,10},{9,11},{10,... | collective-permute-start | bytes 786440 | tf_op jit(solution)/shard_map/cond/branch_0_fun/ppermute | solution.py:413
  99.0 6.4 %collective-permute-start.11 = (bf16[128,1024]{1,0:T(8,128)(2,1)S(1)}, bf16[128,1024]{1,0:T(8,128)(2,1)S(1)}, u32[]{:S(2)}, u32[]{:S(2)}) collective-permute-start(bf16[128,1024]{1,0:T(8,128)(2,1)S(1)} %branch_0_fun.15), channel_id=1, source_target_pairs={{0,1},{1,0},{2,3},{3,2},{4,5},{5,4},{6,7},{7,6},{8,9},{9,8},{10,11... | collective-permute-start | bytes 786440 | tf_op jit(solution)/shard_map/cond/branch_0_fun/ppermute | solution.py:412
  100.9 6.4 %collective-permute-start.9 = (bf16[128,1024]{1,0:T(8,128)(2,1)S(1)}, bf16[128,1024]{1,0:T(8,128)(2,1)S(1)}, u32[]{:S(2)}, u32[]{:S(2)}) collective-permute-start(bf16[128,1024]{1,0:T(8,128)(2,1)S(1)} %branch_0_fun.14), channel_id=1, source_target_pairs={{0,2},{1,3},{2,0},{3,1},{4,6},{5,7},{6,4},{7,5},{8,10},{9,11},{10,... | collective-permute-start | bytes 786440 | tf_op jit(solution)/shard_map/cond/branch_0_fun/ppermute | solution.py:413
